TPU v7x, 1024 devices: a whole 4x4x32 slice. The times are simulated.
1024 devices in a mesh: seq: 64 (over z, core), tp: 16 (over y, x).
Axes of the slice: x: 4, y: 4, z: 32, core: 2. Of those that a mesh axis runs over, the one named last changes fastest.
Arguments:
- hidden: bfloat16 [16384, 7168], P(('seq', 'tp')), may hold values from -6 to 6
- next_ids: int32 [16384], replicated, may hold values from 0 to 65535, as said below
- live_mask: int32 [16384], P('seq'), may hold values 0 or 1
- emb_table: bfloat16 [65536, 7168], P('seq', 'tp'), may hold values from -90 to 90
- gain_hidden: float32 [7168], replicated, may hold values from 0.25 to 1.75
- gain_embed: float32 [7168], replicated, may hold values from 0.25 to 1.75
- projection: bfloat16 [14336, 3584], P(None, 'tp'), may hold values from -2 to 2
- target: bfloat16 [16384, 3584], P('seq', 'tp'), may hold values from -6 to 6
Outputs:
- projected: bfloat16 [16384, 3584], P('seq', 'tp')
- table_grad: bfloat16 [65536, 7168], P('seq', 'tp')
Inputs may be any that keep to these rules, and one draw needn't show every extreme that they name: `next_ids`: positions come in aligned blocks of 256, one block for each index of seq. In every block at most 8 ids lie in any one range of 1024 ids that starts at a multiple of 1024, and in every block exactly 8 lie in one such range.
All inputs are finite; a program needn't handle non-finite values. No bound on the sum of `live_mask` on one device may be relied on, other than what follows from the above.
Results may differ from a plain program's by a relative error of at most 0.019.
Values may be sent and summed in bfloat16 or wider, within the bound.
No kernel may reach another device: no remote copies, remote signals or barrier semaphores. Data moves between devices by JAX's collectives and lax.ppermute only.
A program may use at most 64 MiB of HBM per device.

v0:
```python
import jax
import jax.numpy as jnp
from jax import lax
from jax.sharding import PartitionSpec as P


def rms_scale(values):
    return lax.rsqrt(jnp.mean(values * values, axis=-1, keepdims=True) + 1e-06)


def local(hidden, next_ids, live_mask, emb_table, gain_hidden, gain_embed, projection, target):
    width = hidden.shape[1]
    groups = lax.axis_size("seq")
    my_group = lax.axis_index("seq")
    tokens_here = live_mask.shape[0]
    capacity = 2 * tokens_here // groups
    row_count = emb_table.shape[0]
    local_width = emb_table.shape[1]
    ids_all = next_ids.reshape(groups, tokens_here)
    owner_all = ids_all // row_count
    mine = owner_all == my_group
    local_ids = ids_all - my_group * row_count
    slot_all = jnp.cumsum(mine.astype(jnp.int32), axis=1) - 1
    slot_hit = mine[:, :, None] & (
        slot_all[:, :, None] == jnp.arange(capacity, dtype=jnp.int32)[None, None, :]
    )
    rows_index = jnp.sum(jnp.where(slot_hit, local_ids[:, :, None], 0), axis=1)
    outgoing = emb_table[rows_index]
    fetched = lax.all_to_all(outgoing, "seq", split_axis=0, concat_axis=0, tiled=True)
    ids_mine = lax.dynamic_index_in_dim(ids_all, my_group, 0, keepdims=False)
    owner_mine = ids_mine // row_count
    owner_hit = owner_mine[:, None] == jnp.arange(groups, dtype=jnp.int32)[None, :]
    running = jnp.cumsum(owner_hit.astype(jnp.int32), axis=0) - 1
    slot_mine = jnp.sum(jnp.where(owner_hit, running, 0), axis=1)
    keep_rows = live_mask.astype(jnp.bfloat16)[:, None]
    emb_local = fetched[owner_mine, slot_mine] * keep_rows
    hidden_f32 = hidden.astype(jnp.float32)
    hid_norm = (hidden_f32 * rms_scale(hidden_f32) * gain_hidden).astype(jnp.bfloat16)
    proj_hidden = projection[:width]
    proj_embed = projection[width:]
    hid_all, emb_all = (
        lax.all_gather(hid_norm, "tp", axis=0, tiled=True),
        lax.all_gather(emb_local, "tp", axis=1, tiled=True),
    )
    emb_all_f32 = emb_all.astype(jnp.float32)
    scale = rms_scale(emb_all_f32)
    emb_norm = (emb_all_f32 * scale * gain_embed).astype(jnp.bfloat16)
    emb_part = jnp.dot(emb_norm, proj_embed, preferred_element_type=jnp.float32)
    combined = jnp.dot(hid_all, proj_hidden, preferred_element_type=jnp.float32) + emb_part
    projected = combined.astype(jnp.bfloat16)
    upstream = (combined - target.astype(jnp.float32)).astype(jnp.bfloat16)
    feature_cols = lax.psum_scatter(
        lax.dot_general(
            proj_embed, upstream, (((1,), (1,)), ((), ())), preferred_element_type=jnp.float32
        ).astype(jnp.bfloat16),
        "tp",
        scatter_dimension=0,
        tiled=True,
    ).astype(jnp.float32)
    feature_grad = feature_cols.T
    emb_mine = emb_local.astype(jnp.float32)
    gain_local = lax.dynamic_slice_in_dim(
        gain_embed, lax.axis_index("tp") * local_width, local_width
    )
    curve_part = jnp.sum(emb_mine * gain_local * feature_grad, axis=1)
    curvature = lax.psum(curve_part, "tp")[:, None]
    keep_f32 = live_mask.astype(jnp.float32)[:, None]
    emb_grad = keep_f32 * (
        scale * gain_local * feature_grad - scale * scale * scale * curvature / width * emb_mine
    )
    emb_grad = emb_grad.astype(jnp.bfloat16)
    returned = (
        jnp.zeros((groups, capacity, local_width), jnp.bfloat16)
        .at[owner_mine, slot_mine]
        .set(emb_grad)
    )
    arrived = lax.all_to_all(returned, "seq", split_axis=0, concat_axis=0, tiled=True)
    table_grad = (
        jnp.zeros((row_count, local_width), jnp.float32)
        .at[rows_index.reshape(-1)]
        .add(arrived.reshape(-1, local_width).astype(jnp.float32))
    )
    return (projected, table_grad.astype(jnp.bfloat16))


def solution(mesh):
    return jax.shard_map(
        local,
        mesh=mesh,
        in_specs=(
            P(("seq", "tp"), None),
            P(),
            P("seq"),
            P("seq", "tp"),
            P(),
            P(),
            P(None, "tp"),
            P("seq", "tp"),
        ),
        out_specs=(P("seq", "tp"), P("seq", "tp")),
        check_vma=False,
    )
```

profile of v0, /device:TPU:1, one launch (start us, length us, event | category | flops | bytes accessed | tf_op | source)
XLA Modules:
  0.0 571.3 jit_solution(3800297466338170767)
XLA Ops:
  7.2 0.9 reshape.268
  8.0 0.9 fusion.37
  9.9 1.2 select_reduce_fusion
  11.2 1.5 copy.33
  12.7 2.6 gather_fusion
  15.3 30.5 %all-to-all-start = ((bf16[64,8,448]{2,1,0:T(8,128)(2,1)}), bf16[64,8,448]{2,1,0:T(8,128)(2,1)S(1)}, u32[]{:S(2)}, u32[]{:S(2)}) async-start(bf16[64,8,448]{2,1,0:T(8,128)(2,1)} %bitcast.2), calls=%async_computation | async-start | bytes 1048576 | tf_op jit(solution)/shard_map/all_to_all | solution.py:29
  47.0 63.0 %all-to-all-done = bf16[64,8,448]{2,1,0:T(8,128)(2,1)S(1)} async-done(((bf16[64,8,448]{2,1,0:T(8,128)(2,1)}), bf16[64,8,448]{2,1,0:T(8,128)(2,1)S(1)}, u32[]{:S(2)}, u32[]{:S(2)}) %all-to-all-start) | async-done | bytes 458784 | tf_op jit(solution)/shard_map/all_to_all | solution.py:29
  109.9 2.0 gather_fusion.1
  114.1 66.7 %all-gather.5.cloned.1.call-done = bf16[256,7168]{0,1:T(8,128)(2,1)} async-done(((bf16[256,448]{0,1:T(8,128)(2,1)}), bf16[256,7168]{0,1:T(8,128)(2,1)}) %all-gather.5.cloned.1.call-update) | async-done | bytes 3670032 | tf_op jit(solution)/shard_map/all_gather | solution.py:43
  180.8 3.2 fusion.1
  184.0 5.2 fusion.4
  189.2 80.8 %all-gather.3.cloned.1.call-done = bf16[256,7168]{1,0:T(8,128)(2,1)} async-done(((bf16[16,7168]{1,0:T(8,128)(2,1)}), bf16[256,7168]{1,0:T(8,128)(2,1)}) %all-gather.3.cloned.1.call-update) | async-done | bytes 3670032 | tf_op jit(solution)/shard_map/all_gather | solution.py:42
  269.9 5.0 fusion.43
  274.9 4.9 fusion
  279.8 5.9 %copy.37 = bf16[7168,256]{1,0:T(8,128)(2,1)} copy(bf16[7168,256]{0,1:T(8,128)(2,1)} %fusion) | data formatting | bytes 7340032
  285.8 110.6 %reduce-scatter.4.cloned.1.call-done = bf16[448,256]{1,0:T(8,128)(2,1)} async-done(((bf16[7168,256]{1,0:T(8,128)(2,1)}), bf16[448,256]{1,0:T(8,128)(2,1)}) %reduce-scatter.4.cloned.1.call-update) | async-done | bytes 229392
  396.4 1.1 copy.38
  397.8 30.9 %psum.7 = f32[256]{0:T(256)S(1)} all-reduce(f32[256]{0:T(256)S(1)} %fusion.19), channel_id=1, replica_groups=mesh['seq'=64,'tp'=16] {'tp'}, use_global_device_ids=true, to_apply=%region_10.11 | all-reduce | flops 256 | bytes 2048 | tf_op jit(solution)/shard_map/psum | solution.py:66
  429.0 0.8 broadcast_in_dim.24
  429.8 32.5 %scatter_fusion = bf16[64,8,448]{2,1,0:T(8,128)(2,1)} fusion(bf16[64,8,448]{2,1,0:T(8,128)(2,1)} %broadcast_in_dim.24, s32[256]{0:T(256)S(1)} %bitcast.57, bf16[256,448]{1,0:T(8,128)(2,1)S(1)} %fusion.22), kind=kCustom, calls=%fused_computation.2 | custom fusion | bytes 690176 | tf_op jit(solution)/shard_map/scatter | solution.py:75
  462.3 32.8 %all-to-all-start.1 = ((bf16[64,8,448]{2,1,0:T(8,128)(2,1)}), bf16[64,8,448]{2,1,0:T(8,128)(2,1)S(1)}, u32[]{:S(2)}, u32[]{:S(2)}) async-start(bf16[64,8,448]{2,1,0:T(8,128)(2,1)} %scatter_fusion), calls=%async_computation.1 | async-start | bytes 1048576 | tf_op jit(solution)/shard_map/all_to_all | solution.py:77
  495.2 64.0 %all-to-all-done.1 = bf16[64,8,448]{2,1,0:T(8,128)(2,1)S(1)} async-done(((bf16[64,8,448]{2,1,0:T(8,128)(2,1)}), bf16[64,8,448]{2,1,0:T(8,128)(2,1)S(1)}, u32[]{:S(2)}, u32[]{:S(2)}) %all-to-all-start.1) | async-done | bytes 458784 | tf_op jit(solution)/shard_map/all_to_all | solution.py:77
  559.2 4.2 scatter_custom_fusion.1
  563.5 1.3 copy.36
  (52 shorter events, 5.1 us)
Async XLA Ops:
  11.2 35.7 %copy-start.4 = (s32[256]{0:T(256)S(1)}, s32[256]{0:T(256)}, u32[]{:S(2)}) copy-start(s32[256]{0:T(256)} %param.10) | copy-start | bytes 3076
  15.3 97.7 %copy-start.1 = (bf16[16,7168]{1,0:T(8,128)(2,1)S(1)}, bf16[16,7168]{1,0:T(8,128)(2,1)}, u32[]{:S(2)}) copy-start(bf16[16,7168]{1,0:T(8,128)(2,1)} %param.8) | copy-start | bytes 688132
  15.3 97.8 %copy-start.3 = (f32[7168]{0:T(1024)S(1)}, f32[7168]{0:T(1024)}, u32[]{:S(2)}) copy-start(f32[7168]{0:T(1024)} %param.12) | copy-start | bytes 86020
  15.3 94.6 %all-to-all-start = ((bf16[64,8,448]{2,1,0:T(8,128)(2,1)}), bf16[64,8,448]{2,1,0:T(8,128)(2,1)S(1)}, u32[]{:S(2)}, u32[]{:S(2)}) async-start(bf16[64,8,448]{2,1,0:T(8,128)(2,1)} %bitcast.2), calls=%async_computation | async-start | bytes 1048576 | tf_op jit(solution)/shard_map/all_to_all | solution.py:29
  45.9 134.9 %all-gather.5.cloned.1.call-start = ((), (), s32[]{:S(2)}) async-start(), calls=%async_computation.4 | async-start | bytes 3899392 | tf_op jit(solution)/shard_map/all_gather | solution.py:43
  109.9 74.0 %copy-start.5 = (f32[7168]{0:T(1024)S(1)}, f32[7168]{0:T(1024)}, u32[]{:S(2)}) copy-start(f32[7168]{0:T(1024)} %param.13) | copy-start | bytes 86020
  112.9 157.0 %all-gather.3.cloned.1.call-start = ((), (), s32[]{:S(2)}) async-start(), calls=%async_computation.3 | async-start | bytes 3899392 | tf_op jit(solution)/shard_map/all_gather | solution.py:42
  114.0 282.4 %reduce-scatter.4.cloned.1.call-start = ((), (), s32[]{:S(2)}) async-start(), calls=%async_computation.5 | async-start | bytes 3899392
  180.8 3.2 copy-start
  189.2 85.7 %copy-start.2 = (bf16[256,224]{0,1:T(8,128)(2,1)S(1)}, bf16[256,224]{0,1:T(8,128)(2,1)}, u32[]{:S(2)}) copy-start(bf16[256,224]{0,1:T(8,128)(2,1)} %param.15) | copy-start | bytes 344068
  462.3 96.8 %all-to-all-start.1 = ((bf16[64,8,448]{2,1,0:T(8,128)(2,1)}), bf16[64,8,448]{2,1,0:T(8,128)(2,1)S(1)}, u32[]{:S(2)}, u32[]{:S(2)}) async-start(bf16[64,8,448]{2,1,0:T(8,128)(2,1)} %scatter_fusion), calls=%async_computation.1 | async-start | bytes 1048576 | tf_op jit(solution)/shard_map/all_to_all | solution.py:77
Sparse Core Ops, SparseCore 0:
  113.1 67.6 all-gather.4
  184.9 84.9 all-gather.2
  285.8 110.5 reduce-scatter.3
where the time goes:
time: 573 us; the launch traced here: 571 us
  waiting for transfers between devices  385 us (67%)
  starting transfers between devices  63.4 us (11%)
  local copies, waits for them, and re-layouts  50.1 us (9%)
  blocking collectives  30.9 us (5%)
  matrix products  15 us (3%)
  between operations  14 us (2%)
  other arithmetic  12.8 us (2%)
    unnamed x4, waiting for transfers between devices  111 us
    all_gather x1, waiting for transfers between devices, local(): lax.all_gather(hid_norm, 'tp', axis=0, tiled=True)  80.8 us
    all_gather x1, waiting for transfers between devices, local(): lax.all_gather(emb_local, 'tp', axis=1, tiled=True)  66.7 us
    all_to_all x1, waiting for transfers between devices, local(): lax.all_to_all(returned, 'seq', split_axis=0, concat_axis=0, tiled=True)  64 us
    all_to_all x1, waiting for transfers between devices, local(): lax.all_to_all(outgoing, 'seq', split_axis=0, concat_axis=0, tiled=True)  63 us
    all_to_all x1, starting transfers between devices, local(): lax.all_to_all(returned, 'seq', split_axis=0, concat_axis=0, tiled=True)  32.8 us
    scatter x1, local copies, waits for them, and re-layouts, local(): returned = jnp.zeros((groups, capacity, local_width), jnp.bfloat16).at[ow...  32.5 us
    psum x1, blocking collectives, local(): curvature = lax.psum(curve_part, 'tp')[:, None]  30.9 us
  transfers between devices with their start and end apart: 5, of which 5 were waited for; matrix products, arithmetic and copies ran while one was open for 2% of the time, Pallas kernels for 0%

commit v1 on v0

v1 whole, which is shorter than its diff:
```python
import jax
import jax.numpy as jnp
from jax import lax
from jax.sharding import PartitionSpec as P

BF16 = jnp.bfloat16
F32 = jnp.float32
I32 = jnp.int32
SIDE = 4
PIECES = 16


def contract(left, right, dims):
    return lax.dot_general(left, right, ((dims[:1], dims[1:]), ((), ())), preferred_element_type=F32)


def split_rows(row):
    high = row.astype(BF16)
    rest = row - high.astype(F32)
    middle = rest.astype(BF16)
    low = (rest - middle.astype(F32)).astype(BF16)
    pieces = jnp.concatenate([high, middle, low], axis=0)
    return jnp.pad(pieces, ((0, PIECES - 3), (0, 0)))


def join_rows(rows):
    return jnp.sum(rows.astype(F32), axis=(0, 1))[None, :]


def along_x(value):
    groups = [[SIDE * y + x for x in range(SIDE)] for y in range(SIDE)]
    return lax.all_to_all(value, "tp", 0, 0, tiled=True, axis_index_groups=groups)


def along_y(value):
    groups = [[SIDE * y + x for y in range(SIDE)] for x in range(SIDE)]
    return lax.all_to_all(value, "tp", 0, 0, tiled=True, axis_index_groups=groups)


def to_all(value):
    return jnp.broadcast_to(value, (SIDE,) + value.shape)


def local(hidden, next_ids, live_mask, emb_table, gain_hidden, gain_embed, projection, target):
    width = hidden.shape[1]
    groups = lax.axis_size("seq")
    my_group = lax.axis_index("seq")
    place_tp = lax.axis_index("tp")
    my_y = place_tp // SIDE
    tokens = live_mask.shape[0]
    capacity = 2 * tokens // groups
    slots = groups * capacity
    row_count, local_width = emb_table.shape
    columns = projection.shape[1]
    quarter = width // SIDE

    hidden_f32 = hidden.astype(F32)
    hidden_scale = lax.rsqrt(jnp.mean(hidden_f32 * hidden_f32, axis=-1, keepdims=True) + 1e-06)
    hid_norm = (hidden_f32 * hidden_scale * gain_hidden).astype(BF16)
    hid_all = lax.all_gather(hid_norm, "tp", axis=0, tiled=True)

    proj_t = projection.T

    def piece(y):
        return lax.dynamic_slice(proj_t, (0, width + y * quarter), (columns, quarter))

    weights = jnp.zeros((SIDE, columns, quarter), BF16)
    weights = lax.dynamic_update_slice(weights, piece(my_y)[None], (my_y, 0, 0))
    for step in range(1, SIDE):
        moved = lax.ppermute(
            piece((my_y + step) % SIDE),
            "tp",
            [(SIDE * y + x, SIDE * ((y + step) % SIDE) + x) for y in range(SIDE) for x in range(SIDE)],
        )
        weights = lax.dynamic_update_slice(weights, moved[None], ((my_y - step) % SIDE, 0, 0))
    weights = weights.reshape(SIDE * columns, quarter)

    ids_all = next_ids.reshape(groups, tokens)
    mine = ids_all // row_count == my_group
    token = jnp.arange(tokens, dtype=I32)
    upto = (token[:, None] <= token[None, :]).astype(BF16)
    rank_all = contract(mine.astype(BF16), upto, (1, 0)).astype(I32) - 1
    hit = mine[:, :, None] & (rank_all[:, :, None] == jnp.arange(capacity, dtype=I32))
    local_ids = ids_all - my_group * row_count
    row_of_slot = jnp.sum(jnp.where(hit, local_ids[:, :, None] + 1, 0), axis=1).reshape(slots) - 1
    pick = (row_of_slot[:, None] == jnp.arange(row_count, dtype=I32)[None, :]).astype(BF16)
    outgoing = contract(pick, emb_table, (1, 0)).astype(BF16).reshape(groups, capacity, local_width)
    fetched = lax.all_to_all(outgoing, "seq", split_axis=0, concat_axis=0, tiled=True)

    ids_mine = lax.dynamic_index_in_dim(ids_all, my_group, 0, keepdims=False)
    owner = ids_mine // row_count
    earlier = (owner[:, None] == owner[None, :]) & (token[:, None] < token[None, :])
    slot = owner * capacity + jnp.sum(earlier.astype(I32), axis=0)
    place = (jnp.arange(slots, dtype=I32)[:, None] == slot[None, :]) & (live_mask[None, :] != 0)
    place = place.astype(BF16)

    emb = contract(fetched.reshape(slots, local_width), place, (0, 0))
    gain = lax.dynamic_slice_in_dim(gain_embed, place_tp * local_width, local_width)[:, None]
    square_part = jnp.sum(emb * emb, axis=0, keepdims=True)
    got = along_x(to_all(jnp.concatenate([(emb * gain).astype(BF16), split_rows(square_part)], axis=0)))
    square_part = join_rows(got[:, local_width:])
    partial = contract(weights, got[:, :local_width].reshape(quarter, tokens), (1, 0)).astype(BF16)
    partial = partial.reshape(SIDE, columns, tokens)
    got = along_y(jnp.concatenate([partial, to_all(split_rows(square_part))], axis=1))
    emb_raw = jnp.sum(got[:, :columns].astype(F32), axis=0)
    scale = lax.rsqrt(join_rows(got[:, columns:]) / width + 1e-06)

    hid_part = contract(proj_t[:, :width], hid_all, (1, 1))
    combined = hid_part + emb_raw * scale
    projected = combined.astype(BF16)
    upstream = (combined - target.T.astype(F32)).astype(BF16)
    curve_part = jnp.sum(upstream.astype(F32) * emb_raw, axis=0, keepdims=True)
    got = along_y(to_all(jnp.concatenate([upstream, split_rows(curve_part)], axis=0)))
    curve_part = join_rows(got[:, columns:])
    partial = contract(weights, got[:, :columns].reshape(SIDE * columns, tokens), (0, 0)).astype(BF16)
    partial = partial.reshape(SIDE, local_width, tokens)
    got = along_x(jnp.concatenate([partial, to_all(split_rows(curve_part))], axis=1))
    feature_grad = jnp.sum(got[:, :local_width].astype(F32), axis=0)
    curvature = join_rows(got[:, local_width:])

    emb_grad = scale * gain * feature_grad - scale * scale * scale * curvature / width * emb
    returned = contract(place, emb_grad.astype(BF16), (1, 1)).astype(BF16)
    arrived = lax.all_to_all(
        returned.reshape(groups, capacity, local_width), "seq", split_axis=0, concat_axis=0, tiled=True
    )
    table_grad = contract(arrived.reshape(slots, local_width), pick, (0, 0)).astype(BF16)
    return (projected.T, table_grad.T)


def solution(mesh):
    return jax.shard_map(
        local,
        mesh=mesh,
        in_specs=(
            P(("seq", "tp"), None),
            P(),
            P("seq"),
            P("seq", "tp"),
            P(),
            P(),
            P(None, "tp"),
            P("seq", "tp"),
        ),
        out_specs=(P("seq", "tp"), P("seq", "tp")),
        check_vma=False,
    )
```

time: 573 us -> 273 us (0.48)
  waiting for transfers between devices: 385 us -> 56 us
  blocking collectives: 30.9 us -> 123 us
  local copies, waits for them, and re-layouts: 50.1 us -> 14.2 us
  starting transfers between devices: 63.4 us -> 45.3 us
  other arithmetic: 12.8 us -> 2.99 us
    all_gather x2 -> x1, waiting for transfers between devices: 147 us -> 0.02 us  [local(): hid_all = lax.all_gather(hid_norm, 'tp', axis=0, tiled=True)]
    all_to_all x0 -> x4, blocking collectives: none -> 123 us  [the longest x1 88.9 us: local(): lax.all_to_all(returned.reshape(groups, capacity, local_width), 'seq', sp...]
    unnamed x4 -> x1, waiting for transfers between devices: 111 us -> 0.02 us
    all_to_all x1, waiting for transfers between devices: 64 us -> 13.1 us  [along_x(): lax.all_to_all(value, 'tp', 0, 0, tiled=True, axis_index_groups=groups)]
    scatter x1 -> x0, local copies, waits for them, and re-layouts: 32.5 us -> none  [local(): returned = jnp.zeros((groups, capacity, local_width), jnp.bfloat16).at[ow...]
    psum x1 -> x0, blocking collectives: 30.9 us -> none  [local(): curvature = lax.psum(curve_part, 'tp')[:, None]]
    all_to_all x1, starting transfers between devices: 32.8 us -> 4 us  [along_x(): lax.all_to_all(value, 'tp', 0, 0, tiled=True, axis_index_groups=groups)]
    all_to_all x1, waiting for transfers between devices: 63 us -> 36.2 us  [local(): lax.all_to_all(outgoing, 'seq', split_axis=0, concat_axis=0, tiled=True)]
  transfers between devices with their start and end apart: 5 -> 6, of which waited for: 5 -> 3; matrix products, arithmetic and copies ran while one was open for 2% -> 7% of each run, Pallas kernels for 0% -> 0%
where the time goes in v1:
time: 273 us; the launch traced here: 272 us
  blocking collectives  123 us (45%)
  waiting for transfers between devices  56 us (21%)
  starting transfers between devices  45.3 us (17%)
  matrix products  16.4 us (6%)
  between operations  14.5 us (5%)
  local copies, waits for them, and re-layouts  14.2 us (5%)
  other arithmetic  2.99 us (1%)
    all_to_all x1, blocking collectives, local(): lax.all_to_all(returned.reshape(groups, capacity, local_width), 'seq', sp...  88.9 us
    all_to_all x1, waiting for transfers between devices, local(): lax.all_to_all(outgoing, 'seq', split_axis=0, concat_axis=0, tiled=True)  36.2 us
    all_to_all x1, starting transfers between devices, local(): lax.all_to_all(outgoing, 'seq', split_axis=0, concat_axis=0, tiled=True)  30.6 us
    all_to_all x2, blocking collectives, along_y(): lax.all_to_all(value, 'tp', 0, 0, tiled=True, axis_index_groups=groups)  22.2 us
    dot_general x8, matrix products, contract(): lax.dot_general(left, right, ((dims[:1], dims[1:]), ((), ())), preferred_...  16.4 us
    all_to_all x1, waiting for transfers between devices, along_x(): lax.all_to_all(value, 'tp', 0, 0, tiled=True, axis_index_groups=groups)  13.1 us
    all_to_all x1, blocking collectives, along_x(): lax.all_to_all(value, 'tp', 0, 0, tiled=True, axis_index_groups=groups)  11.7 us
    ppermute x3, starting transfers between devices, local(): lax.ppermute(piece((my_y + step) % SIDE), 'tp', [(SIDE * y + x, SIDE * ((...  10.7 us
  transfers between devices with their start and end apart: 6, of which 3 were waited for; matrix products, arithmetic and copies ran while one was open for 7% of the time, Pallas kernels for 0%

profile of v1, /device:TPU:1, one launch (start us, length us, event | category | flops | bytes accessed | tf_op | source)
XLA Modules:
  0.0 272.3 jit_solution(11237785320228559954)
XLA Ops:
  8.4 1.2 select_reduce_fusion
  10.5 1.0 copy.12
  11.6 30.6 %all-to-all-start = ((bf16[64,8,448]{2,1,0:T(8,128)(2,1)}), bf16[64,8,448]{2,1,0:T(8,128)(2,1)}, u32[]{:S(2)}, u32[]{:S(2)}) async-start(bf16[64,8,448]{2,1,0:T(8,128)(2,1)} %bitcast.10), calls=%async_computation | async-start | bytes 1048576 | tf_op jit(solution)/shard_map/all_to_all | solution.py:88
  43.3 3.1 %dynamic-slice_bitcast_fusion = (bf16[224,1792]{1,0:T(8,128)(2,1)}, bf16[224,1792]{1,0:T(8,128)(2,1)}, bf16[224,1792]{1,0:T(8,128)(2,1)}) fusion(bf16[14336,224]{0,1:T(8,128)(2,1)} %param.14, s32[]{:T(128)S(6)} %select_n.100, s32[]{:T(128)S(6)} %select_n.92, s32[]{:T(128)S(6)} %select_n.96), kind=kLoop, calls=%fused_computation.22 | loop fusion | bytes 4816908 | tf_op jit(solution)/shard_map/dynamic_slice | solution.py:65
  46.5 3.2 %collective-permute-start = (bf16[224,1792]{1,0:T(8,128)(2,1)}, bf16[224,1792]{1,0:T(8,128)(2,1)S(1)}, u32[]{:S(2)}, u32[]{:S(2)}) collective-permute-start(bf16[224,1792]{1,0:T(8,128)(2,1)} %get-tuple-element.7), channel_id=1, source_target_pairs={{0,4},{1,5},{2,6},{3,7},{4,8},{5,9},{6,10},{7,11},{8,12},{9,13},{1... | collective-permute-start | bytes 2408456 | tf_op jit(solution)/shard_map/ppermute | solution.py:70
  49.7 4.5 %collective-permute-start.1 = (bf16[224,1792]{1,0:T(8,128)(2,1)}, bf16[224,1792]{1,0:T(8,128)(2,1)S(1)}, u32[]{:S(2)}, u32[]{:S(2)}) collective-permute-start(bf16[224,1792]{1,0:T(8,128)(2,1)} %get-tuple-element.8), channel_id=1, source_target_pairs={{0,8},{1,9},{2,10},{3,11},{4,12},{5,13},{6,14},{7,15},{8,0},{9,1},... | collective-permute-start | bytes 2408456 | tf_op jit(solution)/shard_map/ppermute | solution.py:70
  54.2 3.0 %collective-permute-start.2 = (bf16[224,1792]{1,0:T(8,128)(2,1)}, bf16[224,1792]{1,0:T(8,128)(2,1)S(1)}, u32[]{:S(2)}, u32[]{:S(2)}) collective-permute-start(bf16[224,1792]{1,0:T(8,128)(2,1)} %get-tuple-element.6), channel_id=1, source_target_pairs={{0,12},{1,13},{2,14},{3,15},{4,0},{5,1},{6,2},{7,3},{8,4},{9,5},{1... | collective-permute-start | bytes 2408456 | tf_op jit(solution)/shard_map/ppermute | solution.py:70
  58.2 1.9 broadcast_in_dim.30
  60.2 2.1 bitcast_dynamic-update-slice_fusion
  62.3 6.7 %collective-permute-done = bf16[224,1792]{1,0:T(8,128)(2,1)S(1)} collective-permute-done((bf16[224,1792]{1,0:T(8,128)(2,1)}, bf16[224,1792]{1,0:T(8,128)(2,1)S(1)}, u32[]{:S(2)}, u32[]{:S(2)}) %collective-permute-start) | collective-permute-done | bytes 802848 | tf_op jit(solution)/shard_map/ppermute | solution.py:70
  69.9 36.2 %all-to-all-done = bf16[64,8,448]{2,1,0:T(8,128)(2,1)} async-done(((bf16[64,8,448]{2,1,0:T(8,128)(2,1)}), bf16[64,8,448]{2,1,0:T(8,128)(2,1)}, u32[]{:S(2)}, u32[]{:S(2)}) %all-to-all-start) | async-done | bytes 458784 | tf_op jit(solution)/shard_map/all_to_all | solution.py:88
  106.1 2.2 multiply_convert_fusion
  108.4 1.0 broadcast_in_dim.37
  109.4 4.0 %all-to-all-start.1 = ((bf16[4,464,256]{2,1,0:T(8,128)(2,1)}), bf16[4,464,256]{2,1,0:T(8,128)(2,1)S(1)}, u32[]{:S(2)}, u32[]{:S(2)}) async-start(bf16[4,464,256]{2,1,0:T(8,128)(2,1)} %broadcast_in_dim.37), calls=%async_computation.1 | async-start | bytes 1900544 | tf_op jit(solution)/shard_map/all_to_all | solution.py:32
  113.4 1.0 bitcast_dynamic-update-slice_fusion.2
  115.3 13.1 %all-to-all-done.1 = bf16[4,464,256]{2,1,0:T(8,128)(2,1)S(1)} async-done(((bf16[4,464,256]{2,1,0:T(8,128)(2,1)}), bf16[4,464,256]{2,1,0:T(8,128)(2,1)S(1)}, u32[]{:S(2)}, u32[]{:S(2)}) %all-to-all-start.1) | async-done | bytes 950304 | tf_op jit(solution)/shard_map/all_to_all | solution.py:32
  128.5 3.0 %convolution_convert_fusion = bf16[896,256]{1,0:T(8,128)(2,1)S(1)} fusion(bf16[896,1792]{1,0:T(8,128)(2,1)} %bitcast.9, bf16[1792,256]{1,0:T(8,128)(2,1)S(1)} %bitcast.65), kind=kOutput, calls=%fused_computation.10 | convolution fusion | flops 822312960 | bytes 4587520 | tf_op jit(solution)/shard_map/dot_general | solution.py:14
  131.5 12.1 %all_to_all.30 = bf16[4,240,256]{2,1,0:T(8,128)(2,1)S(1)} all-to-all(bf16[4,240,256]{2,1,0:T(8,128)(2,1)S(1)} %pad_maximum_fusion.1), channel_id=1, replica_groups={{0,4,8,12},{1,5,9,13},{2,6,10,14},{3,7,11,15},{16,20,24,28},{17,21,25,2..., dimensions={0} | all-to-all | bytes 983040 | tf_op jit(solution)/shard_map/all_to_all | solution.py:37
  143.8 5.0 %fusion.27 = (bf16[256,224]{0,1:T(8,128)(2,1)}, f32[256,224]{0,1:T(8,128)S(1)}) fusion(f32[224,256]{1,0:T(8,128)S(1)} %convert_reduce_fusion.1, f32[256]{0:T(256)S(1)} %add_rsqrt_fusion, bf16[256,7168]{1,0:T(8,128)(2,1)} %all-gather.2.cloned.1.call-done, bf16[224,14336]{1,0:T(8,128)(2,1)} %bitcast.64), kind=kOutput, calls=%fused_computation.56 | convolution fusion | flops 822255616 | bytes 7455744 | tf_op jit(solution)/shard_map/dot_general | solution.py:14
  148.9 10.1 %all_to_all.31 = bf16[4,240,256]{2,1,0:T(8,128)(2,1)S(1)} all-to-all(bf16[4,240,256]{2,1,0:T(8,128)(2,1)S(1)} %broadcast_in_dim.39), channel_id=1, replica_groups={{0,4,8,12},{1,5,9,13},{2,6,10,14},{3,7,11,15},{16,20,24,28},{17,21,25,2..., dimensions={0} | all-to-all | bytes 983040 | tf_op jit(solution)/shard_map/all_to_all | solution.py:37
  159.1 3.1 %fusion.2 = bf16[1792,256]{1,0:T(8,128)(2,1)S(1)} fusion(bf16[4,224,1792]{2,1,0:T(8,128)(2,1)} %bitcast_dynamic-update-slice_fusion.1, bf16[4,240,256]{2,1,0:T(8,128)(2,1)S(1)} %all_to_all.31), kind=kOutput, calls=%fused_computation.3 | convolution fusion | flops 822542336 | bytes 4587520 | tf_op jit(solution)/shard_map/dot_general | solution.py:14
  162.3 11.7 %all_to_all.32 = bf16[4,464,256]{2,1,0:T(8,128)(2,1)S(1)} all-to-all(bf16[4,464,256]{2,1,0:T(8,128)(2,1)S(1)} %pad_maximum_fusion), channel_id=1, replica_groups={{0,1,2,3},{4,5,6,7},{8,9,10,11},{12,13,14,15},{16,17,18,19},{20,21,22,2..., dimensions={0} | all-to-all | bytes 1900544 | tf_op jit(solution)/shard_map/all_to_all | solution.py:32
  174.8 88.9 %all_to_all.33 = bf16[64,8,448]{2,1,0:T(8,128)(2,1)S(1)} all-to-all(bf16[64,8,448]{2,1,0:T(8,128)(2,1)S(1)} %bitcast.63), channel_id=1, replica_groups=mesh['seq'=64,'tp'=16] {'seq'}, dimensions={0} | all-to-all | bytes 917504 | tf_op jit(solution)/shard_map/all_to_all | solution.py:123
  263.7 1.8 fusion.5
  (66 shorter events, 7.3 us)
Async XLA Ops:
  7.2 2.5 copy-start
  7.2 35.0 %copy-start.1 = (bf16[16,7168]{1,0:T(8,128)(2,1)S(1)}, bf16[16,7168]{1,0:T(8,128)(2,1)}, u32[]{:S(2)}) copy-start(bf16[16,7168]{1,0:T(8,128)(2,1)} %param.8) | copy-start | bytes 688132
  7.2 35.2 %copy-start.4 = (f32[7168]{0:T(1024)S(1)}, f32[7168]{0:T(1024)}, u32[]{:S(2)}) copy-start(f32[7168]{0:T(1024)} %param.12) | copy-start | bytes 86020
  11.6 94.6 %all-to-all-start = ((bf16[64,8,448]{2,1,0:T(8,128)(2,1)}), bf16[64,8,448]{2,1,0:T(8,128)(2,1)}, u32[]{:S(2)}, u32[]{:S(2)}) async-start(bf16[64,8,448]{2,1,0:T(8,128)(2,1)} %bitcast.10), calls=%async_computation | async-start | bytes 1048576 | tf_op jit(solution)/shard_map/all_to_all | solution.py:88
  42.1 16.1 %copy-start.5 = (s32[256]{0:T(256)S(1)}, s32[256]{0:T(256)}, u32[]{:S(2)}) copy-start(s32[256]{0:T(256)} %param.10) | copy-start | bytes 3076
  42.2 101.6 %all-gather.2.cloned.1.call-start = ((), (), s32[]{:S(2)}) async-start(), calls=%async_computation.6 | async-start | bytes 3899392 | tf_op jit(solution)/shard_map/all_gather | solution.py:60
  46.5 22.5 %collective-permute-start = (bf16[224,1792]{1,0:T(8,128)(2,1)}, bf16[224,1792]{1,0:T(8,128)(2,1)S(1)}, u32[]{:S(2)}, u32[]{:S(2)}) collective-permute-start(bf16[224,1792]{1,0:T(8,128)(2,1)} %get-tuple-element.7), channel_id=1, source_target_pairs={{0,4},{1,5},{2,6},{3,7},{4,8},{5,9},{6,10},{7,11},{8,12},{9,13},{1... | collective-permute-start | bytes 2408456 | tf_op jit(solution)/shard_map/ppermute | solution.py:70
  49.7 63.7 %collective-permute-start.1 = (bf16[224,1792]{1,0:T(8,128)(2,1)}, bf16[224,1792]{1,0:T(8,128)(2,1)S(1)}, u32[]{:S(2)}, u32[]{:S(2)}) collective-permute-start(bf16[224,1792]{1,0:T(8,128)(2,1)} %get-tuple-element.8), channel_id=1, source_target_pairs={{0,8},{1,9},{2,10},{3,11},{4,12},{5,13},{6,14},{7,15},{8,0},{9,1},... | collective-permute-start | bytes 2408456 | tf_op jit(solution)/shard_map/ppermute | solution.py:70
  54.2 60.1 %collective-permute-start.2 = (bf16[224,1792]{1,0:T(8,128)(2,1)}, bf16[224,1792]{1,0:T(8,128)(2,1)S(1)}, u32[]{:S(2)}, u32[]{:S(2)}) collective-permute-start(bf16[224,1792]{1,0:T(8,128)(2,1)} %get-tuple-element.6), channel_id=1, source_target_pairs={{0,12},{1,13},{2,14},{3,15},{4,0},{5,1},{6,2},{7,3},{8,4},{9,5},{1... | collective-permute-start | bytes 2408456 | tf_op jit(solution)/shard_map/ppermute | solution.py:70
  109.4 19.0 %all-to-all-start.1 = ((bf16[4,464,256]{2,1,0:T(8,128)(2,1)}), bf16[4,464,256]{2,1,0:T(8,128)(2,1)S(1)}, u32[]{:S(2)}, u32[]{:S(2)}) async-start(bf16[4,464,256]{2,1,0:T(8,128)(2,1)} %broadcast_in_dim.37), calls=%async_computation.1 | async-start | bytes 1900544 | tf_op jit(solution)/shard_map/all_to_all | solution.py:32
  143.7 5.0 %copy-start.3 = (bf16[256,224]{0,1:T(8,128)(2,1)S(1)}, bf16[256,224]{0,1:T(8,128)(2,1)}, u32[]{:S(2)}) copy-start(bf16[256,224]{0,1:T(8,128)(2,1)} %param.15) | copy-start | bytes 344068
  162.2 12.0 %copy-start.2 = (f32[448,256]{1,0:T(8,128)S(1)}, f32[448,256]{1,0:T(8,128)}, u32[]{:S(2)}) copy-start(f32[448,256]{1,0:T(8,128)} %get-tuple-element.19) | copy-start | bytes 1376260
Sparse Core Ops, SparseCore 0:
  47.2 96.1 all-gather.1

commit v2 on v1

v2 whole, which is shorter than its diff:
```python
import jax
import jax.numpy as jnp
from jax import lax
from jax.sharding import PartitionSpec as P

BF16 = jnp.bfloat16
F32 = jnp.float32
I32 = jnp.int32
SIDE = 4
PIECES = 16


def contract(left, right, dims):
    return lax.dot_general(left, right, ((dims[:1], dims[1:]), ((), ())), preferred_element_type=F32)


def split_rows(row):
    high = row.astype(BF16)
    rest = row - high.astype(F32)
    middle = rest.astype(BF16)
    low = (rest - middle.astype(F32)).astype(BF16)
    pieces = jnp.concatenate([high, middle, low], axis=0)
    return jnp.pad(pieces, ((0, PIECES - 3), (0, 0)))


def join_rows(row, messages, start):
    return row + sum(jnp.sum(m[start:].astype(F32), axis=0, keepdims=True) for m in messages)


def shift_x(value, step):
    pairs = [(SIDE * y + x, SIDE * y + (x + step) % SIDE) for y in range(SIDE) for x in range(SIDE)]
    return lax.ppermute(value, "tp", pairs)


def shift_y(value, step):
    pairs = [(SIDE * y + x, SIDE * ((y + step) % SIDE) + x) for y in range(SIDE) for x in range(SIDE)]
    return lax.ppermute(value, "tp", pairs)


def gather_xy(value, over_y):
    side = range(SIDE)
    if over_y:
        groups = [[SIDE * y + x for y in side] for x in side]
    else:
        groups = [[SIDE * y + x for x in side] for y in side]
    return lax.all_gather(value, "tp", axis=0, tiled=True, axis_index_groups=groups)


def at(stack, index):
    return lax.dynamic_index_in_dim(stack, index, 0, keepdims=False)


def exchange_rows(left, right):
    groups = lax.axis_size("seq")
    both = jnp.concatenate([left, right], axis=0).astype(BF16).T
    both = both.reshape(groups, both.shape[0] // groups, both.shape[1])
    moved = lax.all_to_all(both, "seq", split_axis=0, concat_axis=0, tiled=True)
    return moved.reshape(-1, moved.shape[2])


def local(hidden, next_ids, live_mask, emb_table, gain_hidden, gain_embed, projection, target):
    width = hidden.shape[1]
    groups = lax.axis_size("seq")
    my_group = lax.axis_index("seq")
    place_tp = lax.axis_index("tp")
    my_y = place_tp // SIDE
    my_x = place_tp % SIDE
    tokens = live_mask.shape[0]
    capacity = 2 * tokens // groups
    slots = groups * capacity
    row_count, local_width = emb_table.shape
    columns = projection.shape[1]
    quarter = width // SIDE

    hidden_f32 = hidden.astype(F32)
    hidden_scale = lax.rsqrt(jnp.mean(hidden_f32 * hidden_f32, axis=-1, keepdims=True) + 1e-06)
    hid_norm = (hidden_f32 * hidden_scale * gain_hidden).astype(BF16)
    hid_all = gather_xy(gather_xy(hid_norm, True), False)

    proj_t = projection.T

    def piece(y):
        return lax.dynamic_slice(proj_t, (0, width + y * quarter), (columns, quarter))

    weights = jnp.zeros((SIDE, columns, quarter), BF16)
    for step in range(SIDE):
        block = shift_y(piece((my_y + step) % SIDE), step) if step else piece(my_y)
        weights = lax.dynamic_update_slice(weights, block[None], (step, 0, 0))
    weights = weights.reshape(SIDE * columns, quarter)

    ids_all = next_ids.reshape(groups, tokens)
    mine = ids_all // row_count == my_group
    token = jnp.arange(tokens, dtype=I32)
    upto = (token[:, None] <= token[None, :]).astype(BF16)
    rank_all = contract(mine.astype(BF16), upto, (1, 0)).astype(I32) - 1
    local_ids = ids_all - my_group * row_count
    half = capacity // 2
    row = jnp.arange(row_count, dtype=I32)

    def picked(first):
        ranks = first + jnp.arange(half, dtype=I32)
        hit = mine[:, None, :] & (rank_all[:, None, :] == ranks[None, :, None])
        rows = jnp.sum(jnp.where(hit, local_ids[:, None, :] + 1, 0), axis=2).reshape(slots // 2) - 1
        return (row[:, None] == rows[None, :]).astype(BF16)

    pick_left, pick_right = picked(0), picked(half)
    table_t = emb_table.T
    fetched = exchange_rows(contract(table_t, pick_left, (1, 0)), contract(table_t, pick_right, (1, 0)))

    ids_mine = lax.dynamic_index_in_dim(ids_all, my_group, 0, keepdims=False)
    owner = ids_mine // row_count
    earlier = (owner[:, None] == owner[None, :]) & (token[:, None] < token[None, :])
    rank = jnp.sum(earlier.astype(I32), axis=0)
    slot = owner * half + rank % half
    place = (jnp.arange(slots // 2, dtype=I32)[:, None] == slot[None, :]) & (live_mask[None, :] != 0)
    place_left = (place & (rank < half)[None, :]).astype(BF16)
    place_right = (place & (rank >= half)[None, :]).astype(BF16)

    emb = contract(fetched, place_left, (0, 0))[:local_width] + contract(fetched, place_right, (0, 0))[local_width:]
    gain = lax.dynamic_slice_in_dim(gain_embed, place_tp * local_width, local_width)[:, None]
    squares = jnp.sum(emb * emb, axis=0, keepdims=True)
    message = jnp.concatenate([(emb * gain).astype(BF16), split_rows(squares)], axis=0)
    got = [shift_x(message, step) for step in range(1, SIDE)]
    squares = join_rows(squares, got, local_width)
    features = jnp.zeros((SIDE, local_width, tokens), BF16)
    for step, part in enumerate([message] + got):
        features = lax.dynamic_update_slice(
            features, part[None, :local_width], ((my_x - step) % SIDE, 0, 0)
        )
    partial = contract(weights, features.reshape(quarter, tokens), (1, 0)).reshape(SIDE, columns, tokens)
    square_rows = split_rows(squares)
    partial, hid_all = lax.optimization_barrier((partial, hid_all))
    got = [
        shift_y(jnp.concatenate([partial[step].astype(BF16), square_rows], axis=0), -step)
        for step in range(1, SIDE)
    ]
    hid_part = contract(hid_all, proj_t[:, :width], (1, 1))
    hid_part = hid_part.reshape(SIDE, SIDE, tokens // (SIDE * SIDE), columns)
    hid_part = lax.optimization_barrier(hid_part.transpose(1, 0, 2, 3).reshape(tokens, columns).T)
    emb_raw = partial[0] + sum(part[:columns].astype(F32) for part in got)
    scale = lax.rsqrt(join_rows(squares, got, columns) / width + 1e-06)

    combined = hid_part + emb_raw * scale
    projected = combined.astype(BF16)
    upstream = (combined - target.T.astype(F32)).astype(BF16)
    curve = jnp.sum(upstream.astype(F32) * emb_raw, axis=0, keepdims=True)
    message = jnp.concatenate([upstream, split_rows(curve)], axis=0)
    got = [shift_y(message, step) for step in range(1, SIDE)]
    curve = join_rows(curve, got, columns)
    upstream_all = jnp.concatenate([part[:columns] for part in [message] + got], axis=0)
    partial = contract(weights, upstream_all, (0, 0)).astype(BF16).reshape(SIDE, local_width, tokens)
    curve_rows = split_rows(curve)
    got = [
        shift_x(jnp.concatenate([at(partial, (my_x - step) % SIDE), curve_rows], axis=0), -step)
        for step in range(1, SIDE)
    ]
    feature_grad = at(partial, my_x).astype(F32) + sum(part[:local_width].astype(F32) for part in got)
    curvature = join_rows(curve, got, local_width)

    emb_grad = scale * gain * feature_grad - scale * scale * scale * curvature / width * emb
    emb_grad = emb_grad.astype(BF16)
    arrived = exchange_rows(contract(emb_grad, place_left, (1, 1)), contract(emb_grad, place_right, (1, 1)))
    table_grad = (
        contract(arrived, pick_left, (0, 1))[:local_width] + contract(arrived, pick_right, (0, 1))[local_width:]
    ).astype(BF16)
    return (projected.T, table_grad.T)


def solution(mesh):
    return jax.shard_map(
        local,
        mesh=mesh,
        in_specs=(
            P(("seq", "tp"), None),
            P(),
            P("seq"),
            P("seq", "tp"),
            P(),
            P(),
            P(None, "tp"),
            P("seq", "tp"),
        ),
        out_specs=(P("seq", "tp"), P("seq", "tp")),
        check_vma=False,
    )
```

time: 273 us -> 281 us (1.029)
  blocking collectives: 123 us -> 13.4 us
  starting transfers between devices: 45.3 us -> 108 us
  waiting for transfers between devices: 56 us -> 109 us
  matrix products: 16.4 us -> 12.6 us
    all_to_all x4 -> x0, blocking collectives: 123 us -> none  [the longest x1 88.9 us: local(): lax.all_to_all(returned.reshape(groups, capacity, local_width), 'seq', sp...]
    ppermute x3 -> x15, waiting for transfers between devices: 6.73 us -> 49.8 us  [the longest x9 30 us: shift_y(): return lax.ppermute(value, 'tp', pairs)]
    ppermute x3 -> x15, starting transfers between devices: 10.7 us -> 49 us  [the longest x9 27.9 us: shift_y(): return lax.ppermute(value, 'tp', pairs)]
    all_to_all x2, starting transfers between devices: 34.6 us -> 59.4 us  [exchange_rows(): moved = lax.all_to_all(both, 'seq', split_axis=0, concat_axis=0, tiled=True)]
    all_gather x0 -> x1, blocking collectives: none -> 13.4 us  [gather_xy(): lax.all_gather(value, 'tp', axis=0, tiled=True, axis_index_groups=groups)]
    all_to_all x2, waiting for transfers between devices: 49.2 us -> 59.5 us  [exchange_rows(): moved = lax.all_to_all(both, 'seq', split_axis=0, concat_axis=0, tiled=True)]
    dot_general x8 -> x12, matrix products: 16.4 us -> 12.6 us  [contract(): lax.dot_general(left, right, ((dims[:1], dims[1:]), ((), ())), preferred_...]
    broadcast_in_dim x5 -> x1, local copies, waits for them, and re-layouts: 2.95 us -> 0.06 us  [local(): features = jnp.zeros((SIDE, local_width, tokens), BF16)]
  transfers between devices with their start and end apart: 6 -> 18, of which waited for: 3 -> 9; matrix products, arithmetic and copies ran while one was open for 7% -> 7% of each run, Pallas kernels for 0% -> 0%
where the time goes in v2:
time: 281 us; the launch traced here: 279 us
  waiting for transfers between devices  109 us (39%)
  starting transfers between devices  108 us (38%)
  between operations  14.8 us (5%)
  local copies, waits for them, and re-layouts  14.6 us (5%)
  blocking collectives  13.4 us (5%)
  matrix products  12.6 us (4%)
  other arithmetic  5.69 us (2%)
    all_to_all x2, waiting for transfers between devices, exchange_rows(): moved = lax.all_to_all(both, 'seq', split_axis=0, concat_axis=0, tiled=True)  59.5 us
    all_to_all x2, starting transfers between devices, exchange_rows(): moved = lax.all_to_all(both, 'seq', split_axis=0, concat_axis=0, tiled=True)  59.4 us
    ppermute x9, waiting for transfers between devices, shift_y(): return lax.ppermute(value, 'tp', pairs)  30 us
    ppermute x9, starting transfers between devices, shift_y(): return lax.ppermute(value, 'tp', pairs)  27.9 us
    ppermute x6, starting transfers between devices, shift_x(): return lax.ppermute(value, 'tp', pairs)  21.1 us
    ppermute x6, waiting for transfers between devices, shift_x(): return lax.ppermute(value, 'tp', pairs)  19.7 us
    all_gather x1, blocking collectives, gather_xy(): lax.all_gather(value, 'tp', axis=0, tiled=True, axis_index_groups=groups)  13.4 us
    dot_general x12, matrix products, contract(): lax.dot_general(left, right, ((dims[:1], dims[1:]), ((), ())), preferred_...  12.6 us
  transfers between devices with their start and end apart: 18, of which 9 were waited for; matrix products, arithmetic and copies ran while one was open for 7% of the time, Pallas kernels for 0%

profile of v2, /device:TPU:1, one launch (start us, length us, event | category | flops | bytes accessed | tf_op | source)
XLA Modules:
  0.0 278.8 jit_solution(3153434281900592775)
XLA Ops:
  11.2 30.4 %all-to-all-start = ((bf16[64,4,896]{2,1,0:T(4,128)(2,1)}), bf16[64,4,896]{2,1,0:T(4,128)(2,1)S(1)}, u32[]{:S(2)}, u32[]{:S(2)}) async-start(bf16[64,4,896]{2,1,0:T(4,128)(2,1)} %reshape.511), calls=%async_computation | async-start | bytes 917504 | tf_op jit(solution)/shard_map/all_to_all | solution.py:57
  42.0 13.4 %all_gather.6 = bf16[64,7168]{1,0:T(8,128)(2,1)} all-gather(bf16[16,7168]{1,0:T(8,128)(2,1)S(1)} %fusion.13), channel_id=1, replica_groups={{0,4,8,12},{1,5,9,13},{2,6,10,14},{3,7,11,15},{16,20,24,28},{17,21,25,2..., dimensions={0}, use_global_device_ids=true | all-gather | bytes 1146880 | tf_op jit(solution)/shard_map/all_gather | solution.py:46
  55.5 3.4 %dynamic-slice_bitcast_fusion = (bf16[224,1792]{1,0:T(8,128)(2,1)}, bf16[224,1792]{1,0:T(8,128)(2,1)}, bf16[224,1792]{1,0:T(8,128)(2,1)}, bf16[1,224,1792]{2,1,0:T(8,128)(2,1)S(1)}) fusion(bf16[14336,224]{0,1:T(8,128)(2,1)} %param.14, s32[]{:T(128)S(6)} %select_n.132, s32[]{:T(128)S(6)} %select_n.130, s32[]{:T(128)S(6)} %select_n.128, s32[]{:T(128)S(6)} %select_n.126), kind=kLoop, calls=%fused_computation.20 | loop fusion | bytes 6422544 | tf_op jit(solution)/shard_map/dynamic_slice | solution.py:83
  58.9 2.6 collective-permute-start
  61.5 4.3 %collective-permute-start.1 = (bf16[224,1792]{1,0:T(8,128)(2,1)}, bf16[224,1792]{1,0:T(8,128)(2,1)}, u32[]{:S(2)}, u32[]{:S(2)}) collective-permute-start(bf16[224,1792]{1,0:T(8,128)(2,1)} %get-tuple-element.16), channel_id=1, source_target_pairs={{0,8},{1,9},{2,10},{3,11},{4,12},{5,13},{6,14},{7,15},{8,0},{9,1},... | collective-permute-start | bytes 2408456 | tf_op jit(solution)/shard_map/ppermute | solution.py:37
  71.1 9.5 %collective-permute-done = bf16[224,1792]{1,0:T(8,128)(2,1)} collective-permute-done((bf16[224,1792]{1,0:T(8,128)(2,1)}, bf16[224,1792]{1,0:T(8,128)(2,1)}, u32[]{:S(2)}, u32[]{:S(2)}) %collective-permute-start) | collective-permute-done | bytes 802848 | tf_op jit(solution)/shard_map/ppermute | solution.py:37
  82.6 13.3 %collective-permute-done.1 = bf16[224,1792]{1,0:T(8,128)(2,1)} collective-permute-done((bf16[224,1792]{1,0:T(8,128)(2,1)}, bf16[224,1792]{1,0:T(8,128)(2,1)}, u32[]{:S(2)}, u32[]{:S(2)}) %collective-permute-start.1) | collective-permute-done | bytes 802848 | tf_op jit(solution)/shard_map/ppermute | solution.py:37
  101.0 3.2 %collective-permute-start.3 = (bf16[464,256]{1,0:T(8,128)(2,1)S(1)}, bf16[464,256]{1,0:T(8,128)(2,1)S(1)}, u32[]{:S(2)}, u32[]{:S(2)}) collective-permute-start(bf16[464,256]{1,0:T(8,128)(2,1)S(1)} %pad_maximum_fusion.3), channel_id=1, source_target_pairs={{0,1},{1,2},{2,3},{3,0},{4,5},{5,6},{6,7},{7,4},{8,9},{9,10},{10,1... | collective-permute-start | bytes 712712 | tf_op jit(solution)/shard_map/ppermute | solution.py:32
  104.2 4.4 %collective-permute-start.4 = (bf16[464,256]{1,0:T(8,128)(2,1)S(1)}, bf16[464,256]{1,0:T(8,128)(2,1)S(1)}, u32[]{:S(2)}, u32[]{:S(2)}) collective-permute-start(bf16[464,256]{1,0:T(8,128)(2,1)S(1)} %pad_maximum_fusion.3), channel_id=1, source_target_pairs={{0,2},{1,3},{2,0},{3,1},{4,6},{5,7},{6,4},{7,5},{8,10},{9,11},{10,... | collective-permute-start | bytes 712712 | tf_op jit(solution)/shard_map/ppermute | solution.py:32
  108.6 3.1 %collective-permute-start.5 = (bf16[464,256]{1,0:T(8,128)(2,1)S(1)}, bf16[464,256]{1,0:T(8,128)(2,1)S(1)}, u32[]{:S(2)}, u32[]{:S(2)}) collective-permute-start(bf16[464,256]{1,0:T(8,128)(2,1)S(1)} %pad_maximum_fusion.3), channel_id=1, source_target_pairs={{0,3},{1,0},{2,1},{3,2},{4,7},{5,4},{6,5},{7,6},{8,11},{9,8},{10,9... | collective-permute-start | bytes 712712 | tf_op jit(solution)/shard_map/ppermute | solution.py:32
  111.8 16.1 %collective-permute-done.5 = bf16[464,256]{1,0:T(8,128)(2,1)S(1)} collective-permute-done((bf16[464,256]{1,0:T(8,128)(2,1)S(1)}, bf16[464,256]{1,0:T(8,128)(2,1)S(1)}, u32[]{:S(2)}, u32[]{:S(2)}) %collective-permute-start.5) | collective-permute-done | bytes 237600 | tf_op jit(solution)/shard_map/ppermute | solution.py:32
  129.2 3.1 %collective-permute-start.8 = (bf16[240,256]{1,0:T(8,128)(2,1)S(1)}, bf16[240,256]{1,0:T(8,128)(2,1)S(1)}, u32[]{:S(2)}, u32[]{:S(2)}) collective-permute-start(bf16[240,256]{1,0:T(8,128)(2,1)S(1)} %get-tuple-element.29), channel_id=1, source_target_pairs={{0,4},{1,5},{2,6},{3,7},{4,8},{5,9},{6,10},{7,11},{8,12},{9,13},{1... | collective-permute-start | bytes 368648 | tf_op jit(solution)/shard_map/ppermute | solution.py:37
  132.4 3.4 %collective-permute-start.6 = (bf16[240,256]{1,0:T(8,128)(2,1)S(1)}, bf16[240,256]{1,0:T(8,128)(2,1)S(1)}, u32[]{:S(2)}, u32[]{:S(2)}) collective-permute-start(bf16[240,256]{1,0:T(8,128)(2,1)S(1)} %get-tuple-element.30), channel_id=1, source_target_pairs={{0,12},{1,13},{2,14},{3,15},{4,0},{5,1},{6,2},{7,3},{8,4},{9,5},{1... | collective-permute-start | bytes 368648 | tf_op jit(solution)/shard_map/ppermute | solution.py:37
  135.8 4.2 %fusion = f32[256,224]{1,0:T(8,128)S(1)} fusion(bf16[256,7168]{1,0:T(8,128)(2,1)} %all-gather.2.cloned.1.call-done, bf16[224,14336]{1,0:T(8,128)(2,1)} %bitcast.96), kind=kOutput, calls=%fused_computation | convolution fusion | flops 822083584 | bytes 7110656 | tf_op jit(solution)/shard_map/dot_general | solution.py:14
  140.1 3.4 %collective-permute-start.7 = (bf16[240,256]{1,0:T(8,128)(2,1)S(1)}, bf16[240,256]{1,0:T(8,128)(2,1)S(1)}, u32[]{:S(2)}, u32[]{:S(2)}) collective-permute-start(bf16[240,256]{1,0:T(8,128)(2,1)S(1)} %get-tuple-element.28), channel_id=1, source_target_pairs={{0,8},{1,9},{2,10},{3,11},{4,12},{5,13},{6,14},{7,15},{8,0},{9,1},... | collective-permute-start | bytes 368648 | tf_op jit(solution)/shard_map/ppermute | solution.py:37
  143.6 3.6 %collective-permute-done.7 = bf16[240,256]{1,0:T(8,128)(2,1)S(1)} collective-permute-done((bf16[240,256]{1,0:T(8,128)(2,1)S(1)}, bf16[240,256]{1,0:T(8,128)(2,1)S(1)}, u32[]{:S(2)}, u32[]{:S(2)}) %collective-permute-start.7) | collective-permute-done | bytes 122912 | tf_op jit(solution)/shard_map/ppermute | solution.py:37
  147.5 3.2 %collective-permute-start.11 = (bf16[240,256]{1,0:T(8,128)(2,1)S(1)}, bf16[240,256]{1,0:T(8,128)(2,1)S(1)}, u32[]{:S(2)}, u32[]{:S(2)}) collective-permute-start(bf16[240,256]{1,0:T(8,128)(2,1)S(1)} %pad_maximum_fusion.7), channel_id=1, source_target_pairs={{0,12},{1,13},{2,14},{3,15},{4,0},{5,1},{6,2},{7,3},{8,4},{9,5},{1... | collective-permute-start | bytes 368648 | tf_op jit(solution)/shard_map/ppermute | solution.py:37
  152.8 3.4 %collective-permute-start.10 = (bf16[240,256]{1,0:T(8,128)(2,1)S(1)}, bf16[240,256]{1,0:T(8,128)(2,1)S(1)}, u32[]{:S(2)}, u32[]{:S(2)}) collective-permute-start(bf16[240,256]{1,0:T(8,128)(2,1)S(1)} %pad_maximum_fusion.7), channel_id=1, source_target_pairs={{0,8},{1,9},{2,10},{3,11},{4,12},{5,13},{6,14},{7,15},{8,0},{9,1},... | collective-permute-start | bytes 368648 | tf_op jit(solution)/shard_map/ppermute | solution.py:37
  160.0 3.1 %convolution_convert_fusion = bf16[1792,256]{1,0:T(8,128)(2,1)S(1)} fusion(bf16[896,1792]{1,0:T(8,128)(2,1)} %bitcast.93, bf16[224,256]{1,0:T(8,128)(2,1)S(1)} %slice.159, bf16[224,256]{1,0:T(8,128)(2,1)S(1)} %slice.158, bf16[224,256]{1,0:T(8,128)(2,1)S(1)} %slice.157, bf16[224,256]{1,0:T(8,128)(2,1)S(1)} %get-tuple-element.9), kind=kOutput, calls=%fused_computation.2 | convolution fusion | flops 824377344 | bytes 4587520 | tf_op jit(solution)/shard_map/dot_general | solution.py:14
  163.2 4.0 %collective-permute-start.14 = (bf16[464,256]{1,0:T(8,128)(2,1)S(1)}, bf16[464,256]{1,0:T(8,128)(2,1)}, u32[]{:S(2)}, u32[]{:S(2)}) collective-permute-start(bf16[464,256]{1,0:T(8,128)(2,1)S(1)} %get-tuple-element.27), channel_id=1, source_target_pairs={{0,1},{1,2},{2,3},{3,0},{4,5},{5,6},{6,7},{7,4},{8,9},{9,10},{10,1... | collective-permute-start | bytes 712712 | tf_op jit(solution)/shard_map/ppermute | solution.py:32
  169.7 3.9 %collective-permute-start.13 = (bf16[464,256]{1,0:T(8,128)(2,1)S(1)}, bf16[464,256]{1,0:T(8,128)(2,1)}, u32[]{:S(2)}, u32[]{:S(2)}) collective-permute-start(bf16[464,256]{1,0:T(8,128)(2,1)S(1)} %get-tuple-element.26), channel_id=1, source_target_pairs={{0,2},{1,3},{2,0},{3,1},{4,6},{5,7},{6,4},{7,5},{8,10},{9,11},{10,... | collective-permute-start | bytes 712712 | tf_op jit(solution)/shard_map/ppermute | solution.py:32
  175.1 3.6 %collective-permute-done.13 = bf16[464,256]{1,0:T(8,128)(2,1)} collective-permute-done((bf16[464,256]{1,0:T(8,128)(2,1)S(1)}, bf16[464,256]{1,0:T(8,128)(2,1)}, u32[]{:S(2)}, u32[]{:S(2)}) %collective-permute-start.13) | collective-permute-done | bytes 237600 | tf_op jit(solution)/shard_map/ppermute | solution.py:32
  182.5 29.0 %all-to-all-start.1 = ((bf16[64,4,896]{2,1,0:T(4,128)(2,1)}), bf16[64,4,896]{2,1,0:T(4,128)(2,1)S(1)}, u32[]{:S(2)}, u32[]{:S(2)}) async-start(bf16[64,4,896]{2,1,0:T(4,128)(2,1)} %reshape.518), calls=%async_computation.1 | async-start | bytes 917504 | tf_op jit(solution)/shard_map/all_to_all | solution.py:57
  212.2 57.6 %all-to-all-done.1 = bf16[64,4,896]{2,1,0:T(4,128)(2,1)S(1)} async-done(((bf16[64,4,896]{2,1,0:T(4,128)(2,1)}), bf16[64,4,896]{2,1,0:T(4,128)(2,1)S(1)}, u32[]{:S(2)}, u32[]{:S(2)}) %all-to-all-start.1) | async-done | bytes 458784 | tf_op jit(solution)/shard_map/all_to_all | solution.py:57
  (118 shorter events, 34.8 us)
Async XLA Ops:
  9.1 32.6 %copy-start.3 = (bf16[16,7168]{1,0:T(8,128)(2,1)S(1)}, bf16[16,7168]{1,0:T(8,128)(2,1)}, u32[]{:S(2)}) copy-start(bf16[16,7168]{1,0:T(8,128)(2,1)} %param.8) | copy-start | bytes 688132
  9.1 32.8 %copy-start.5 = (f32[7168]{0:T(1024)S(1)}, f32[7168]{0:T(1024)}, u32[]{:S(2)}) copy-start(f32[7168]{0:T(1024)} %param.12) | copy-start | bytes 86020
  11.2 88.7 %all-to-all-start = ((bf16[64,4,896]{2,1,0:T(4,128)(2,1)}), bf16[64,4,896]{2,1,0:T(4,128)(2,1)S(1)}, u32[]{:S(2)}, u32[]{:S(2)}) async-start(bf16[64,4,896]{2,1,0:T(4,128)(2,1)} %reshape.511), calls=%async_computation | async-start | bytes 917504 | tf_op jit(solution)/shard_map/all_to_all | solution.py:57
  41.6 87.5 %all-gather.2.cloned.1.call-start = ((), (), s32[]{:S(2)}) async-start(), calls=%async_computation.2 | async-start | bytes 4587520 | tf_op jit(solution)/shard_map/all_gather | solution.py:46
  58.9 12.2 %copy-start.6 = (s32[256]{0:T(256)S(1)}, s32[256]{0:T(256)}, u32[]{:S(2)}) copy-start(s32[256]{0:T(256)} %param.10) | copy-start | bytes 3076
  58.9 21.7 %collective-permute-start = (bf16[224,1792]{1,0:T(8,128)(2,1)}, bf16[224,1792]{1,0:T(8,128)(2,1)}, u32[]{:S(2)}, u32[]{:S(2)}) collective-permute-start(bf16[224,1792]{1,0:T(8,128)(2,1)} %get-tuple-element.17), channel_id=1, source_target_pairs={{0,4},{1,5},{2,6},{3,7},{4,8},{5,9},{6,10},{7,11},{8,12},{9,13},{1... | collective-permute-start | bytes 2408456 | tf_op jit(solution)/shard_map/ppermute | solution.py:37
  61.5 34.5 %collective-permute-start.1 = (bf16[224,1792]{1,0:T(8,128)(2,1)}, bf16[224,1792]{1,0:T(8,128)(2,1)}, u32[]{:S(2)}, u32[]{:S(2)}) collective-permute-start(bf16[224,1792]{1,0:T(8,128)(2,1)} %get-tuple-element.16), channel_id=1, source_target_pairs={{0,8},{1,9},{2,10},{3,11},{4,12},{5,13},{6,14},{7,15},{8,0},{9,1},... | collective-permute-start | bytes 2408456 | tf_op jit(solution)/shard_map/ppermute | solution.py:37
  65.8 45.9 %collective-permute-start.2 = (bf16[224,1792]{1,0:T(8,128)(2,1)}, bf16[224,1792]{1,0:T(8,128)(2,1)S(1)}, u32[]{:S(2)}, u32[]{:S(2)}) collective-permute-start(bf16[224,1792]{1,0:T(8,128)(2,1)} %get-tuple-element.15), channel_id=1, source_target_pairs={{0,12},{1,13},{2,14},{3,15},{4,0},{5,1},{6,2},{7,3},{8,4},{9,5},{1... | collective-permute-start | bytes 2408456 | tf_op jit(solution)/shard_map/ppermute | solution.py:37
  100.1 11.6 %copy-start.1 = (bf16[4,224,1792]{2,1,0:T(8,128)(2,1)S(1)}, bf16[4,224,1792]{2,1,0:T(8,128)(2,1)}, u32[]{:S(2)}) copy-start(bf16[4,224,1792]{2,1,0:T(8,128)(2,1)} %bitcast_dynamic-update-slice_fusion.1) | copy-start | bytes 9633796
  101.0 26.9 %collective-permute-start.3 = (bf16[464,256]{1,0:T(8,128)(2,1)S(1)}, bf16[464,256]{1,0:T(8,128)(2,1)S(1)}, u32[]{:S(2)}, u32[]{:S(2)}) collective-permute-start(bf16[464,256]{1,0:T(8,128)(2,1)S(1)} %pad_maximum_fusion.3), channel_id=1, source_target_pairs={{0,1},{1,2},{2,3},{3,0},{4,5},{5,6},{6,7},{7,4},{8,9},{9,10},{10,1... | collective-permute-start | bytes 712712 | tf_op jit(solution)/shard_map/ppermute | solution.py:32
  104.2 23.7 %collective-permute-start.4 = (bf16[464,256]{1,0:T(8,128)(2,1)S(1)}, bf16[464,256]{1,0:T(8,128)(2,1)S(1)}, u32[]{:S(2)}, u32[]{:S(2)}) collective-permute-start(bf16[464,256]{1,0:T(8,128)(2,1)S(1)} %pad_maximum_fusion.3), channel_id=1, source_target_pairs={{0,2},{1,3},{2,0},{3,1},{4,6},{5,7},{6,4},{7,5},{8,10},{9,11},{10,... | collective-permute-start | bytes 712712 | tf_op jit(solution)/shard_map/ppermute | solution.py:32
  108.6 19.3 %collective-permute-start.5 = (bf16[464,256]{1,0:T(8,128)(2,1)S(1)}, bf16[464,256]{1,0:T(8,128)(2,1)S(1)}, u32[]{:S(2)}, u32[]{:S(2)}) collective-permute-start(bf16[464,256]{1,0:T(8,128)(2,1)S(1)} %pad_maximum_fusion.3), channel_id=1, source_target_pairs={{0,3},{1,0},{2,1},{3,2},{4,7},{5,4},{6,5},{7,6},{8,11},{9,8},{10,9... | collective-permute-start | bytes 712712 | tf_op jit(solution)/shard_map/ppermute | solution.py:32
  111.8 16.3 %copy-start.2 = (bf16[4,224,1792]{2,1,0:T(8,128)(2,1)}, bf16[4,224,1792]{2,1,0:T(8,128)(2,1)S(1)}, u32[]{:S(2)}) copy-start(bf16[4,224,1792]{2,1,0:T(8,128)(2,1)S(1)} %bitcast_dynamic-update-slice_fusion) | copy-start | bytes 9633796
  129.2 14.3 %collective-permute-start.8 = (bf16[240,256]{1,0:T(8,128)(2,1)S(1)}, bf16[240,256]{1,0:T(8,128)(2,1)S(1)}, u32[]{:S(2)}, u32[]{:S(2)}) collective-permute-start(bf16[240,256]{1,0:T(8,128)(2,1)S(1)} %get-tuple-element.29), channel_id=1, source_target_pairs={{0,4},{1,5},{2,6},{3,7},{4,8},{5,9},{6,10},{7,11},{8,12},{9,13},{1... | collective-permute-start | bytes 368648 | tf_op jit(solution)/shard_map/ppermute | solution.py:37
  132.4 11.2 %collective-permute-start.6 = (bf16[240,256]{1,0:T(8,128)(2,1)S(1)}, bf16[240,256]{1,0:T(8,128)(2,1)S(1)}, u32[]{:S(2)}, u32[]{:S(2)}) collective-permute-start(bf16[240,256]{1,0:T(8,128)(2,1)S(1)} %get-tuple-element.30), channel_id=1, source_target_pairs={{0,12},{1,13},{2,14},{3,15},{4,0},{5,1},{6,2},{7,3},{8,4},{9,5},{1... | collective-permute-start | bytes 368648 | tf_op jit(solution)/shard_map/ppermute | solution.py:37
  135.7 11.5 %copy-start.4 = (bf16[256,224]{0,1:T(8,128)(2,1)S(1)}, bf16[256,224]{0,1:T(8,128)(2,1)}, u32[]{:S(2)}) copy-start(bf16[256,224]{0,1:T(8,128)(2,1)} %param.15) | copy-start | bytes 344068
  140.1 7.1 %collective-permute-start.7 = (bf16[240,256]{1,0:T(8,128)(2,1)S(1)}, bf16[240,256]{1,0:T(8,128)(2,1)S(1)}, u32[]{:S(2)}, u32[]{:S(2)}) collective-permute-start(bf16[240,256]{1,0:T(8,128)(2,1)S(1)} %get-tuple-element.28), channel_id=1, source_target_pairs={{0,8},{1,9},{2,10},{3,11},{4,12},{5,13},{6,14},{7,15},{8,0},{9,1},... | collective-permute-start | bytes 368648 | tf_op jit(solution)/shard_map/ppermute | solution.py:37
  147.5 8.8 %collective-permute-start.11 = (bf16[240,256]{1,0:T(8,128)(2,1)S(1)}, bf16[240,256]{1,0:T(8,128)(2,1)S(1)}, u32[]{:S(2)}, u32[]{:S(2)}) collective-permute-start(bf16[240,256]{1,0:T(8,128)(2,1)S(1)} %pad_maximum_fusion.7), channel_id=1, source_target_pairs={{0,12},{1,13},{2,14},{3,15},{4,0},{5,1},{6,2},{7,3},{8,4},{9,5},{1... | collective-permute-start | bytes 368648 | tf_op jit(solution)/shard_map/ppermute | solution.py:37
  150.6 6.8 %collective-permute-start.9 = (bf16[240,256]{1,0:T(8,128)(2,1)S(1)}, bf16[240,256]{1,0:T(8,128)(2,1)S(1)}, u32[]{:S(2)}, u32[]{:S(2)}) collective-permute-start(bf16[240,256]{1,0:T(8,128)(2,1)S(1)} %pad_maximum_fusion.7), channel_id=1, source_target_pairs={{0,4},{1,5},{2,6},{3,7},{4,8},{5,9},{6,10},{7,11},{8,12},{9,13},{1... | collective-permute-start | bytes 368648 | tf_op jit(solution)/shard_map/ppermute | solution.py:37
  152.8 7.1 %collective-permute-start.10 = (bf16[240,256]{1,0:T(8,128)(2,1)S(1)}, bf16[240,256]{1,0:T(8,128)(2,1)S(1)}, u32[]{:S(2)}, u32[]{:S(2)}) collective-permute-start(bf16[240,256]{1,0:T(8,128)(2,1)S(1)} %pad_maximum_fusion.7), channel_id=1, source_target_pairs={{0,8},{1,9},{2,10},{3,11},{4,12},{5,13},{6,14},{7,15},{8,0},{9,1},... | collective-permute-start | bytes 368648 | tf_op jit(solution)/shard_map/ppermute | solution.py:37
  163.2 10.5 %collective-permute-start.14 = (bf16[464,256]{1,0:T(8,128)(2,1)S(1)}, bf16[464,256]{1,0:T(8,128)(2,1)}, u32[]{:S(2)}, u32[]{:S(2)}) collective-permute-start(bf16[464,256]{1,0:T(8,128)(2,1)S(1)} %get-tuple-element.27), channel_id=1, source_target_pairs={{0,1},{1,2},{2,3},{3,0},{4,5},{5,6},{6,7},{7,4},{8,9},{9,10},{10,1... | collective-permute-start | bytes 712712 | tf_op jit(solution)/shard_map/ppermute | solution.py:32
  167.3 7.1 %collective-permute-start.12 = (bf16[464,256]{1,0:T(8,128)(2,1)S(1)}, bf16[464,256]{1,0:T(8,128)(2,1)}, u32[]{:S(2)}, u32[]{:S(2)}) collective-permute-start(bf16[464,256]{1,0:T(8,128)(2,1)S(1)} %get-tuple-element.25), channel_id=1, source_target_pairs={{0,3},{1,0},{2,1},{3,2},{4,7},{5,4},{6,5},{7,6},{8,11},{9,8},{10,9... | collective-permute-start | bytes 712712 | tf_op jit(solution)/shard_map/ppermute | solution.py:32
  169.7 9.0 %collective-permute-start.13 = (bf16[464,256]{1,0:T(8,128)(2,1)S(1)}, bf16[464,256]{1,0:T(8,128)(2,1)}, u32[]{:S(2)}, u32[]{:S(2)}) collective-permute-start(bf16[464,256]{1,0:T(8,128)(2,1)S(1)} %get-tuple-element.26), channel_id=1, source_target_pairs={{0,2},{1,3},{2,0},{3,1},{4,6},{5,7},{6,4},{7,5},{8,10},{9,11},{10,... | collective-permute-start | bytes 712712 | tf_op jit(solution)/shard_map/ppermute | solution.py:32
  182.5 87.3 %all-to-all-start.1 = ((bf16[64,4,896]{2,1,0:T(4,128)(2,1)}), bf16[64,4,896]{2,1,0:T(4,128)(2,1)S(1)}, u32[]{:S(2)}, u32[]{:S(2)}) async-start(bf16[64,4,896]{2,1,0:T(4,128)(2,1)} %reshape.518), calls=%async_computation.1 | async-start | bytes 917504 | tf_op jit(solution)/shard_map/all_to_all | solution.py:57
  (1 other events, 1.9 us)
Sparse Core Ops, SparseCore 0:
  55.6 73.4 all-gather.1

commit v3 on v1

--- a/solution.py
+++ b/solution.py
@@ -1,6 +1,9 @@
+import functools
+
 import jax
 import jax.numpy as jnp
 from jax import lax
+from jax.experimental import pallas as pl
 from jax.sharding import PartitionSpec as P
 
 BF16 = jnp.bfloat16
@@ -8,6 +11,8 @@
 I32 = jnp.int32
 SIDE = 4
 PIECES = 16
+COST = 1000000
+BYTES = 400000000
 
 
 def contract(left, right, dims):
@@ -27,6 +32,28 @@
     return jnp.sum(rows.astype(F32), axis=(0, 1))[None, :]
 
 
+def place_kernel(half, owner_row, owner_column, live, left, right):
+    tokens = owner_row.shape[1]
+    below = lax.broadcasted_iota(I32, (tokens, tokens), 0)
+    across = lax.broadcasted_iota(I32, (tokens, tokens), 1)
+    earlier = (owner_column[...] == owner_row[...]) & (below < across)
+    rank = jnp.sum(earlier.astype(I32), axis=0, keepdims=True)
+    base = owner_row[...] * half
+    row = lax.broadcasted_iota(I32, left.shape, 0)
+    used = live[...] != 0
+    left[...] = jnp.where((row == base + rank) & (rank < half) & used, 1.0, 0.0).astype(BF16)
+    right[...] = jnp.where((row == base + rank - half) & (rank >= half) & used, 1.0, 0.0).astype(BF16)
+
+
+def placed(owner, live, half, slots):
+    tokens = owner.shape[0]
+    return pl.pallas_call(
+        functools.partial(place_kernel, half),
+        out_shape=[jax.ShapeDtypeStruct((slots // 2, tokens), BF16)] * 2,
+        cost_estimate=pl.CostEstimate(flops=COST, bytes_accessed=BYTES, transcendentals=0),
+    )(owner[None, :], owner[:, None], live[None, :])
+
+
 def along_x(value):
     groups = [[SIDE * y + x for x in range(SIDE)] for y in range(SIDE)]
     return lax.all_to_all(value, "tp", 0, 0, tiled=True, axis_index_groups=groups)
@@ -39,6 +66,14 @@
 
 def to_all(value):
     return jnp.broadcast_to(value, (SIDE,) + value.shape)
+
+
+def exchange_rows(left, right):
+    groups = lax.axis_size("seq")
+    both = jnp.concatenate([left, right], axis=0).astype(BF16).T
+    both = both.reshape(groups, both.shape[0] // groups, both.shape[1])
+    moved = lax.all_to_all(both, "seq", split_axis=0, concat_axis=0, tiled=True)
+    return moved.reshape(-1, moved.shape[2])
 
 
 def local(hidden, next_ids, live_mask, emb_table, gain_hidden, gain_embed, projection, target):
@@ -80,32 +115,37 @@
     token = jnp.arange(tokens, dtype=I32)
     upto = (token[:, None] <= token[None, :]).astype(BF16)
     rank_all = contract(mine.astype(BF16), upto, (1, 0)).astype(I32) - 1
-    hit = mine[:, :, None] & (rank_all[:, :, None] == jnp.arange(capacity, dtype=I32))
     local_ids = ids_all - my_group * row_count
-    row_of_slot = jnp.sum(jnp.where(hit, local_ids[:, :, None] + 1, 0), axis=1).reshape(slots) - 1
-    pick = (row_of_slot[:, None] == jnp.arange(row_count, dtype=I32)[None, :]).astype(BF16)
-    outgoing = contract(pick, emb_table, (1, 0)).astype(BF16).reshape(groups, capacity, local_width)
-    fetched = lax.all_to_all(outgoing, "seq", split_axis=0, concat_axis=0, tiled=True)
+    half = capacity // 2
+    row = jnp.arange(row_count, dtype=I32)
+
+    def picked(first):
+        ranks = first + jnp.arange(half, dtype=I32)
+        hit = mine[:, None, :] & (rank_all[:, None, :] == ranks[None, :, None])
+        rows = jnp.sum(jnp.where(hit, local_ids[:, None, :] + 1, 0), axis=2).reshape(slots // 2) - 1
+        return (row[:, None] == rows[None, :]).astype(BF16)
+
+    pick_left, pick_right = picked(0), picked(half)
+    table_t = emb_table.T
+    fetched = exchange_rows(contract(table_t, pick_left, (1, 0)), contract(table_t, pick_right, (1, 0)))
 
     ids_mine = lax.dynamic_index_in_dim(ids_all, my_group, 0, keepdims=False)
     owner = ids_mine // row_count
-    earlier = (owner[:, None] == owner[None, :]) & (token[:, None] < token[None, :])
-    slot = owner * capacity + jnp.sum(earlier.astype(I32), axis=0)
-    place = (jnp.arange(slots, dtype=I32)[:, None] == slot[None, :]) & (live_mask[None, :] != 0)
-    place = place.astype(BF16)
+    place_left, place_right = placed(owner, live_mask, half, slots)
 
-    emb = contract(fetched.reshape(slots, local_width), place, (0, 0))
+    emb = contract(fetched, place_left, (0, 0))[:local_width] + contract(fetched, place_right, (0, 0))[local_width:]
     gain = lax.dynamic_slice_in_dim(gain_embed, place_tp * local_width, local_width)[:, None]
     square_part = jnp.sum(emb * emb, axis=0, keepdims=True)
     got = along_x(to_all(jnp.concatenate([(emb * gain).astype(BF16), split_rows(square_part)], axis=0)))
     square_part = join_rows(got[:, local_width:])
     partial = contract(weights, got[:, :local_width].reshape(quarter, tokens), (1, 0)).astype(BF16)
+    partial, hid_all = lax.optimization_barrier((partial, hid_all))
     partial = partial.reshape(SIDE, columns, tokens)
     got = along_y(jnp.concatenate([partial, to_all(split_rows(square_part))], axis=1))
     emb_raw = jnp.sum(got[:, :columns].astype(F32), axis=0)
     scale = lax.rsqrt(join_rows(got[:, columns:]) / width + 1e-06)
 
-    hid_part = contract(proj_t[:, :width], hid_all, (1, 1))
+    hid_part = lax.optimization_barrier(contract(proj_t[:, :width], hid_all, (1, 1)))
     combined = hid_part + emb_raw * scale
     projected = combined.astype(BF16)
     upstream = (combined - target.T.astype(F32)).astype(BF16)
@@ -119,11 +159,11 @@
     curvature = join_rows(got[:, local_width:])
 
     emb_grad = scale * gain * feature_grad - scale * scale * scale * curvature / width * emb
-    returned = contract(place, emb_grad.astype(BF16), (1, 1)).astype(BF16)
-    arrived = lax.all_to_all(
-        returned.reshape(groups, capacity, local_width), "seq", split_axis=0, concat_axis=0, tiled=True
-    )
-    table_grad = contract(arrived.reshape(slots, local_width), pick, (0, 0)).astype(BF16)
+    emb_grad = emb_grad.astype(BF16)
+    arrived = exchange_rows(contract(emb_grad, place_left, (1, 1)), contract(emb_grad, place_right, (1, 1)))
+    table_grad = (
+        contract(arrived, pick_left, (0, 1))[:local_width] + contract(arrived, pick_right, (0, 1))[local_width:]
+    ).astype(BF16)
     return (projected.T, table_grad.T)
 
 

time: 273 us -> 260 us (0.952)
  blocking collectives: 123 us -> 98.5 us
  other arithmetic: 2.99 us -> 6.77 us
  starting transfers between devices: 45.3 us -> 48.9 us
    all_to_all x2 -> x1, blocking collectives: 22.2 us -> 9.15 us  [along_y(): lax.all_to_all(value, 'tp', 0, 0, tiled=True, axis_index_groups=groups)]
    all_to_all x1, blocking collectives: 88.9 us -> 76.9 us  [exchange_rows(): moved = lax.all_to_all(both, 'seq', split_axis=0, concat_axis=0, tiled=True)]
    all_to_all x1, waiting for transfers between devices: 13.1 us -> 19.6 us  [along_x(): lax.all_to_all(value, 'tp', 0, 0, tiled=True, axis_index_groups=groups)]
    all_to_all x1 -> x2, waiting for transfers between devices: 36.2 us -> 31.9 us  [the longest x1 29.1 us: exchange_rows(): moved = lax.all_to_all(both, 'seq', split_axis=0, concat_axis=0, tiled=True)]
    all_to_all x1 -> x2, starting transfers between devices: 30.6 us -> 34.2 us  [the longest x1 30.4 us: exchange_rows(): moved = lax.all_to_all(both, 'seq', split_axis=0, concat_axis=0, tiled=True)]
    dot_general x8 -> x12, matrix products: 16.4 us -> 14.6 us  [contract(): lax.dot_general(left, right, ((dims[:1], dims[1:]), ((), ())), preferred_...]
  transfers between devices with their start and end apart: 6 -> 7, of which waited for: 3 -> 4; matrix products, arithmetic and copies ran while one was open for 7% -> 10% of each run, Pallas kernels for 0% -> 1%
where the time goes in v3:
time: 260 us; the launch traced here: 259 us
  blocking collectives  98.5 us (38%)
  waiting for transfers between devices  57.8 us (22%)
  starting transfers between devices  48.9 us (19%)
  local copies, waits for them, and re-layouts  16.3 us (6%)
  matrix products  14.6 us (6%)
  between operations  14.6 us (6%)
  other arithmetic  6.77 us (3%)
    all_to_all x1, blocking collectives, exchange_rows(): moved = lax.all_to_all(both, 'seq', split_axis=0, concat_axis=0, tiled=True)  76.9 us
    all_to_all x1, starting transfers between devices, exchange_rows(): moved = lax.all_to_all(both, 'seq', split_axis=0, concat_axis=0, tiled=True)  30.4 us
    all_to_all x1, waiting for transfers between devices, exchange_rows(): moved = lax.all_to_all(both, 'seq', split_axis=0, concat_axis=0, tiled=True)  29.1 us
    all_to_all x1, waiting for transfers between devices, along_x(): lax.all_to_all(value, 'tp', 0, 0, tiled=True, axis_index_groups=groups)  19.6 us
    dot_general x12, matrix products, contract(): lax.dot_general(left, right, ((dims[:1], dims[1:]), ((), ())), preferred_...  14.6 us
    all_to_all x1, blocking collectives, along_x(): lax.all_to_all(value, 'tp', 0, 0, tiled=True, axis_index_groups=groups)  12.4 us
    ppermute x3, starting transfers between devices, local(): lax.ppermute(piece((my_y + step) % SIDE), 'tp', [(SIDE * y + x, SIDE * ((...  10.7 us
    all_to_all x1, blocking collectives, along_y(): lax.all_to_all(value, 'tp', 0, 0, tiled=True, axis_index_groups=groups)  9.15 us
  transfers between devices with their start and end apart: 7, of which 4 were waited for; matrix products, arithmetic and copies ran while one was open for 10% of the time, Pallas kernels for 1%

profile of v3, /device:TPU:1, one launch (start us, length us, event | category | flops | bytes accessed | tf_op | source)
XLA Modules:
  0.0 259.3 jit_solution(11440866928579411516)
XLA Ops:
  7.2 1.2 fusion.15
  8.4 1.8 fusion.17
  14.2 30.4 %all-to-all-start = ((bf16[64,4,896]{2,1,0:T(4,128)(2,1)}), bf16[64,4,896]{2,1,0:T(4,128)(2,1)S(1)}, u32[]{:S(2)}, u32[]{:S(2)}) async-start(bf16[64,4,896]{2,1,0:T(4,128)(2,1)} %reshape.351), calls=%async_computation | async-start | bytes 917504 | tf_op jit(solution)/shard_map/all_to_all | solution.py:75
  44.6 3.1 %dynamic-slice_bitcast_fusion = (bf16[224,1792]{1,0:T(8,128)(2,1)}, bf16[224,1792]{1,0:T(8,128)(2,1)}, bf16[224,1792]{1,0:T(8,128)(2,1)}) fusion(bf16[14336,224]{0,1:T(8,128)(2,1)} %param.14, s32[]{:T(128)S(6)} %select_n.105, s32[]{:T(128)S(6)} %select_n.101, s32[]{:T(128)S(6)} %select_n.97), kind=kLoop, calls=%fused_computation.27 | loop fusion | bytes 4816908 | tf_op jit(solution)/shard_map/dynamic_slice | solution.py:100
  47.8 3.2 %collective-permute-start = (bf16[224,1792]{1,0:T(8,128)(2,1)}, bf16[224,1792]{1,0:T(8,128)(2,1)S(1)}, u32[]{:S(2)}, u32[]{:S(2)}) collective-permute-start(bf16[224,1792]{1,0:T(8,128)(2,1)} %get-tuple-element.16), channel_id=1, source_target_pairs={{0,4},{1,5},{2,6},{3,7},{4,8},{5,9},{6,10},{7,11},{8,12},{9,13},{1... | collective-permute-start | bytes 2408456 | tf_op jit(solution)/shard_map/ppermute | solution.py:105
  51.0 4.5 %collective-permute-start.1 = (bf16[224,1792]{1,0:T(8,128)(2,1)}, bf16[224,1792]{1,0:T(8,128)(2,1)}, u32[]{:S(2)}, u32[]{:S(2)}) collective-permute-start(bf16[224,1792]{1,0:T(8,128)(2,1)} %get-tuple-element.15), channel_id=1, source_target_pairs={{0,8},{1,9},{2,10},{3,11},{4,12},{5,13},{6,14},{7,15},{8,0},{9,1},... | collective-permute-start | bytes 2408456 | tf_op jit(solution)/shard_map/ppermute | solution.py:105
  55.5 3.0 %collective-permute-start.2 = (bf16[224,1792]{1,0:T(8,128)(2,1)}, bf16[224,1792]{1,0:T(8,128)(2,1)S(1)}, u32[]{:S(2)}, u32[]{:S(2)}) collective-permute-start(bf16[224,1792]{1,0:T(8,128)(2,1)} %get-tuple-element.14), channel_id=1, source_target_pairs={{0,12},{1,13},{2,14},{3,15},{4,0},{5,1},{6,2},{7,3},{8,4},{9,5},{1... | collective-permute-start | bytes 2408456 | tf_op jit(solution)/shard_map/ppermute | solution.py:105
  60.8 1.8 shard_map.95
  62.6 1.9 broadcast_in_dim.36
  64.5 2.1 bitcast_dynamic-update-slice_fusion
  66.6 6.2 %collective-permute-done = bf16[224,1792]{1,0:T(8,128)(2,1)S(1)} collective-permute-done((bf16[224,1792]{1,0:T(8,128)(2,1)}, bf16[224,1792]{1,0:T(8,128)(2,1)S(1)}, u32[]{:S(2)}, u32[]{:S(2)}) %collective-permute-start) | collective-permute-done | bytes 802848 | tf_op jit(solution)/shard_map/ppermute | solution.py:105
  73.8 29.1 %all-to-all-done = bf16[64,4,896]{2,1,0:T(4,128)(2,1)S(1)} async-done(((bf16[64,4,896]{2,1,0:T(4,128)(2,1)}), bf16[64,4,896]{2,1,0:T(4,128)(2,1)S(1)}, u32[]{:S(2)}, u32[]{:S(2)}) %all-to-all-start) | async-done | bytes 458784 | tf_op jit(solution)/shard_map/all_to_all | solution.py:75
  104.9 4.0 %all-to-all-start.1 = ((bf16[4,464,256]{2,1,0:T(8,128)(2,1)}), bf16[4,464,256]{2,1,0:T(8,128)(2,1)S(1)}, u32[]{:S(2)}, u32[]{:S(2)}) async-start(bf16[4,464,256]{2,1,0:T(8,128)(2,1)} %broadcast_in_dim.79), calls=%async_computation.1 | async-start | bytes 1900544 | tf_op jit(solution)/shard_map/all_to_all | solution.py:59
  108.9 2.2 bitcast_dynamic-update-slice_fusion.2
  112.0 19.6 %all-to-all-done.1 = bf16[4,464,256]{2,1,0:T(8,128)(2,1)S(1)} async-done(((bf16[4,464,256]{2,1,0:T(8,128)(2,1)}), bf16[4,464,256]{2,1,0:T(8,128)(2,1)S(1)}, u32[]{:S(2)}, u32[]{:S(2)}) %all-to-all-start.1) | async-done | bytes 950304 | tf_op jit(solution)/shard_map/all_to_all | solution.py:59
  131.7 2.9 %convolution_convert_fusion = bf16[896,256]{1,0:T(8,128)(2,1)S(1)} fusion(bf16[896,1792]{1,0:T(8,128)(2,1)} %bitcast.8, bf16[1792,256]{1,0:T(8,128)(2,1)S(1)} %bitcast.65), kind=kOutput, calls=%fused_computation.7 | convolution fusion | flops 822312960 | bytes 4587520 | tf_op jit(solution)/shard_map/dot_general | solution.py:19
  135.5 3.8 %all-to-all-start.2 = ((bf16[4,240,256]{2,1,0:T(8,128)(2,1)}), bf16[4,240,256]{2,1,0:T(8,128)(2,1)S(1)}, u32[]{:S(2)}, u32[]{:S(2)}) async-start(bf16[4,240,256]{2,1,0:T(8,128)(2,1)} %pad_maximum_fusion.1), calls=%async_computation.2 | async-start | bytes 983040 | tf_op jit(solution)/shard_map/all_to_all | solution.py:64
  139.3 4.3 %fusion.4 = f32[224,256]{1,0:T(8,128)S(1)} fusion(bf16[256,7168]{1,0:T(8,128)(2,1)} %all-gather.2.cloned.1.call-done, bf16[224,14336]{1,0:T(8,128)(2,1)} %bitcast.64), kind=kOutput, calls=%fused_computation.13 | convolution fusion | flops 822083584 | bytes 7110656 | tf_op jit(solution)/shard_map/dot_general | solution.py:19
  143.6 2.8 %all-to-all-done.2 = bf16[4,240,256]{2,1,0:T(8,128)(2,1)S(1)} async-done(((bf16[4,240,256]{2,1,0:T(8,128)(2,1)}), bf16[4,240,256]{2,1,0:T(8,128)(2,1)S(1)}, u32[]{:S(2)}, u32[]{:S(2)}) %all-to-all-start.2) | async-done | bytes 491552 | tf_op jit(solution)/shard_map/all_to_all | solution.py:64
  147.4 9.1 %all_to_all.30 = bf16[4,240,256]{2,1,0:T(8,128)(2,1)S(1)} all-to-all(bf16[4,240,256]{2,1,0:T(8,128)(2,1)S(1)} %broadcast_in_dim.81), channel_id=1, replica_groups={{0,4,8,12},{1,5,9,13},{2,6,10,14},{3,7,11,15},{16,20,24,28},{17,21,25,2..., dimensions={0} | all-to-all | bytes 983040 | tf_op jit(solution)/shard_map/all_to_all | solution.py:64
  156.6 3.1 %fusion.2 = bf16[1792,256]{1,0:T(8,128)(2,1)S(1)} fusion(bf16[4,224,1792]{2,1,0:T(8,128)(2,1)} %bitcast_dynamic-update-slice_fusion.1, bf16[4,240,256]{2,1,0:T(8,128)(2,1)S(1)} %all_to_all.30), kind=kOutput, calls=%fused_computation.3 | convolution fusion | flops 822542336 | bytes 4587520 | tf_op jit(solution)/shard_map/dot_general | solution.py:19
  159.7 12.4 %all_to_all.31 = bf16[4,464,256]{2,1,0:T(8,128)(2,1)S(1)} all-to-all(bf16[4,464,256]{2,1,0:T(8,128)(2,1)S(1)} %pad_maximum_fusion), channel_id=1, replica_groups={{0,1,2,3},{4,5,6,7},{8,9,10,11},{12,13,14,15},{16,17,18,19},{20,21,22,2..., dimensions={0} | all-to-all | bytes 1900544 | tf_op jit(solution)/shard_map/all_to_all | solution.py:59
  173.4 76.9 %all_to_all.32 = bf16[64,4,896]{2,1,0:T(4,128)(2,1)S(1)} all-to-all(bf16[64,4,896]{2,1,0:T(4,128)(2,1)S(1)} %reshape.356), channel_id=1, replica_groups=mesh['seq'=64,'tp'=16] {'seq'}, dimensions={0} | all-to-all | bytes 917504 | tf_op jit(solution)/shard_map/all_to_all | solution.py:75
  250.9 1.6 fusion.3
  (77 shorter events, 13.7 us)
Async XLA Ops:
  7.2 4.8 %copy-start = (bf16[1024,448]{0,1:T(8,128)(2,1)S(1)}, bf16[1024,448]{0,1:T(8,128)(2,1)}, u32[]{:S(2)}) copy-start(bf16[1024,448]{0,1:T(8,128)(2,1)} %param.11) | copy-start | bytes 2752516
  7.2 127.5 %all-gather.2.cloned.1.call-start = ((), (), s32[]{:S(2)}) async-start(), calls=%async_computation.6 | async-start | bytes 3899392 | tf_op jit(solution)/shard_map/all_gather | solution.py:95
  14.2 88.7 %all-to-all-start = ((bf16[64,4,896]{2,1,0:T(4,128)(2,1)}), bf16[64,4,896]{2,1,0:T(4,128)(2,1)S(1)}, u32[]{:S(2)}, u32[]{:S(2)}) async-start(bf16[64,4,896]{2,1,0:T(4,128)(2,1)} %reshape.351), calls=%async_computation | async-start | bytes 917504 | tf_op jit(solution)/shard_map/all_to_all | solution.py:75
  47.8 25.1 %collective-permute-start = (bf16[224,1792]{1,0:T(8,128)(2,1)}, bf16[224,1792]{1,0:T(8,128)(2,1)S(1)}, u32[]{:S(2)}, u32[]{:S(2)}) collective-permute-start(bf16[224,1792]{1,0:T(8,128)(2,1)} %get-tuple-element.16), channel_id=1, source_target_pairs={{0,4},{1,5},{2,6},{3,7},{4,8},{5,9},{6,10},{7,11},{8,12},{9,13},{1... | collective-permute-start | bytes 2408456 | tf_op jit(solution)/shard_map/ppermute | solution.py:105
  51.0 57.9 %collective-permute-start.1 = (bf16[224,1792]{1,0:T(8,128)(2,1)}, bf16[224,1792]{1,0:T(8,128)(2,1)}, u32[]{:S(2)}, u32[]{:S(2)}) collective-permute-start(bf16[224,1792]{1,0:T(8,128)(2,1)} %get-tuple-element.15), channel_id=1, source_target_pairs={{0,8},{1,9},{2,10},{3,11},{4,12},{5,13},{6,14},{7,15},{8,0},{9,1},... | collective-permute-start | bytes 2408456 | tf_op jit(solution)/shard_map/ppermute | solution.py:105
  55.5 55.6 %collective-permute-start.2 = (bf16[224,1792]{1,0:T(8,128)(2,1)}, bf16[224,1792]{1,0:T(8,128)(2,1)S(1)}, u32[]{:S(2)}, u32[]{:S(2)}) collective-permute-start(bf16[224,1792]{1,0:T(8,128)(2,1)} %get-tuple-element.14), channel_id=1, source_target_pairs={{0,12},{1,13},{2,14},{3,15},{4,0},{5,1},{6,2},{7,3},{8,4},{9,5},{1... | collective-permute-start | bytes 2408456 | tf_op jit(solution)/shard_map/ppermute | solution.py:105
  62.6 40.4 %copy-start.1 = (bf16[256,256]{1,0:T(8,128)(2,1)S(1)}, bf16[256,256]{1,0:T(8,128)(2,1)}, u32[]{:S(2)}) copy-start(bf16[256,256]{1,0:T(8,128)(2,1)} %get-tuple-element.6) | copy-start | bytes 393220
  64.5 38.8 %copy-start.2 = (bf16[256,256]{1,0:T(8,128)(2,1)S(1)}, bf16[256,256]{1,0:T(8,128)(2,1)}, u32[]{:S(2)}) copy-start(bf16[256,256]{1,0:T(8,128)(2,1)} %get-tuple-element.7) | copy-start | bytes 393220
  104.9 26.7 %all-to-all-start.1 = ((bf16[4,464,256]{2,1,0:T(8,128)(2,1)}), bf16[4,464,256]{2,1,0:T(8,128)(2,1)S(1)}, u32[]{:S(2)}, u32[]{:S(2)}) async-start(bf16[4,464,256]{2,1,0:T(8,128)(2,1)} %broadcast_in_dim.79), calls=%async_computation.1 | async-start | bytes 1900544 | tf_op jit(solution)/shard_map/all_to_all | solution.py:59
  135.5 11.0 %all-to-all-start.2 = ((bf16[4,240,256]{2,1,0:T(8,128)(2,1)}), bf16[4,240,256]{2,1,0:T(8,128)(2,1)S(1)}, u32[]{:S(2)}, u32[]{:S(2)}) async-start(bf16[4,240,256]{2,1,0:T(8,128)(2,1)} %pad_maximum_fusion.1), calls=%async_computation.2 | async-start | bytes 983040 | tf_op jit(solution)/shard_map/all_to_all | solution.py:64
  139.3 7.3 %copy-start.3 = (bf16[256,224]{0,1:T(8,128)(2,1)S(1)}, bf16[256,224]{0,1:T(8,128)(2,1)}, u32[]{:S(2)}) copy-start(bf16[256,224]{0,1:T(8,128)(2,1)} %param.15) | copy-start | bytes 344068
Sparse Core Ops, SparseCore 0:
  12.2 117.3 all-gather.1

commit v4 on v3

--- a/solution.py
+++ b/solution.py
@@ -10,26 +10,25 @@
 F32 = jnp.float32
 I32 = jnp.int32
 SIDE = 4
+CORES = 2
 PIECES = 16
-COST = 1000000
-BYTES = 400000000
 
 
 def contract(left, right, dims):
     return lax.dot_general(left, right, ((dims[:1], dims[1:]), ((), ())), preferred_element_type=F32)
 
 
-def split_rows(row):
-    high = row.astype(BF16)
-    rest = row - high.astype(F32)
+def split_rows(rows):
+    high = rows.astype(BF16)
+    rest = rows - high.astype(F32)
     middle = rest.astype(BF16)
     low = (rest - middle.astype(F32)).astype(BF16)
     pieces = jnp.concatenate([high, middle, low], axis=0)
-    return jnp.pad(pieces, ((0, PIECES - 3), (0, 0)))
-
-
-def join_rows(rows):
-    return jnp.sum(rows.astype(F32), axis=(0, 1))[None, :]
+    return jnp.pad(pieces, ((0, PIECES - pieces.shape[0]), (0, 0)))
+
+
+def join_rows(messages, count):
+    return sum(jnp.sum(messages[:, k * count : (k + 1) * count].astype(F32), axis=0) for k in range(3))
 
 
 def place_kernel(half, owner_row, owner_column, live, left, right):
@@ -50,7 +49,6 @@
     return pl.pallas_call(
         functools.partial(place_kernel, half),
         out_shape=[jax.ShapeDtypeStruct((slots // 2, tokens), BF16)] * 2,
-        cost_estimate=pl.CostEstimate(flops=COST, bytes_accessed=BYTES, transcendentals=0),
     )(owner[None, :], owner[:, None], live[None, :])
 
 
@@ -89,26 +87,36 @@
     columns = projection.shape[1]
     quarter = width // SIDE
 
+    hid_all = lax.all_gather(hidden, "tp", axis=0, tiled=True)
     hidden_f32 = hidden.astype(F32)
-    hidden_scale = lax.rsqrt(jnp.mean(hidden_f32 * hidden_f32, axis=-1, keepdims=True) + 1e-06)
-    hid_norm = (hidden_f32 * hidden_scale * gain_hidden).astype(BF16)
-    hid_all = lax.all_gather(hid_norm, "tp", axis=0, tiled=True)
+    hidden_scale = lax.rsqrt(jnp.mean(hidden_f32 * hidden_f32, axis=-1) + 1e-06)
+    rows_here = hidden.shape[0]
+    lane = jnp.arange(tokens, dtype=I32)
+    hidden_scale = jnp.where(lane // rows_here == place_tp, jnp.tile(hidden_scale, tokens // rows_here), 0.0)
 
     proj_t = projection.T
+    part = columns // CORES
+    my_core = my_group % CORES
 
     def piece(y):
-        return lax.dynamic_slice(proj_t, (0, width + y * quarter), (columns, quarter))
-
-    weights = jnp.zeros((SIDE, columns, quarter), BF16)
-    weights = lax.dynamic_update_slice(weights, piece(my_y)[None], (my_y, 0, 0))
+        return lax.dynamic_slice(proj_t, (my_core * part, width + y * quarter), (part, quarter))
+
+    fetched_half = jnp.zeros((SIDE, part, quarter), BF16)
+    fetched_half = lax.dynamic_update_slice(fetched_half, piece(my_y)[None], (my_y, 0, 0))
     for step in range(1, SIDE):
         moved = lax.ppermute(
             piece((my_y + step) % SIDE),
             "tp",
             [(SIDE * y + x, SIDE * ((y + step) % SIDE) + x) for y in range(SIDE) for x in range(SIDE)],
         )
-        weights = lax.dynamic_update_slice(weights, moved[None], ((my_y - step) % SIDE, 0, 0))
-    weights = weights.reshape(SIDE * columns, quarter)
+        fetched_half = lax.dynamic_update_slice(fetched_half, moved[None], ((my_y - step) % SIDE, 0, 0))
+    other_half = lax.ppermute(fetched_half, "seq", [(k, k ^ 1) for k in range(groups)])
+    weights_here = fetched_half.reshape(SIDE * part, quarter)
+    weights_other = other_half.reshape(SIDE * part, quarter)
+    first = my_core == 0
+
+    def ordered(here, other):
+        return jnp.where(first, here, other), jnp.where(first, other, here)
 
     ids_all = next_ids.reshape(groups, tokens)
     mine = ids_all // row_count == my_group
@@ -135,28 +143,35 @@
 
     emb = contract(fetched, place_left, (0, 0))[:local_width] + contract(fetched, place_right, (0, 0))[local_width:]
     gain = lax.dynamic_slice_in_dim(gain_embed, place_tp * local_width, local_width)[:, None]
-    square_part = jnp.sum(emb * emb, axis=0, keepdims=True)
-    got = along_x(to_all(jnp.concatenate([(emb * gain).astype(BF16), split_rows(square_part)], axis=0)))
-    square_part = join_rows(got[:, local_width:])
-    partial = contract(weights, got[:, :local_width].reshape(quarter, tokens), (1, 0)).astype(BF16)
-    partial, hid_all = lax.optimization_barrier((partial, hid_all))
-    partial = partial.reshape(SIDE, columns, tokens)
-    got = along_y(jnp.concatenate([partial, to_all(split_rows(square_part))], axis=1))
+    squares = jnp.sum(emb * emb, axis=0, keepdims=True)
+    shared = jnp.concatenate([squares, hidden_scale[None, :]], axis=0)
+    got = along_x(to_all(jnp.concatenate([(emb * gain).astype(BF16), split_rows(shared)], axis=0)))
+    shared = join_rows(got[:, local_width:], 2)
+    features = got[:, :local_width].reshape(quarter, tokens)
+    features, hid_all = lax.optimization_barrier((features, hid_all))
+    halves = ordered(contract(weights_here, features, (1, 0)), contract(weights_other, features, (1, 0)))
+    halves = [half_rows.astype(BF16).reshape(SIDE, part, tokens) for half_rows in halves]
+    got = along_y(jnp.concatenate([*halves, to_all(split_rows(shared))], axis=1))
     emb_raw = jnp.sum(got[:, :columns].astype(F32), axis=0)
-    scale = lax.rsqrt(join_rows(got[:, columns:]) / width + 1e-06)
-
-    hid_part = lax.optimization_barrier(contract(proj_t[:, :width], hid_all, (1, 1)))
-    combined = hid_part + emb_raw * scale
+    shared = join_rows(got[:, columns:], 2)
+    scale = lax.rsqrt(shared[:1] / width + 1e-06)
+    hidden_scale = shared[1:]
+
+    hid_gained = (hid_all.astype(F32) * gain_hidden).astype(BF16)
+    hid_raw = lax.optimization_barrier(contract(proj_t[:, :width], hid_gained, (1, 1)))
+    combined = hid_raw * hidden_scale + emb_raw * scale
     projected = combined.astype(BF16)
     upstream = (combined - target.T.astype(F32)).astype(BF16)
-    curve_part = jnp.sum(upstream.astype(F32) * emb_raw, axis=0, keepdims=True)
-    got = along_y(to_all(jnp.concatenate([upstream, split_rows(curve_part)], axis=0)))
-    curve_part = join_rows(got[:, columns:])
-    partial = contract(weights, got[:, :columns].reshape(SIDE * columns, tokens), (0, 0)).astype(BF16)
-    partial = partial.reshape(SIDE, local_width, tokens)
-    got = along_x(jnp.concatenate([partial, to_all(split_rows(curve_part))], axis=1))
+    curve = jnp.sum(upstream.astype(F32) * emb_raw, axis=0, keepdims=True)
+    got = along_y(to_all(jnp.concatenate([upstream, split_rows(curve)], axis=0)))
+    curve = join_rows(got[:, columns:], 1)
+    here, other = ordered(got[:, :part], got[:, part:columns])
+    partial = contract(weights_here, here.reshape(SIDE * part, tokens), (0, 0))
+    partial = partial + contract(weights_other, other.reshape(SIDE * part, tokens), (0, 0))
+    partial = partial.astype(BF16).reshape(SIDE, local_width, tokens)
+    got = along_x(jnp.concatenate([partial, to_all(split_rows(curve))], axis=1))
     feature_grad = jnp.sum(got[:, :local_width].astype(F32), axis=0)
-    curvature = join_rows(got[:, local_width:])
+    curvature = join_rows(got[:, local_width:], 1)
 
     emb_grad = scale * gain * feature_grad - scale * scale * scale * curvature / width * emb
     emb_grad = emb_grad.astype(BF16)

time: 260 us -> 260 us (level)
  blocking collectives: 98.5 us -> 104 us
  waiting for transfers between devices: 57.8 us -> 52.5 us
  local copies, waits for them, and re-layouts: 16.3 us -> 11.9 us
  starting transfers between devices: 48.9 us -> 52.6 us
  other arithmetic: 6.77 us -> 4.1 us
    all_to_all x1, waiting for transfers between devices: 19.6 us -> 10.1 us  [along_x(): lax.all_to_all(value, 'tp', 0, 0, tiled=True, axis_index_groups=groups)]
    all_to_all x1, blocking collectives: 76.9 us -> 83.1 us  [exchange_rows(): moved = lax.all_to_all(both, 'seq', split_axis=0, concat_axis=0, tiled=True)]
    ppermute x3, waiting for transfers between devices: 6.23 us -> 11.4 us  [local(): lax.ppermute(piece((my_y + step) % SIDE), 'tp', [(SIDE * y + x, SIDE * ((...]
    ppermute x0 -> x1, starting transfers between devices: none -> 4.48 us  [local(): lax.ppermute(fetched_half, 'seq', [(k, k ^ 1) for k in range(groups)])]
    dynamic_update_slice x4, local copies, waits for them, and re-layouts: 6.17 us -> 3.14 us  [the longest x3 2.1 us: local(): lax.dynamic_update_slice(fetched_half, moved[None], ((my_y - step) % SIDE...]
    dot_general x12 -> x14, matrix products: 14.6 us -> 17.1 us  [contract(): lax.dot_general(left, right, ((dims[:1], dims[1:]), ((), ())), preferred_...]
  transfers between devices with their start and end apart: 7 -> 8, of which waited for: 4 -> 5; matrix products, arithmetic and copies ran while one was open for 10% -> 8% of each run, Pallas kernels for 1% -> 1%
where the time goes in v4:
time: 260 us; the launch traced here: 259 us
  blocking collectives  104 us (40%)
  starting transfers between devices  52.6 us (20%)
  waiting for transfers between devices  52.5 us (20%)
  matrix products  17.1 us (7%)
  between operations  14.7 us (6%)
  local copies, waits for them, and re-layouts  11.9 us (5%)
  other arithmetic  4.1 us (2%)
    all_to_all x1, blocking collectives, exchange_rows(): moved = lax.all_to_all(both, 'seq', split_axis=0, concat_axis=0, tiled=True)  83.1 us
    all_to_all x1, starting transfers between devices, exchange_rows(): moved = lax.all_to_all(both, 'seq', split_axis=0, concat_axis=0, tiled=True)  30.5 us
    all_to_all x1, waiting for transfers between devices, exchange_rows(): moved = lax.all_to_all(both, 'seq', split_axis=0, concat_axis=0, tiled=True)  27.8 us
    dot_general x14, matrix products, contract(): lax.dot_general(left, right, ((dims[:1], dims[1:]), ((), ())), preferred_...  17.1 us
    all_to_all x1, blocking collectives, along_x(): lax.all_to_all(value, 'tp', 0, 0, tiled=True, axis_index_groups=groups)  12.1 us
    ppermute x3, waiting for transfers between devices, local(): lax.ppermute(piece((my_y + step) % SIDE), 'tp', [(SIDE * y + x, SIDE * ((...  11.4 us
    ppermute x3, starting transfers between devices, local(): lax.ppermute(piece((my_y + step) % SIDE), 'tp', [(SIDE * y + x, SIDE * ((...  10.1 us
    all_to_all x1, waiting for transfers between devices, along_x(): lax.all_to_all(value, 'tp', 0, 0, tiled=True, axis_index_groups=groups)  10.1 us
  transfers between devices with their start and end apart: 8, of which 5 were waited for; matrix products, arithmetic and copies ran while one was open for 8% of the time, Pallas kernels for 1%

profile of v4, /device:TPU:1, one launch (start us, length us, event | category | flops | bytes accessed | tf_op | source)
XLA Modules:
  0.0 259.1 jit_solution(13549692724347084004)
XLA Ops:
  11.9 30.5 %all-to-all-start = ((bf16[64,4,896]{2,1,0:T(4,128)(2,1)}), bf16[64,4,896]{2,1,0:T(4,128)(2,1)S(1)}, u32[]{:S(2)}, u32[]{:S(2)}) async-start(bf16[64,4,896]{2,1,0:T(4,128)(2,1)} %reshape.357), calls=%async_computation | async-start | bytes 917504 | tf_op jit(solution)/shard_map/all_to_all | solution.py:73
  42.5 2.3 dynamic-slice_bitcast_fusion
  44.8 4.6 %collective-permute-start.2 = (bf16[112,1792]{1,0:T(8,128)(2,1)}, bf16[112,1792]{1,0:T(8,128)(2,1)}, u32[]{:S(2)}, u32[]{:S(2)}) collective-permute-start(bf16[112,1792]{1,0:T(8,128)(2,1)} %get-tuple-element.25), channel_id=1, source_target_pairs={{0,12},{1,13},{2,14},{3,15},{4,0},{5,1},{6,2},{7,3},{8,4},{9,5},{1... | collective-permute-start | bytes 1204232 | tf_op jit(solution)/shard_map/ppermute | solution.py:107
  49.4 1.9 collective-permute-start
  51.4 3.5 %collective-permute-start.1 = (bf16[112,1792]{1,0:T(8,128)(2,1)}, bf16[112,1792]{1,0:T(8,128)(2,1)S(1)}, u32[]{:S(2)}, u32[]{:S(2)}) collective-permute-start(bf16[112,1792]{1,0:T(8,128)(2,1)} %get-tuple-element.27), channel_id=1, source_target_pairs={{0,8},{1,9},{2,10},{3,11},{4,12},{5,13},{6,14},{7,15},{8,0},{9,1},... | collective-permute-start | bytes 1204232 | tf_op jit(solution)/shard_map/ppermute | solution.py:107
  57.5 1.8 shard_map.95
  60.5 5.9 %collective-permute-done = bf16[112,1792]{1,0:T(8,128)(2,1)} collective-permute-done((bf16[112,1792]{1,0:T(8,128)(2,1)}, bf16[112,1792]{1,0:T(8,128)(2,1)}, u32[]{:S(2)}, u32[]{:S(2)}) %collective-permute-start) | collective-permute-done | bytes 401440 | tf_op jit(solution)/shard_map/ppermute | solution.py:107
  67.4 5.5 %collective-permute-done.1 = bf16[112,1792]{1,0:T(8,128)(2,1)S(1)} collective-permute-done((bf16[112,1792]{1,0:T(8,128)(2,1)}, bf16[112,1792]{1,0:T(8,128)(2,1)S(1)}, u32[]{:S(2)}, u32[]{:S(2)}) %collective-permute-start.1) | collective-permute-done | bytes 401440 | tf_op jit(solution)/shard_map/ppermute | solution.py:107
  72.9 27.8 %all-to-all-done = bf16[64,4,896]{2,1,0:T(4,128)(2,1)S(1)} async-done(((bf16[64,4,896]{2,1,0:T(4,128)(2,1)}), bf16[64,4,896]{2,1,0:T(4,128)(2,1)S(1)}, u32[]{:S(2)}, u32[]{:S(2)}) %all-to-all-start) | async-done | bytes 458784 | tf_op jit(solution)/shard_map/all_to_all | solution.py:73
  100.8 1.2 fusion.20
  102.0 2.1 multiply_convert_fusion.4
  105.2 4.0 %all-to-all-start.1 = ((bf16[4,464,256]{2,1,0:T(8,128)(2,1)}), bf16[4,464,256]{2,1,0:T(8,128)(2,1)S(1)}, u32[]{:S(2)}, u32[]{:S(2)}) async-start(bf16[4,464,256]{2,1,0:T(8,128)(2,1)} %broadcast_in_dim.78), calls=%async_computation.1 | async-start | bytes 1900544 | tf_op jit(solution)/shard_map/all_to_all | solution.py:57
  109.2 1.0 bitcast_dynamic-update-slice_fusion.1
  110.3 4.5 %collective-permute-start.3 = (bf16[4,112,1792]{2,1,0:T(8,128)(2,1)S(1)}, bf16[4,112,1792]{2,1,0:T(8,128)(2,1)}, u32[]{:S(2)}, u32[]{:S(2)}) collective-permute-start(bf16[4,112,1792]{2,1,0:T(8,128)(2,1)S(1)} %bitcast_dynamic-update-slice_fusion.1), channel_id=1, source_target_pairs={{0,16},{16,0},{32,48},{48,32},{64,80},{80,64},{96,112},{112,96},{1... | collective-permute-start | bytes 4816904 | tf_op jit(solution)/shard_map/ppermute | solution.py:113
  114.8 10.1 %all-to-all-done.1 = bf16[4,464,256]{2,1,0:T(8,128)(2,1)S(1)} async-done(((bf16[4,464,256]{2,1,0:T(8,128)(2,1)}), bf16[4,464,256]{2,1,0:T(8,128)(2,1)S(1)}, u32[]{:S(2)}, u32[]{:S(2)}) %all-to-all-start.1) | async-done | bytes 950304 | tf_op jit(solution)/shard_map/all_to_all | solution.py:57
  126.0 2.3 fusion.77
  129.8 3.5 %all-to-all-start.2 = ((bf16[4,240,256]{2,1,0:T(8,128)(2,1)}), bf16[4,240,256]{2,1,0:T(8,128)(2,1)S(1)}, u32[]{:S(2)}, u32[]{:S(2)}) async-start(bf16[4,240,256]{2,1,0:T(8,128)(2,1)} %pad_maximum_fusion.1), calls=%async_computation.2 | async-start | bytes 983040 | tf_op jit(solution)/shard_map/all_to_all | solution.py:62
  133.3 4.4 %fusion.6 = f32[224,256]{1,0:T(8,128)S(1)} fusion(bf16[224,14336]{1,0:T(8,128)(2,1)} %bitcast.79, bf16[256,7168]{1,0:T(8,128)(2,1)} %all-gather.2.cloned.1.call-done, f32[7168]{0:T(1024)S(1)} %copy-done.7), kind=kOutput, calls=%fused_computation.16 | convolution fusion | flops 827588608 | bytes 7139328 | tf_op jit(solution)/shard_map/dot_general | solution.py:18
  137.6 2.6 all-to-all-done.2
  141.1 9.1 %all_to_all.30 = bf16[4,240,256]{2,1,0:T(8,128)(2,1)S(1)} all-to-all(bf16[4,240,256]{2,1,0:T(8,128)(2,1)S(1)} %broadcast_in_dim.85), channel_id=1, replica_groups={{0,4,8,12},{1,5,9,13},{2,6,10,14},{3,7,11,15},{16,20,24,28},{17,21,25,2..., dimensions={0} | all-to-all | bytes 983040 | tf_op jit(solution)/shard_map/all_to_all | solution.py:62
  150.3 2.1 convolution_bitcast_fusion
  153.3 12.1 %all_to_all.31 = bf16[4,464,256]{2,1,0:T(8,128)(2,1)S(1)} all-to-all(bf16[4,464,256]{2,1,0:T(8,128)(2,1)S(1)} %pad_maximum_fusion), channel_id=1, replica_groups={{0,1,2,3},{4,5,6,7},{8,9,10,11},{12,13,14,15},{16,17,18,19},{20,21,22,2..., dimensions={0} | all-to-all | bytes 1900544 | tf_op jit(solution)/shard_map/all_to_all | solution.py:57
  167.0 83.1 %all_to_all.32 = bf16[64,4,896]{2,1,0:T(4,128)(2,1)S(1)} all-to-all(bf16[64,4,896]{2,1,0:T(4,128)(2,1)S(1)} %reshape.365), channel_id=1, replica_groups=mesh['seq'=64,'tp'=16] {'seq'}, dimensions={0} | all-to-all | bytes 917504 | tf_op jit(solution)/shard_map/all_to_all | solution.py:73
  250.7 1.6 fusion.5
  (97 shorter events, 16.8 us)
Async XLA Ops:
  7.2 2.5 copy-start
  7.2 118.8 %all-gather.2.cloned.1.call-start = ((), (), s32[]{:S(2)}) async-start(), calls=%async_computation.6 | async-start | bytes 3899392 | tf_op jit(solution)/shard_map/all_gather | solution.py:90
  11.8 43.1 %copy-start.3 = (bf16[16,7168]{1,0:T(8,128)(2,1)S(1)}, bf16[16,7168]{1,0:T(8,128)(2,1)}, u32[]{:S(2)}) copy-start(bf16[16,7168]{1,0:T(8,128)(2,1)} %param.8) | copy-start | bytes 688132
  11.9 88.8 %all-to-all-start = ((bf16[64,4,896]{2,1,0:T(4,128)(2,1)}), bf16[64,4,896]{2,1,0:T(4,128)(2,1)S(1)}, u32[]{:S(2)}, u32[]{:S(2)}) async-start(bf16[64,4,896]{2,1,0:T(4,128)(2,1)} %reshape.357), calls=%async_computation | async-start | bytes 917504 | tf_op jit(solution)/shard_map/all_to_all | solution.py:73
  44.8 64.5 %collective-permute-start.2 = (bf16[112,1792]{1,0:T(8,128)(2,1)}, bf16[112,1792]{1,0:T(8,128)(2,1)}, u32[]{:S(2)}, u32[]{:S(2)}) collective-permute-start(bf16[112,1792]{1,0:T(8,128)(2,1)} %get-tuple-element.25), channel_id=1, source_target_pairs={{0,12},{1,13},{2,14},{3,15},{4,0},{5,1},{6,2},{7,3},{8,4},{9,5},{1... | collective-permute-start | bytes 1204232 | tf_op jit(solution)/shard_map/ppermute | solution.py:107
  49.4 17.0 %collective-permute-start = (bf16[112,1792]{1,0:T(8,128)(2,1)}, bf16[112,1792]{1,0:T(8,128)(2,1)}, u32[]{:S(2)}, u32[]{:S(2)}) collective-permute-start(bf16[112,1792]{1,0:T(8,128)(2,1)} %get-tuple-element.26), channel_id=1, source_target_pairs={{0,4},{1,5},{2,6},{3,7},{4,8},{5,9},{6,10},{7,11},{8,12},{9,13},{1... | collective-permute-start | bytes 1204232 | tf_op jit(solution)/shard_map/ppermute | solution.py:107
  51.4 21.6 %collective-permute-start.1 = (bf16[112,1792]{1,0:T(8,128)(2,1)}, bf16[112,1792]{1,0:T(8,128)(2,1)S(1)}, u32[]{:S(2)}, u32[]{:S(2)}) collective-permute-start(bf16[112,1792]{1,0:T(8,128)(2,1)} %get-tuple-element.27), channel_id=1, source_target_pairs={{0,8},{1,9},{2,10},{3,11},{4,12},{5,13},{6,14},{7,15},{8,0},{9,1},... | collective-permute-start | bytes 1204232 | tf_op jit(solution)/shard_map/ppermute | solution.py:107
  105.2 19.6 %all-to-all-start.1 = ((bf16[4,464,256]{2,1,0:T(8,128)(2,1)}), bf16[4,464,256]{2,1,0:T(8,128)(2,1)S(1)}, u32[]{:S(2)}, u32[]{:S(2)}) async-start(bf16[4,464,256]{2,1,0:T(8,128)(2,1)} %broadcast_in_dim.78), calls=%async_computation.1 | async-start | bytes 1900544 | tf_op jit(solution)/shard_map/all_to_all | solution.py:57
  110.3 15.7 %collective-permute-start.3 = (bf16[4,112,1792]{2,1,0:T(8,128)(2,1)S(1)}, bf16[4,112,1792]{2,1,0:T(8,128)(2,1)}, u32[]{:S(2)}, u32[]{:S(2)}) collective-permute-start(bf16[4,112,1792]{2,1,0:T(8,128)(2,1)S(1)} %bitcast_dynamic-update-slice_fusion.1), channel_id=1, source_target_pairs={{0,16},{16,0},{32,48},{48,32},{64,80},{80,64},{96,112},{112,96},{1... | collective-permute-start | bytes 4816904 | tf_op jit(solution)/shard_map/ppermute | solution.py:113
  126.0 2.3 copy-start.2
  128.9 4.3 %copy-start.7 = (f32[7168]{0:T(1024)S(1)}, f32[7168]{0:T(1024)}, u32[]{:S(2)}) copy-start(f32[7168]{0:T(1024)} %param.12) | copy-start | bytes 86020
  129.8 10.4 %all-to-all-start.2 = ((bf16[4,240,256]{2,1,0:T(8,128)(2,1)}), bf16[4,240,256]{2,1,0:T(8,128)(2,1)S(1)}, u32[]{:S(2)}, u32[]{:S(2)}) async-start(bf16[4,240,256]{2,1,0:T(8,128)(2,1)} %pad_maximum_fusion.1), calls=%async_computation.2 | async-start | bytes 983040 | tf_op jit(solution)/shard_map/all_to_all | solution.py:62
  133.2 7.1 %copy-start.6 = (bf16[256,224]{0,1:T(8,128)(2,1)S(1)}, bf16[256,224]{0,1:T(8,128)(2,1)}, u32[]{:S(2)}) copy-start(bf16[256,224]{0,1:T(8,128)(2,1)} %param.15) | copy-start | bytes 344068
  153.3 12.3 %copy-start.1 = (f32[448,256]{1,0:T(8,128)S(1)}, f32[448,256]{1,0:T(8,128)}, u32[]{:S(2)}) copy-start(f32[448,256]{1,0:T(8,128)} %get-tuple-element.48) | copy-start | bytes 1376260
  153.3 12.4 %copy-start.5 = (bf16[256,256]{1,0:T(8,128)(2,1)S(1)}, bf16[256,256]{1,0:T(8,128)(2,1)}, u32[]{:S(2)}) copy-start(bf16[256,256]{1,0:T(8,128)(2,1)} %get-tuple-element.7) | copy-start | bytes 393220
  165.4 0.9 copy-start.4
Sparse Core Ops, SparseCore 0:
  12.2 104.1 all-gather.1

commit v5 on v4

--- a/solution.py
+++ b/solution.py
@@ -88,11 +88,13 @@
     quarter = width // SIDE
 
     hid_all = lax.all_gather(hidden, "tp", axis=0, tiled=True)
-    hidden_f32 = hidden.astype(F32)
-    hidden_scale = lax.rsqrt(jnp.mean(hidden_f32 * hidden_f32, axis=-1) + 1e-06)
-    rows_here = hidden.shape[0]
-    lane = jnp.arange(tokens, dtype=I32)
-    hidden_scale = jnp.where(lane // rows_here == place_tp, jnp.tile(hidden_scale, tokens // rows_here), 0.0)
+
+    def scale_row():
+        hidden_f32 = hidden.astype(F32)
+        own = lax.rsqrt(jnp.mean(hidden_f32 * hidden_f32, axis=-1) + 1e-06)
+        rows_here = hidden.shape[0]
+        lane = jnp.arange(tokens, dtype=I32)
+        return jnp.where(lane // rows_here == place_tp, jnp.tile(own, tokens // rows_here), 0.0)
 
     proj_t = projection.T
     part = columns // CORES
@@ -101,18 +103,18 @@
     def piece(y):
         return lax.dynamic_slice(proj_t, (my_core * part, width + y * quarter), (part, quarter))
 
-    fetched_half = jnp.zeros((SIDE, part, quarter), BF16)
-    fetched_half = lax.dynamic_update_slice(fetched_half, piece(my_y)[None], (my_y, 0, 0))
-    for step in range(1, SIDE):
-        moved = lax.ppermute(
-            piece((my_y + step) % SIDE),
-            "tp",
-            [(SIDE * y + x, SIDE * ((y + step) % SIDE) + x) for y in range(SIDE) for x in range(SIDE)],
-        )
-        fetched_half = lax.dynamic_update_slice(fetched_half, moved[None], ((my_y - step) % SIDE, 0, 0))
-    other_half = lax.ppermute(fetched_half, "seq", [(k, k ^ 1) for k in range(groups)])
-    weights_here = fetched_half.reshape(SIDE * part, quarter)
-    weights_other = other_half.reshape(SIDE * part, quarter)
+    def fetch_half():
+        fetched_half = jnp.zeros((SIDE, part, quarter), BF16)
+        fetched_half = lax.dynamic_update_slice(fetched_half, piece(my_y)[None], (my_y, 0, 0))
+        for step in range(1, SIDE):
+            moved = lax.ppermute(
+                piece((my_y + step) % SIDE),
+                "tp",
+                [(SIDE * y + x, SIDE * ((y + step) % SIDE) + x) for y in range(SIDE) for x in range(SIDE)],
+            )
+            fetched_half = lax.dynamic_update_slice(fetched_half, moved[None], ((my_y - step) % SIDE, 0, 0))
+        return fetched_half
+
     first = my_core == 0
 
     def ordered(here, other):
@@ -127,19 +129,31 @@
     half = capacity // 2
     row = jnp.arange(row_count, dtype=I32)
 
-    def picked(first):
+    def asked(first):
         ranks = first + jnp.arange(half, dtype=I32)
         hit = mine[:, None, :] & (rank_all[:, None, :] == ranks[None, :, None])
-        rows = jnp.sum(jnp.where(hit, local_ids[:, None, :] + 1, 0), axis=2).reshape(slots // 2) - 1
+        return jnp.sum(jnp.where(hit, local_ids[:, None, :] + 1, 0), axis=2).reshape(slots // 2) - 1
+
+    def picked(rows):
         return (row[:, None] == rows[None, :]).astype(BF16)
 
-    pick_left, pick_right = picked(0), picked(half)
+    rows_left, rows_right = asked(0), asked(half)
     table_t = emb_table.T
-    fetched = exchange_rows(contract(table_t, pick_left, (1, 0)), contract(table_t, pick_right, (1, 0)))
 
     ids_mine = lax.dynamic_index_in_dim(ids_all, my_group, 0, keepdims=False)
     owner = ids_mine // row_count
-    place_left, place_right = placed(owner, live_mask, half, slots)
+
+    def fetch():
+        left, right = contract(table_t, picked(rows_left), (1, 0)), contract(table_t, picked(rows_right), (1, 0))
+        return exchange_rows(left, right), fetch_half(), scale_row(), *placed(owner, live_mask, half, slots)
+
+    def skip():
+        return jax.tree.map(lambda leaf: jnp.zeros(leaf.shape, leaf.dtype), jax.eval_shape(fetch))
+
+    fetched, fetched_half, hidden_scale, place_left, place_right = lax.cond(next_ids[0] >= 0, fetch, skip)
+    other_half = lax.ppermute(fetched_half, "seq", [(k, k ^ 1) for k in range(groups)])
+    weights_here = fetched_half.reshape(SIDE * part, quarter)
+    weights_other = other_half.reshape(SIDE * part, quarter)
 
     emb = contract(fetched, place_left, (0, 0))[:local_width] + contract(fetched, place_right, (0, 0))[local_width:]
     gain = lax.dynamic_slice_in_dim(gain_embed, place_tp * local_width, local_width)[:, None]
@@ -148,7 +162,6 @@
     got = along_x(to_all(jnp.concatenate([(emb * gain).astype(BF16), split_rows(shared)], axis=0)))
     shared = join_rows(got[:, local_width:], 2)
     features = got[:, :local_width].reshape(quarter, tokens)
-    features, hid_all = lax.optimization_barrier((features, hid_all))
     halves = ordered(contract(weights_here, features, (1, 0)), contract(weights_other, features, (1, 0)))
     halves = [half_rows.astype(BF16).reshape(SIDE, part, tokens) for half_rows in halves]
     got = along_y(jnp.concatenate([*halves, to_all(split_rows(shared))], axis=1))
@@ -177,7 +190,7 @@
     emb_grad = emb_grad.astype(BF16)
     arrived = exchange_rows(contract(emb_grad, place_left, (1, 1)), contract(emb_grad, place_right, (1, 1)))
     table_grad = (
-        contract(arrived, pick_left, (0, 1))[:local_width] + contract(arrived, pick_right, (0, 1))[local_width:]
+        contract(arrived, picked(rows_left), (0, 1))[:local_width] + contract(arrived, picked(rows_right), (0, 1))[local_width:]
     ).astype(BF16)
     return (projected.T, table_grad.T)
 

time: 260 us -> 260 us (level)
  blocking collectives: 104 us -> 31.5 us
  waiting for transfers between devices: 52.5 us -> 102 us
  starting transfers between devices: 52.6 us -> 74.5 us
  local copies, waits for them, and re-layouts: 11.9 us -> 18.5 us
  matrix products: 17.1 us -> 14 us
    all_to_all x1 -> x0, blocking collectives: 83.1 us -> none  [exchange_rows(): moved = lax.all_to_all(both, 'seq', split_axis=0, concat_axis=0, tiled=True)]
    all_to_all x1 -> x2, waiting for transfers between devices: 27.8 us -> 85.5 us  [exchange_rows(): moved = lax.all_to_all(both, 'seq', split_axis=0, concat_axis=0, tiled=True)]
    all_to_all x1 -> x2, starting transfers between devices: 30.5 us -> 55.3 us  [exchange_rows(): moved = lax.all_to_all(both, 'seq', split_axis=0, concat_axis=0, tiled=True)]
    all_to_all x1 -> x2, blocking collectives: 9.15 us -> 19.9 us  [along_y(): lax.all_to_all(value, 'tp', 0, 0, tiled=True, axis_index_groups=groups)]
    all_to_all x1 -> x0, starting transfers between devices: 3.47 us -> none  [along_y(): lax.all_to_all(value, 'tp', 0, 0, tiled=True, axis_index_groups=groups)]
    all_to_all x1, waiting for transfers between devices: 10.1 us -> 6.7 us  [along_x(): lax.all_to_all(value, 'tp', 0, 0, tiled=True, axis_index_groups=groups)]
    dot_general x14, matrix products: 17.1 us -> 14 us  [contract(): lax.dot_general(left, right, ((dims[:1], dims[1:]), ((), ())), preferred_...]
  transfers between devices with their start and end apart: 8 -> 8, of which waited for: 5 -> 6; matrix products, arithmetic and copies ran while one was open for 8% -> 8% of each run, Pallas kernels for 1% -> 0%
where the time goes in v5:
time: 260 us; the launch traced here: 259 us
  waiting for transfers between devices  102 us (39%)
  starting transfers between devices  74.5 us (29%)
  blocking collectives  31.5 us (12%)
  local copies, waits for them, and re-layouts  18.5 us (7%)
  between operations  15.1 us (6%)
  matrix products  14 us (5%)
    all_to_all x2, waiting for transfers between devices, exchange_rows(): moved = lax.all_to_all(both, 'seq', split_axis=0, concat_axis=0, tiled=True)  85.5 us
    all_to_all x2, starting transfers between devices, exchange_rows(): moved = lax.all_to_all(both, 'seq', split_axis=0, concat_axis=0, tiled=True)  55.3 us
    all_to_all x2, blocking collectives, along_y(): lax.all_to_all(value, 'tp', 0, 0, tiled=True, axis_index_groups=groups)  19.9 us
    dot_general x14, matrix products, contract(): lax.dot_general(left, right, ((dims[:1], dims[1:]), ((), ())), preferred_...  14 us
    all_to_all x1, blocking collectives, along_x(): lax.all_to_all(value, 'tp', 0, 0, tiled=True, axis_index_groups=groups)  11.6 us
    ppermute x3, starting transfers between devices, fetch_half(): lax.ppermute(piece((my_y + step) % SIDE), 'tp', [(SIDE * y + x, SIDE * ((...  10.7 us
    ppermute x3, waiting for transfers between devices, fetch_half(): lax.ppermute(piece((my_y + step) % SIDE), 'tp', [(SIDE * y + x, SIDE * ((...  9.26 us
    all_to_all x1, waiting for transfers between devices, along_x(): lax.all_to_all(value, 'tp', 0, 0, tiled=True, axis_index_groups=groups)  6.7 us
  transfers between devices with their start and end apart: 8, of which 6 were waited for; matrix products, arithmetic and copies ran while one was open for 8% of the time, Pallas kernels for 0%

profile of v5, /device:TPU:1, one launch (start us, length us, event | category | flops | bytes accessed | tf_op | source)
XLA Modules:
  0.0 259.4 jit_solution(1780975254000429868)
XLA Ops:
  12.0 92.7 %conditional.1 = (bf16[256,896]{1,0:T(8,128)(2,1)S(1)}, bf16[4,112,1792]{2,1,0:T(8,128)(2,1)}, bf16[256,256]{1,0:T(8,128)(2,1)S(1)}, bf16[256,256]{1,0:T(8,128)(...) conditional(s32[]{:T(128)} %bitcast.13, () %tuple.22, (s32[1024]{0:T(1024)S(1)}, ...), branch_computations={%region_2.3_spmd, %region_3.5_spmd} | conditional | flops 471784224 | bytes 27453296 | solution.py:153
  12.4 1.7 fusion
  15.9 30.4 %all-to-all-start = ((bf16[64,4,896]{2,1,0:T(4,128)(2,1)}), bf16[64,4,896]{2,1,0:T(4,128)(2,1)S(1)}, u32[]{:S(2)}, u32[]{:S(2)}) async-start(bf16[64,4,896]{2,1,0:T(4,128)(2,1)} %reshape.277), calls=%async_computation | async-start | bytes 917504 | tf_op jit(solution)/shard_map/cond/branch_1_fun/all_to_all | solution.py:73
  46.4 1.4 fusion.76
  47.7 3.2 %collective-permute-start = (bf16[112,1792]{1,0:T(8,128)(2,1)S(1)}, bf16[112,1792]{1,0:T(8,128)(2,1)S(1)}, u32[]{:S(2)}, u32[]{:S(2)}) collective-permute-start(bf16[112,1792]{1,0:T(8,128)(2,1)S(1)} %get-tuple-element.217), channel_id=1, source_target_pairs={{0,4},{1,5},{2,6},{3,7},{4,8},{5,9},{6,10},{7,11},{8,12},{9,13},{1... | collective-permute-start | bytes 1204232 | tf_op jit(solution)/shard_map/cond/branch_1_fun/ppermute | solution.py:110
  50.9 4.5 %collective-permute-start.1 = (bf16[112,1792]{1,0:T(8,128)(2,1)S(1)}, bf16[112,1792]{1,0:T(8,128)(2,1)S(1)}, u32[]{:S(2)}, u32[]{:S(2)}) collective-permute-start(bf16[112,1792]{1,0:T(8,128)(2,1)S(1)} %get-tuple-element.216), channel_id=1, source_target_pairs={{0,8},{1,9},{2,10},{3,11},{4,12},{5,13},{6,14},{7,15},{8,0},{9,1},... | collective-permute-start | bytes 1204232 | tf_op jit(solution)/shard_map/cond/branch_1_fun/ppermute | solution.py:110
  55.5 3.0 %collective-permute-start.2 = (bf16[112,1792]{1,0:T(8,128)(2,1)S(1)}, bf16[112,1792]{1,0:T(8,128)(2,1)S(1)}, u32[]{:S(2)}, u32[]{:S(2)}) collective-permute-start(bf16[112,1792]{1,0:T(8,128)(2,1)S(1)} %get-tuple-element.215), channel_id=1, source_target_pairs={{0,12},{1,13},{2,14},{3,15},{4,0},{5,1},{6,2},{7,3},{8,4},{9,5},{1... | collective-permute-start | bytes 1204232 | tf_op jit(solution)/shard_map/cond/branch_1_fun/ppermute | solution.py:110
  60.8 1.3 broadcast.167
  62.1 1.8 bitcast_dynamic-update-slice_fusion.3
  65.2 8.3 %collective-permute-done.1 = bf16[112,1792]{1,0:T(8,128)(2,1)S(1)} collective-permute-done((bf16[112,1792]{1,0:T(8,128)(2,1)S(1)}, bf16[112,1792]{1,0:T(8,128)(2,1)S(1)}, u32[]{:S(2)}, u32[]{:S(2)}) %collective-permute-start.1) | collective-permute-done | bytes 401440 | tf_op jit(solution)/shard_map/cond/branch_1_fun/ppermute | solution.py:110
  75.5 1.4 copy.69
  76.9 27.6 %all-to-all-done = bf16[64,4,896]{2,1,0:T(4,128)(2,1)S(1)} async-done(((bf16[64,4,896]{2,1,0:T(4,128)(2,1)}), bf16[64,4,896]{2,1,0:T(4,128)(2,1)S(1)}, u32[]{:S(2)}, u32[]{:S(2)}) %all-to-all-start) | async-done | bytes 458784 | tf_op jit(solution)/shard_map/cond/branch_1_fun/all_to_all | solution.py:73
  107.4 4.0 %all-to-all-start.1 = ((bf16[4,464,256]{2,1,0:T(8,128)(2,1)}), bf16[4,464,256]{2,1,0:T(8,128)(2,1)S(1)}, u32[]{:S(2)}, u32[]{:S(2)}) async-start(bf16[4,464,256]{2,1,0:T(8,128)(2,1)} %broadcast_in_dim.85), calls=%async_computation.1 | async-start | bytes 1900544 | tf_op jit(solution)/shard_map/all_to_all | solution.py:57
  111.4 4.5 %collective-permute-start.3 = (bf16[4,112,1792]{2,1,0:T(8,128)(2,1)}, bf16[4,112,1792]{2,1,0:T(8,128)(2,1)S(1)}, u32[]{:S(2)}, u32[]{:S(2)}) collective-permute-start(bf16[4,112,1792]{2,1,0:T(8,128)(2,1)} %get-tuple-element.123), channel_id=1, source_target_pairs={{0,16},{16,0},{32,48},{48,32},{64,80},{80,64},{96,112},{112,96},{1... | collective-permute-start | bytes 4816904 | tf_op jit(solution)/shard_map/ppermute | solution.py:154
  115.9 6.7 %all-to-all-done.1 = bf16[4,464,256]{2,1,0:T(8,128)(2,1)S(1)} async-done(((bf16[4,464,256]{2,1,0:T(8,128)(2,1)}), bf16[4,464,256]{2,1,0:T(8,128)(2,1)S(1)}, u32[]{:S(2)}, u32[]{:S(2)}) %all-to-all-start.1) | async-done | bytes 950304 | tf_op jit(solution)/shard_map/all_to_all | solution.py:57
  122.7 1.2 copy-done.1
  125.2 10.7 %all_to_all.29 = bf16[4,240,256]{2,1,0:T(8,128)(2,1)S(1)} all-to-all(bf16[4,240,256]{2,1,0:T(8,128)(2,1)S(1)} %pad_maximum_fusion.1), channel_id=1, replica_groups={{0,4,8,12},{1,5,9,13},{2,6,10,14},{3,7,11,15},{16,20,24,28},{17,21,25,2..., dimensions={0} | all-to-all | bytes 983040 | tf_op jit(solution)/shard_map/all_to_all | solution.py:62
  136.2 4.4 %fusion.14 = f32[224,256]{1,0:T(8,128)S(1)} fusion(bf16[224,14336]{1,0:T(8,128)(2,1)} %bitcast.75, bf16[256,7168]{1,0:T(8,128)(2,1)} %all-gather.2.cloned.1.call-done, f32[7168]{0:T(1024)S(1)} %copy-done.7), kind=kOutput, calls=%fused_computation.42 | convolution fusion | flops 827588608 | bytes 7139328 | tf_op jit(solution)/shard_map/dot_general | solution.py:18
  141.4 9.1 %all_to_all.30 = bf16[4,240,256]{2,1,0:T(8,128)(2,1)S(1)} all-to-all(bf16[4,240,256]{2,1,0:T(8,128)(2,1)S(1)} %broadcast_in_dim.87), channel_id=1, replica_groups={{0,4,8,12},{1,5,9,13},{2,6,10,14},{3,7,11,15},{16,20,24,28},{17,21,25,2..., dimensions={0} | all-to-all | bytes 983040 | tf_op jit(solution)/shard_map/all_to_all | solution.py:62
  150.6 2.1 convolution_bitcast_fusion.1
  153.6 11.6 %all_to_all.31 = bf16[4,464,256]{2,1,0:T(8,128)(2,1)S(1)} all-to-all(bf16[4,464,256]{2,1,0:T(8,128)(2,1)S(1)} %pad_maximum_fusion), channel_id=1, replica_groups={{0,1,2,3},{4,5,6,7},{8,9,10,11},{12,13,14,15},{16,17,18,19},{20,21,22,2..., dimensions={0} | all-to-all | bytes 1900544 | tf_op jit(solution)/shard_map/all_to_all | solution.py:57
  167.2 24.9 %all-to-all-start.5 = ((bf16[64,4,896]{2,1,0:T(4,128)(2,1)}), bf16[64,4,896]{2,1,0:T(4,128)(2,1)S(1)}, u32[]{:S(2)}, u32[]{:S(2)}) async-start(bf16[64,4,896]{2,1,0:T(4,128)(2,1)} %reshape.294), calls=%async_computation.5 | async-start | bytes 917504 | tf_op jit(solution)/shard_map/all_to_all | solution.py:73
  192.5 57.9 %all-to-all-done.5 = bf16[64,4,896]{2,1,0:T(4,128)(2,1)S(1)} async-done(((bf16[64,4,896]{2,1,0:T(4,128)(2,1)}), bf16[64,4,896]{2,1,0:T(4,128)(2,1)S(1)}, u32[]{:S(2)}, u32[]{:S(2)}) %all-to-all-start.5) | async-done | bytes 458784 | tf_op jit(solution)/shard_map/all_to_all | solution.py:73
  251.0 1.6 fusion.13
  (105 shorter events, 20.6 us)
Async XLA Ops:
  7.2 129.0 %all-gather.2.cloned.1.call-start = ((), (), s32[]{:S(2)}) async-start(), calls=%async_computation.6 | async-start | bytes 3899392 | tf_op jit(solution)/shard_map/all_gather | solution.py:90
  12.0 2.1 copy-start.6
  15.9 88.7 %all-to-all-start = ((bf16[64,4,896]{2,1,0:T(4,128)(2,1)}), bf16[64,4,896]{2,1,0:T(4,128)(2,1)S(1)}, u32[]{:S(2)}, u32[]{:S(2)}) async-start(bf16[64,4,896]{2,1,0:T(4,128)(2,1)} %reshape.277), calls=%async_computation | async-start | bytes 917504 | tf_op jit(solution)/shard_map/cond/branch_1_fun/all_to_all | solution.py:73
  46.3 13.1 %copy-start.2 = (bf16[16,7168]{1,0:T(8,128)(2,1)S(1)}, bf16[16,7168]{1,0:T(8,128)(2,1)}, u32[]{:S(2)}) copy-start(bf16[16,7168]{1,0:T(8,128)(2,1)} %get-tuple-element.109) | copy-start | bytes 688132 | tf_op jit(solution)/shard_map/cond
  46.3 13.4 %copy-start.5 = (s32[256]{0:T(256)S(1)}, s32[256]{0:T(256)}, u32[]{:S(2)}) copy-start(s32[256]{0:T(256)} %get-tuple-element.131) | copy-start | bytes 3076 | tf_op jit(solution)/shard_map/cond
  47.7 16.7 %collective-permute-start = (bf16[112,1792]{1,0:T(8,128)(2,1)S(1)}, bf16[112,1792]{1,0:T(8,128)(2,1)S(1)}, u32[]{:S(2)}, u32[]{:S(2)}) collective-permute-start(bf16[112,1792]{1,0:T(8,128)(2,1)S(1)} %get-tuple-element.217), channel_id=1, source_target_pairs={{0,4},{1,5},{2,6},{3,7},{4,8},{5,9},{6,10},{7,11},{8,12},{9,13},{1... | collective-permute-start | bytes 1204232 | tf_op jit(solution)/shard_map/cond/branch_1_fun/ppermute | solution.py:110
  50.9 22.6 %collective-permute-start.1 = (bf16[112,1792]{1,0:T(8,128)(2,1)S(1)}, bf16[112,1792]{1,0:T(8,128)(2,1)S(1)}, u32[]{:S(2)}, u32[]{:S(2)}) collective-permute-start(bf16[112,1792]{1,0:T(8,128)(2,1)S(1)} %get-tuple-element.216), channel_id=1, source_target_pairs={{0,8},{1,9},{2,10},{3,11},{4,12},{5,13},{6,14},{7,15},{8,0},{9,1},... | collective-permute-start | bytes 1204232 | tf_op jit(solution)/shard_map/cond/branch_1_fun/ppermute | solution.py:110
  55.5 19.3 %collective-permute-start.2 = (bf16[112,1792]{1,0:T(8,128)(2,1)S(1)}, bf16[112,1792]{1,0:T(8,128)(2,1)S(1)}, u32[]{:S(2)}, u32[]{:S(2)}) collective-permute-start(bf16[112,1792]{1,0:T(8,128)(2,1)S(1)} %get-tuple-element.215), channel_id=1, source_target_pairs={{0,12},{1,13},{2,14},{3,15},{4,0},{5,1},{6,2},{7,3},{8,4},{9,5},{1... | collective-permute-start | bytes 1204232 | tf_op jit(solution)/shard_map/cond/branch_1_fun/ppermute | solution.py:110
  58.6 1.1 copy-start.4
  104.7 1.2 copy-start
  107.4 15.2 %all-to-all-start.1 = ((bf16[4,464,256]{2,1,0:T(8,128)(2,1)}), bf16[4,464,256]{2,1,0:T(8,128)(2,1)S(1)}, u32[]{:S(2)}, u32[]{:S(2)}) async-start(bf16[4,464,256]{2,1,0:T(8,128)(2,1)} %broadcast_in_dim.85), calls=%async_computation.1 | async-start | bytes 1900544 | tf_op jit(solution)/shard_map/all_to_all | solution.py:57
  111.4 13.2 %collective-permute-start.3 = (bf16[4,112,1792]{2,1,0:T(8,128)(2,1)}, bf16[4,112,1792]{2,1,0:T(8,128)(2,1)S(1)}, u32[]{:S(2)}, u32[]{:S(2)}) collective-permute-start(bf16[4,112,1792]{2,1,0:T(8,128)(2,1)} %get-tuple-element.123), channel_id=1, source_target_pairs={{0,16},{16,0},{32,48},{48,32},{64,80},{80,64},{96,112},{112,96},{1... | collective-permute-start | bytes 4816904 | tf_op jit(solution)/shard_map/ppermute | solution.py:154
  122.6 1.4 copy-start.1
  125.2 11.0 %copy-start.7 = (f32[7168]{0:T(1024)S(1)}, f32[7168]{0:T(1024)}, u32[]{:S(2)}) copy-start(f32[7168]{0:T(1024)} %param.14) | copy-start | bytes 86020
  136.1 4.4 %copy-start.3 = (bf16[256,224]{0,1:T(8,128)(2,1)S(1)}, bf16[256,224]{0,1:T(8,128)(2,1)}, u32[]{:S(2)}) copy-start(bf16[256,224]{0,1:T(8,128)(2,1)} %param.17) | copy-start | bytes 344068
  167.2 83.2 %all-to-all-start.5 = ((bf16[64,4,896]{2,1,0:T(4,128)(2,1)}), bf16[64,4,896]{2,1,0:T(4,128)(2,1)S(1)}, u32[]{:S(2)}, u32[]{:S(2)}) async-start(bf16[64,4,896]{2,1,0:T(4,128)(2,1)} %reshape.294), calls=%async_computation.5 | async-start | bytes 917504 | tf_op jit(solution)/shard_map/all_to_all | solution.py:73
Sparse Core Ops, SparseCore 0:
  12.2 102.9 all-gather.1

commit v6 on v5

--- a/solution.py
+++ b/solution.py
@@ -113,7 +113,7 @@
                 [(SIDE * y + x, SIDE * ((y + step) % SIDE) + x) for y in range(SIDE) for x in range(SIDE)],
             )
             fetched_half = lax.dynamic_update_slice(fetched_half, moved[None], ((my_y - step) % SIDE, 0, 0))
-        return fetched_half
+        return fetched_half, lax.ppermute(fetched_half, "seq", [(k, k ^ 1) for k in range(groups)])
 
     first = my_core == 0
 
@@ -145,13 +145,12 @@
 
     def fetch():
         left, right = contract(table_t, picked(rows_left), (1, 0)), contract(table_t, picked(rows_right), (1, 0))
-        return exchange_rows(left, right), fetch_half(), scale_row(), *placed(owner, live_mask, half, slots)
+        return exchange_rows(left, right), *fetch_half(), scale_row(), *placed(owner, live_mask, half, slots)
 
     def skip():
         return jax.tree.map(lambda leaf: jnp.zeros(leaf.shape, leaf.dtype), jax.eval_shape(fetch))
 
-    fetched, fetched_half, hidden_scale, place_left, place_right = lax.cond(next_ids[0] >= 0, fetch, skip)
-    other_half = lax.ppermute(fetched_half, "seq", [(k, k ^ 1) for k in range(groups)])
+    fetched, fetched_half, other_half, hidden_scale, place_left, place_right = lax.cond(next_ids[0] >= 0, fetch, skip)
     weights_here = fetched_half.reshape(SIDE * part, quarter)
     weights_other = other_half.reshape(SIDE * part, quarter)
 
@@ -159,7 +158,9 @@
     gain = lax.dynamic_slice_in_dim(gain_embed, place_tp * local_width, local_width)[:, None]
     squares = jnp.sum(emb * emb, axis=0, keepdims=True)
     shared = jnp.concatenate([squares, hidden_scale[None, :]], axis=0)
-    got = along_x(to_all(jnp.concatenate([(emb * gain).astype(BF16), split_rows(shared)], axis=0)))
+    message = jnp.concatenate([(emb * gain).astype(BF16), split_rows(shared)], axis=0)
+    rows_of_devices = [[SIDE * y + x for x in range(SIDE)] for y in range(SIDE)]
+    got = lax.all_gather(message, "tp", axis=0, tiled=False, axis_index_groups=rows_of_devices)
     shared = join_rows(got[:, local_width:], 2)
     features = got[:, :local_width].reshape(quarter, tokens)
     halves = ordered(contract(weights_here, features, (1, 0)), contract(weights_other, features, (1, 0)))

time: 260 us -> 253 us (0.973)
  blocking collectives: 31.5 us -> 45.9 us
  starting transfers between devices: 74.5 us -> 63 us
  waiting for transfers between devices: 102 us -> 92.1 us
  matrix products: 14 us -> 16.8 us
  local copies, waits for them, and re-layouts: 18.5 us -> 15.8 us
    all_gather x0 -> x1, blocking collectives: none -> 14.1 us  [local(): lax.all_gather(message, 'tp', axis=0, tiled=False, axis_index_groups=rows...]
    all_to_all x2, waiting for transfers between devices: 85.5 us -> 77.7 us  [exchange_rows(): moved = lax.all_to_all(both, 'seq', split_axis=0, concat_axis=0, tiled=True)]
    all_to_all x1 -> x0, waiting for transfers between devices: 6.7 us -> none  [along_x(): lax.all_to_all(value, 'tp', 0, 0, tiled=True, axis_index_groups=groups)]
    all_to_all x2, starting transfers between devices: 55.3 us -> 49.3 us  [exchange_rows(): moved = lax.all_to_all(both, 'seq', split_axis=0, concat_axis=0, tiled=True)]
    ppermute x3, waiting for transfers between devices: 9.26 us -> 13.8 us  [fetch_half(): lax.ppermute(piece((my_y + step) % SIDE), 'tp', [(SIDE * y + x, SIDE * ((...]
    all_to_all x1 -> x0, starting transfers between devices: 4.01 us -> none  [along_x(): lax.all_to_all(value, 'tp', 0, 0, tiled=True, axis_index_groups=groups)]
    dot_general x14, matrix products: 14 us -> 16.8 us  [contract(): lax.dot_general(left, right, ((dims[:1], dims[1:]), ((), ())), preferred_...]
    cond x9 -> x14, local copies, waits for them, and re-layouts: 1.44 us -> 4.07 us
  transfers between devices with their start and end apart: 8 -> 7, of which waited for: 6 -> 5; matrix products, arithmetic and copies ran while one was open for 8% -> 9% of each run, Pallas kernels for 0% -> 0%
where the time goes in v6:
time: 253 us; the launch traced here: 252 us
  waiting for transfers between devices  92.1 us (36%)
  starting transfers between devices  63 us (25%)
  blocking collectives  45.9 us (18%)
  matrix products  16.8 us (7%)
  local copies, waits for them, and re-layouts  15.8 us (6%)
  between operations  15.1 us (6%)
    all_to_all x2, waiting for transfers between devices, exchange_rows(): moved = lax.all_to_all(both, 'seq', split_axis=0, concat_axis=0, tiled=True)  77.7 us
    all_to_all x2, starting transfers between devices, exchange_rows(): moved = lax.all_to_all(both, 'seq', split_axis=0, concat_axis=0, tiled=True)  49.3 us
    all_to_all x2, blocking collectives, along_y(): lax.all_to_all(value, 'tp', 0, 0, tiled=True, axis_index_groups=groups)  20.2 us
    dot_general x14, matrix products, contract(): lax.dot_general(left, right, ((dims[:1], dims[1:]), ((), ())), preferred_...  16.8 us
    all_gather x1, blocking collectives, local(): lax.all_gather(message, 'tp', axis=0, tiled=False, axis_index_groups=rows...  14.1 us
    ppermute x3, waiting for transfers between devices, fetch_half(): lax.ppermute(piece((my_y + step) % SIDE), 'tp', [(SIDE * y + x, SIDE * ((...  13.8 us
    all_to_all x1, blocking collectives, along_x(): lax.all_to_all(value, 'tp', 0, 0, tiled=True, axis_index_groups=groups)  11.6 us
    ppermute x3, starting transfers between devices, fetch_half(): lax.ppermute(piece((my_y + step) % SIDE), 'tp', [(SIDE * y + x, SIDE * ((...  10.7 us
  transfers between devices with their start and end apart: 7, of which 5 were waited for; matrix products, arithmetic and copies ran while one was open for 9% of the time, Pallas kernels for 0%

profile of v6, /device:TPU:1, one launch (start us, length us, event | category | flops | bytes accessed | tf_op | source)
XLA Modules:
  0.0 252.3 jit_solution(8620490023939245035)
XLA Ops:
  8.8 1.2 slice.92
  12.0 92.7 %conditional.1 = (bf16[256,896]{1,0:T(8,128)(2,1)S(1)}, bf16[4,112,1792]{2,1,0:T(8,128)(2,1)S(1)}, bf16[4,112,1792]{2,1,0:T(8,128)(2,1)}, bf16[256,256]{1,0:T(8,...) conditional(s32[]{:T(128)} %bitcast.14, () %tuple.24, ...), branch_computations={%region_2.3_spmd, %region_3.5_spmd} | conditional | flops 471784224 | bytes 49932256 | solution.py:153
  12.4 1.7 fusion
  15.9 30.4 %all-to-all-start = ((bf16[64,4,896]{2,1,0:T(4,128)(2,1)}), bf16[64,4,896]{2,1,0:T(4,128)(2,1)S(1)}, u32[]{:S(2)}, u32[]{:S(2)}) async-start(bf16[64,4,896]{2,1,0:T(4,128)(2,1)} %reshape.279), calls=%async_computation | async-start | bytes 917504 | tf_op jit(solution)/shard_map/cond/branch_1_fun/all_to_all | solution.py:73
  46.3 2.3 fusion.76
  48.6 3.2 %collective-permute-start = (bf16[112,1792]{1,0:T(8,128)(2,1)}, bf16[112,1792]{1,0:T(8,128)(2,1)}, u32[]{:S(2)}, u32[]{:S(2)}) collective-permute-start(bf16[112,1792]{1,0:T(8,128)(2,1)} %get-tuple-element.174), channel_id=1, source_target_pairs={{0,4},{1,5},{2,6},{3,7},{4,8},{5,9},{6,10},{7,11},{8,12},{9,13},{1... | collective-permute-start | bytes 1204232 | tf_op jit(solution)/shard_map/cond/branch_1_fun/ppermute | solution.py:110
  51.8 4.5 %collective-permute-start.1 = (bf16[112,1792]{1,0:T(8,128)(2,1)}, bf16[112,1792]{1,0:T(8,128)(2,1)S(1)}, u32[]{:S(2)}, u32[]{:S(2)}) collective-permute-start(bf16[112,1792]{1,0:T(8,128)(2,1)} %get-tuple-element.173), channel_id=1, source_target_pairs={{0,8},{1,9},{2,10},{3,11},{4,12},{5,13},{6,14},{7,15},{8,0},{9,1},... | collective-permute-start | bytes 1204232 | tf_op jit(solution)/shard_map/cond/branch_1_fun/ppermute | solution.py:110
  56.4 3.0 %collective-permute-start.2 = (bf16[112,1792]{1,0:T(8,128)(2,1)}, bf16[112,1792]{1,0:T(8,128)(2,1)S(1)}, u32[]{:S(2)}, u32[]{:S(2)}) collective-permute-start(bf16[112,1792]{1,0:T(8,128)(2,1)} %get-tuple-element.172), channel_id=1, source_target_pairs={{0,12},{1,13},{2,14},{3,15},{4,0},{5,1},{6,2},{7,3},{8,4},{9,5},{1... | collective-permute-start | bytes 1204232 | tf_op jit(solution)/shard_map/cond/branch_1_fun/ppermute | solution.py:110
  60.7 4.4 %collective-permute-done = bf16[112,1792]{1,0:T(8,128)(2,1)} collective-permute-done((bf16[112,1792]{1,0:T(8,128)(2,1)}, bf16[112,1792]{1,0:T(8,128)(2,1)}, u32[]{:S(2)}, u32[]{:S(2)}) %collective-permute-start) | collective-permute-done | bytes 401440 | tf_op jit(solution)/shard_map/cond/branch_1_fun/ppermute | solution.py:110
  66.1 8.6 %collective-permute-done.1 = bf16[112,1792]{1,0:T(8,128)(2,1)S(1)} collective-permute-done((bf16[112,1792]{1,0:T(8,128)(2,1)}, bf16[112,1792]{1,0:T(8,128)(2,1)S(1)}, u32[]{:S(2)}, u32[]{:S(2)}) %collective-permute-start.1) | collective-permute-done | bytes 401440 | tf_op jit(solution)/shard_map/cond/branch_1_fun/ppermute | solution.py:110
  75.5 2.9 %collective-permute-start.3 = (bf16[4,112,1792]{2,1,0:T(8,128)(2,1)S(1)}, bf16[4,112,1792]{2,1,0:T(8,128)(2,1)}, u32[]{:S(2)}, u32[]{:S(2)}) collective-permute-start(bf16[4,112,1792]{2,1,0:T(8,128)(2,1)S(1)} %bitcast_dynamic-update-slice_fusion), channel_id=1, source_target_pairs={{0,16},{16,0},{32,48},{48,32},{64,80},{80,64},{96,112},{112,96},{1... | collective-permute-start | bytes 4816904 | tf_op jit(solution)/shard_map/cond/branch_1_fun/ppermute | solution.py:116
  81.9 2.9 %copy.39 = bf16[448,1792]{1,0:T(8,128)(2,1)} copy(bf16[448,1792]{1,0:T(8,128)(2,1)} %bitcast.11) | data formatting | bytes 3211264 | tf_op jit(solution)/shard_map/cond
  84.8 19.8 %all-to-all-done = bf16[64,4,896]{2,1,0:T(4,128)(2,1)S(1)} async-done(((bf16[64,4,896]{2,1,0:T(4,128)(2,1)}), bf16[64,4,896]{2,1,0:T(4,128)(2,1)S(1)}, u32[]{:S(2)}, u32[]{:S(2)}) %all-to-all-start) | async-done | bytes 458784 | tf_op jit(solution)/shard_map/cond/branch_1_fun/all_to_all | solution.py:73
  105.5 14.1 %all-gather = bf16[1856,256]{1,0:T(8,128)(2,1)S(1)} all-gather(bf16[464,256]{1,0:T(8,128)(2,1)S(1)} %pad_maximum_fusion.2), channel_id=2, replica_groups={{0,1,2,3},{4,5,6,7},{8,9,10,11},{12,13,14,15},{16,17,18,19},{20,21,22,2..., dimensions={0}, use_global_device_ids=true | all-gather | bytes 1187840 | tf_op jit(solution)/shard_map/all_gather | solution.py:163
  119.7 2.0 fusion.78
  121.7 2.0 select_convert_fusion.1
  123.8 11.1 %all_to_all.24 = bf16[4,240,256]{2,1,0:T(8,128)(2,1)S(1)} all-to-all(bf16[4,240,256]{2,1,0:T(8,128)(2,1)S(1)} %pad_maximum_fusion.1), channel_id=1, replica_groups={{0,4,8,12},{1,5,9,13},{2,6,10,14},{3,7,11,15},{16,20,24,28},{17,21,25,2..., dimensions={0} | all-to-all | bytes 983040 | tf_op jit(solution)/shard_map/all_to_all | solution.py:62
  135.0 4.4 %fusion.14 = f32[224,256]{1,0:T(8,128)S(1)} fusion(bf16[224,14336]{1,0:T(8,128)(2,1)} %bitcast.78, bf16[256,7168]{1,0:T(8,128)(2,1)} %all-gather.3.cloned.1.call-done, f32[7168]{0:T(1024)S(1)} %copy-done.7), kind=kOutput, calls=%fused_computation.42 | convolution fusion | flops 827588608 | bytes 7139328 | tf_op jit(solution)/shard_map/dot_general | solution.py:18
  140.2 9.1 %all_to_all.25 = bf16[4,240,256]{2,1,0:T(8,128)(2,1)S(1)} all-to-all(bf16[4,240,256]{2,1,0:T(8,128)(2,1)S(1)} %broadcast_in_dim.83), channel_id=1, replica_groups={{0,4,8,12},{1,5,9,13},{2,6,10,14},{3,7,11,15},{16,20,24,28},{17,21,25,2..., dimensions={0} | all-to-all | bytes 983040 | tf_op jit(solution)/shard_map/all_to_all | solution.py:62
  149.5 2.1 convolution_bitcast_fusion
  152.4 11.6 %all_to_all.26 = bf16[4,464,256]{2,1,0:T(8,128)(2,1)S(1)} all-to-all(bf16[4,464,256]{2,1,0:T(8,128)(2,1)S(1)} %pad_maximum_fusion), channel_id=1, replica_groups={{0,1,2,3},{4,5,6,7},{8,9,10,11},{12,13,14,15},{16,17,18,19},{20,21,22,2..., dimensions={0} | all-to-all | bytes 1900544 | tf_op jit(solution)/shard_map/all_to_all | solution.py:57
  166.0 18.9 %all-to-all-start.4 = ((bf16[64,4,896]{2,1,0:T(4,128)(2,1)}), bf16[64,4,896]{2,1,0:T(4,128)(2,1)S(1)}, u32[]{:S(2)}, u32[]{:S(2)}) async-start(bf16[64,4,896]{2,1,0:T(4,128)(2,1)} %reshape.295), calls=%async_computation.4 | async-start | bytes 917504 | tf_op jit(solution)/shard_map/all_to_all | solution.py:73
  185.4 57.9 %all-to-all-done.4 = bf16[64,4,896]{2,1,0:T(4,128)(2,1)S(1)} async-done(((bf16[64,4,896]{2,1,0:T(4,128)(2,1)}), bf16[64,4,896]{2,1,0:T(4,128)(2,1)S(1)}, u32[]{:S(2)}, u32[]{:S(2)}) %all-to-all-start.4) | async-done | bytes 458784 | tf_op jit(solution)/shard_map/all_to_all | solution.py:73
  243.9 1.6 fusion.13
  (102 shorter events, 17.2 us)
Async XLA Ops:
  7.2 127.9 %all-gather.3.cloned.1.call-start = ((), (), s32[]{:S(2)}) async-start(), calls=%async_computation.5 | async-start | bytes 3899392 | tf_op jit(solution)/shard_map/all_gather | solution.py:90
  12.0 2.1 copy-start.6
  15.9 88.7 %all-to-all-start = ((bf16[64,4,896]{2,1,0:T(4,128)(2,1)}), bf16[64,4,896]{2,1,0:T(4,128)(2,1)S(1)}, u32[]{:S(2)}, u32[]{:S(2)}) async-start(bf16[64,4,896]{2,1,0:T(4,128)(2,1)} %reshape.279), calls=%async_computation | async-start | bytes 917504 | tf_op jit(solution)/shard_map/cond/branch_1_fun/all_to_all | solution.py:73
  48.6 16.4 %collective-permute-start = (bf16[112,1792]{1,0:T(8,128)(2,1)}, bf16[112,1792]{1,0:T(8,128)(2,1)}, u32[]{:S(2)}, u32[]{:S(2)}) collective-permute-start(bf16[112,1792]{1,0:T(8,128)(2,1)} %get-tuple-element.174), channel_id=1, source_target_pairs={{0,4},{1,5},{2,6},{3,7},{4,8},{5,9},{6,10},{7,11},{8,12},{9,13},{1... | collective-permute-start | bytes 1204232 | tf_op jit(solution)/shard_map/cond/branch_1_fun/ppermute | solution.py:110
  51.8 22.8 %collective-permute-start.1 = (bf16[112,1792]{1,0:T(8,128)(2,1)}, bf16[112,1792]{1,0:T(8,128)(2,1)S(1)}, u32[]{:S(2)}, u32[]{:S(2)}) collective-permute-start(bf16[112,1792]{1,0:T(8,128)(2,1)} %get-tuple-element.173), channel_id=1, source_target_pairs={{0,8},{1,9},{2,10},{3,11},{4,12},{5,13},{6,14},{7,15},{8,0},{9,1},... | collective-permute-start | bytes 1204232 | tf_op jit(solution)/shard_map/cond/branch_1_fun/ppermute | solution.py:110
  56.4 19.1 %collective-permute-start.2 = (bf16[112,1792]{1,0:T(8,128)(2,1)}, bf16[112,1792]{1,0:T(8,128)(2,1)S(1)}, u32[]{:S(2)}, u32[]{:S(2)}) collective-permute-start(bf16[112,1792]{1,0:T(8,128)(2,1)} %get-tuple-element.172), channel_id=1, source_target_pairs={{0,12},{1,13},{2,14},{3,15},{4,0},{5,1},{6,2},{7,3},{8,4},{9,5},{1... | collective-permute-start | bytes 1204232 | tf_op jit(solution)/shard_map/cond/branch_1_fun/ppermute | solution.py:110
  59.6 19.7 %copy-start.2 = (bf16[16,7168]{1,0:T(8,128)(2,1)S(1)}, bf16[16,7168]{1,0:T(8,128)(2,1)}, u32[]{:S(2)}) copy-start(bf16[16,7168]{1,0:T(8,128)(2,1)} %get-tuple-element.110) | copy-start | bytes 688132 | tf_op jit(solution)/shard_map/cond
  60.7 18.9 %copy-start.5 = (s32[256]{0:T(256)S(1)}, s32[256]{0:T(256)}, u32[]{:S(2)}) copy-start(s32[256]{0:T(256)} %get-tuple-element.136) | copy-start | bytes 3076 | tf_op jit(solution)/shard_map/cond
  75.5 6.4 %copy-start = (bf16[4,112,1792]{2,1,0:T(8,128)(2,1)}, bf16[4,112,1792]{2,1,0:T(8,128)(2,1)S(1)}, u32[]{:S(2)}) copy-start(bf16[4,112,1792]{2,1,0:T(8,128)(2,1)S(1)} %bitcast_dynamic-update-slice_fusion) | copy-start | bytes 4816900 | tf_op jit(solution)/shard_map/cond
  75.5 6.4 %collective-permute-start.3 = (bf16[4,112,1792]{2,1,0:T(8,128)(2,1)S(1)}, bf16[4,112,1792]{2,1,0:T(8,128)(2,1)}, u32[]{:S(2)}, u32[]{:S(2)}) collective-permute-start(bf16[4,112,1792]{2,1,0:T(8,128)(2,1)S(1)} %bitcast_dynamic-update-slice_fusion), channel_id=1, source_target_pairs={{0,16},{16,0},{32,48},{48,32},{64,80},{80,64},{96,112},{112,96},{1... | collective-permute-start | bytes 4816904 | tf_op jit(solution)/shard_map/cond/branch_1_fun/ppermute | solution.py:116
  78.5 1.1 copy-start.4
  81.9 22.8 %copy-start.1 = (bf16[4,112,1792]{2,1,0:T(8,128)(2,1)S(1)}, bf16[4,112,1792]{2,1,0:T(8,128)(2,1)}, u32[]{:S(2)}) copy-start(bf16[4,112,1792]{2,1,0:T(8,128)(2,1)} %copy-done) | copy-start | bytes 4816900 | tf_op jit(solution)/shard_map/cond
  123.7 11.3 %copy-start.7 = (f32[7168]{0:T(1024)S(1)}, f32[7168]{0:T(1024)}, u32[]{:S(2)}) copy-start(f32[7168]{0:T(1024)} %param.14) | copy-start | bytes 86020
  135.0 4.4 %copy-start.3 = (bf16[256,224]{0,1:T(8,128)(2,1)S(1)}, bf16[256,224]{0,1:T(8,128)(2,1)}, u32[]{:S(2)}) copy-start(bf16[256,224]{0,1:T(8,128)(2,1)} %param.17) | copy-start | bytes 344068
  166.0 77.2 %all-to-all-start.4 = ((bf16[64,4,896]{2,1,0:T(4,128)(2,1)}), bf16[64,4,896]{2,1,0:T(4,128)(2,1)S(1)}, u32[]{:S(2)}, u32[]{:S(2)}) async-start(bf16[64,4,896]{2,1,0:T(4,128)(2,1)} %reshape.295), calls=%async_computation.4 | async-start | bytes 917504 | tf_op jit(solution)/shard_map/all_to_all | solution.py:73
Sparse Core Ops, SparseCore 0:
  12.2 102.3 all-gather.2

commit v7 on v6

--- a/solution.py
+++ b/solution.py
@@ -66,10 +66,13 @@
     return jnp.broadcast_to(value, (SIDE,) + value.shape)
 
 
-def exchange_rows(left, right):
+def side_by_side(left, right):
     groups = lax.axis_size("seq")
     both = jnp.concatenate([left, right], axis=0).astype(BF16).T
-    both = both.reshape(groups, both.shape[0] // groups, both.shape[1])
+    return both.reshape(groups, both.shape[0] // groups, both.shape[1])
+
+
+def exchange_rows(both):
     moved = lax.all_to_all(both, "seq", split_axis=0, concat_axis=0, tiled=True)
     return moved.reshape(-1, moved.shape[2])
 
@@ -142,20 +145,20 @@
 
     ids_mine = lax.dynamic_index_in_dim(ids_all, my_group, 0, keepdims=False)
     owner = ids_mine // row_count
+    wanted = side_by_side(contract(table_t, picked(rows_left), (1, 0)), contract(table_t, picked(rows_right), (1, 0)))
 
     def fetch():
-        left, right = contract(table_t, picked(rows_left), (1, 0)), contract(table_t, picked(rows_right), (1, 0))
-        return exchange_rows(left, right), *fetch_half(), scale_row(), *placed(owner, live_mask, half, slots)
+        gain = lax.dynamic_slice_in_dim(gain_embed, place_tp * local_width, local_width)[:, None]
+        return exchange_rows(wanted), *fetch_half(), gain, scale_row(), *placed(owner, live_mask, half, slots)
 
     def skip():
         return jax.tree.map(lambda leaf: jnp.zeros(leaf.shape, leaf.dtype), jax.eval_shape(fetch))
 
-    fetched, fetched_half, other_half, hidden_scale, place_left, place_right = lax.cond(next_ids[0] >= 0, fetch, skip)
+    fetched, fetched_half, other_half, gain, hidden_scale, place_left, place_right = lax.cond(my_group < groups, fetch, skip)
     weights_here = fetched_half.reshape(SIDE * part, quarter)
     weights_other = other_half.reshape(SIDE * part, quarter)
 
     emb = contract(fetched, place_left, (0, 0))[:local_width] + contract(fetched, place_right, (0, 0))[local_width:]
-    gain = lax.dynamic_slice_in_dim(gain_embed, place_tp * local_width, local_width)[:, None]
     squares = jnp.sum(emb * emb, axis=0, keepdims=True)
     shared = jnp.concatenate([squares, hidden_scale[None, :]], axis=0)
     message = jnp.concatenate([(emb * gain).astype(BF16), split_rows(shared)], axis=0)
@@ -189,7 +192,8 @@
 
     emb_grad = scale * gain * feature_grad - scale * scale * scale * curvature / width * emb
     emb_grad = emb_grad.astype(BF16)
-    arrived = exchange_rows(contract(emb_grad, place_left, (1, 1)), contract(emb_grad, place_right, (1, 1)))
+    returned = side_by_side(contract(emb_grad, place_left, (1, 1)), contract(emb_grad, place_right, (1, 1)))
+    arrived = exchange_rows(returned)
     table_grad = (
         contract(arrived, picked(rows_left), (0, 1))[:local_width] + contract(arrived, picked(rows_right), (0, 1))[local_width:]
     ).astype(BF16)

time: 253 us -> 251 us (level)
  blocking collectives: 45.9 us -> 123 us
  waiting for transfers between devices: 92.1 us -> 30.5 us
  starting transfers between devices: 63 us -> 44.4 us
    all_to_all x0 -> x1, blocking collectives: none -> 72.5 us  [exchange_rows(): moved = lax.all_to_all(both, 'seq', split_axis=0, concat_axis=0, tiled=True)]
    all_to_all x2 -> x1, waiting for transfers between devices: 77.7 us -> 15.5 us  [exchange_rows(): moved = lax.all_to_all(both, 'seq', split_axis=0, concat_axis=0, tiled=True)]
    all_to_all x2 -> x1, starting transfers between devices: 49.3 us -> 30.4 us  [exchange_rows(): moved = lax.all_to_all(both, 'seq', split_axis=0, concat_axis=0, tiled=True)]
    all_gather x1, blocking collectives: 14.1 us -> 19 us  [local(): lax.all_gather(message, 'tp', axis=0, tiled=False, axis_index_groups=rows...]
  transfers between devices with their start and end apart: 7 -> 6, of which waited for: 5 -> 3; matrix products, arithmetic and copies ran while one was open for 9% -> 9% of each run, Pallas kernels for 0% -> 1%
where the time goes in v7:
time: 251 us
  blocking collectives  123 us (49%)
  starting transfers between devices  44.4 us (18%)
  waiting for transfers between devices  30.5 us (12%)
  matrix products  19.2 us (8%)
  local copies, waits for them, and re-layouts  15.4 us (6%)
  between operations  14.5 us (6%)
    all_to_all x1, blocking collectives, exchange_rows(): moved = lax.all_to_all(both, 'seq', split_axis=0, concat_axis=0, tiled=True)  72.5 us
    all_to_all x1, starting transfers between devices, exchange_rows(): moved = lax.all_to_all(both, 'seq', split_axis=0, concat_axis=0, tiled=True)  30.4 us
    all_to_all x2, blocking collectives, along_y(): lax.all_to_all(value, 'tp', 0, 0, tiled=True, axis_index_groups=groups)  19.4 us
    dot_general x14, matrix products, contract(): lax.dot_general(left, right, ((dims[:1], dims[1:]), ((), ())), preferred_...  19.2 us
    all_gather x1, blocking collectives, local(): lax.all_gather(message, 'tp', axis=0, tiled=False, axis_index_groups=rows...  19 us
    all_to_all x1, waiting for transfers between devices, exchange_rows(): moved = lax.all_to_all(both, 'seq', split_axis=0, concat_axis=0, tiled=True)  15.5 us
    ppermute x3, waiting for transfers between devices, fetch_half(): lax.ppermute(piece((my_y + step) % SIDE), 'tp', [(SIDE * y + x, SIDE * ((...  14.3 us
    all_to_all x1, blocking collectives, along_x(): lax.all_to_all(value, 'tp', 0, 0, tiled=True, axis_index_groups=groups)  11.6 us
  transfers between devices with their start and end apart: 6, of which 3 were waited for; matrix products, arithmetic and copies ran while one was open for 9% of the time, Pallas kernels for 1%

profile of v7, /device:TPU:1, one launch (start us, length us, event | category | flops | bytes accessed | tf_op | source)
XLA Modules:
  0.0 250.6 jit_solution(13927371479662338478)
XLA Ops:
  10.8 90.0 %conditional.1 = (bf16[256,896]{1,0:T(8,128)(2,1)S(1)}, bf16[4,112,1792]{2,1,0:T(8,128)(2,1)S(1)}, bf16[4,112,1792]{2,1,0:T(8,128)(2,1)}, f32[448,1]{0,1:T(1,128...) conditional(s32[]{:T(128)} %convert_element_type.278, () %tuple.24, ...), branch_computations={%region_2.3_spmd, %region_3.5_spmd} | conditional | flops 350607 | bytes 43027940 | solution.py:157
  11.9 30.4 %all-to-all-start = ((bf16[64,4,896]{2,1,0:T(4,128)(2,1)}), bf16[64,4,896]{2,1,0:T(4,128)(2,1)S(1)}, u32[]{:S(2)}, u32[]{:S(2)}) async-start(bf16[64,4,896]{2,1,0:T(4,128)(2,1)} %reshape.266), calls=%async_computation | async-start | bytes 917504 | tf_op jit(solution)/shard_map/cond/branch_1_fun/all_to_all | solution.py:76
  42.4 2.3 fusion.72
  44.7 3.2 %collective-permute-start = (bf16[112,1792]{1,0:T(8,128)(2,1)}, bf16[112,1792]{1,0:T(8,128)(2,1)}, u32[]{:S(2)}, u32[]{:S(2)}) collective-permute-start(bf16[112,1792]{1,0:T(8,128)(2,1)} %get-tuple-element.185), channel_id=1, source_target_pairs={{0,4},{1,5},{2,6},{3,7},{4,8},{5,9},{6,10},{7,11},{8,12},{9,13},{1... | collective-permute-start | bytes 1204232 | tf_op jit(solution)/shard_map/cond/branch_1_fun/ppermute | solution.py:113
  47.9 4.5 %collective-permute-start.1 = (bf16[112,1792]{1,0:T(8,128)(2,1)}, bf16[112,1792]{1,0:T(8,128)(2,1)}, u32[]{:S(2)}, u32[]{:S(2)}) collective-permute-start(bf16[112,1792]{1,0:T(8,128)(2,1)} %get-tuple-element.184), channel_id=1, source_target_pairs={{0,8},{1,9},{2,10},{3,11},{4,12},{5,13},{6,14},{7,15},{8,0},{9,1},... | collective-permute-start | bytes 1204232 | tf_op jit(solution)/shard_map/cond/branch_1_fun/ppermute | solution.py:113
  52.4 3.0 %collective-permute-start.2 = (bf16[112,1792]{1,0:T(8,128)(2,1)}, bf16[112,1792]{1,0:T(8,128)(2,1)}, u32[]{:S(2)}, u32[]{:S(2)}) collective-permute-start(bf16[112,1792]{1,0:T(8,128)(2,1)} %get-tuple-element.183), channel_id=1, source_target_pairs={{0,12},{1,13},{2,14},{3,15},{4,0},{5,1},{6,2},{7,3},{8,4},{9,5},{1... | collective-permute-start | bytes 1204232 | tf_op jit(solution)/shard_map/cond/branch_1_fun/ppermute | solution.py:113
  56.7 4.2 %collective-permute-done = bf16[112,1792]{1,0:T(8,128)(2,1)} collective-permute-done((bf16[112,1792]{1,0:T(8,128)(2,1)}, bf16[112,1792]{1,0:T(8,128)(2,1)}, u32[]{:S(2)}, u32[]{:S(2)}) %collective-permute-start) | collective-permute-done | bytes 401440 | tf_op jit(solution)/shard_map/cond/branch_1_fun/ppermute | solution.py:113
  61.9 10.1 %collective-permute-done.1 = bf16[112,1792]{1,0:T(8,128)(2,1)} collective-permute-done((bf16[112,1792]{1,0:T(8,128)(2,1)}, bf16[112,1792]{1,0:T(8,128)(2,1)}, u32[]{:S(2)}, u32[]{:S(2)}) %collective-permute-start.1) | collective-permute-done | bytes 401440 | tf_op jit(solution)/shard_map/cond/branch_1_fun/ppermute | solution.py:113
  74.1 3.3 %collective-permute-start.3 = (bf16[4,112,1792]{2,1,0:T(8,128)(2,1)S(1)}, bf16[4,112,1792]{2,1,0:T(8,128)(2,1)}, u32[]{:S(2)}, u32[]{:S(2)}) collective-permute-start(bf16[4,112,1792]{2,1,0:T(8,128)(2,1)S(1)} %bitcast_dynamic-update-slice_fusion), channel_id=1, source_target_pairs={{0,16},{16,0},{32,48},{48,32},{64,80},{80,64},{96,112},{112,96},{1... | collective-permute-start | bytes 4816904 | tf_op jit(solution)/shard_map/cond/branch_1_fun/ppermute | solution.py:119
  79.3 1.8 branch_1_fun.1
  81.1 1.2 copy.40
  82.3 2.9 %copy.41 = bf16[448,1792]{1,0:T(8,128)(2,1)} copy(bf16[448,1792]{1,0:T(8,128)(2,1)} %bitcast.9) | data formatting | bytes 3211264 | tf_op jit(solution)/shard_map/cond
  85.1 15.5 %all-to-all-done = bf16[64,4,896]{2,1,0:T(4,128)(2,1)S(1)} async-done(((bf16[64,4,896]{2,1,0:T(4,128)(2,1)}), bf16[64,4,896]{2,1,0:T(4,128)(2,1)S(1)}, u32[]{:S(2)}, u32[]{:S(2)}) %all-to-all-start) | async-done | bytes 458784 | tf_op jit(solution)/shard_map/cond/branch_1_fun/all_to_all | solution.py:76
  101.9 1.3 multiply_convert_fusion.4
  103.3 19.0 %all-gather = bf16[1856,256]{1,0:T(8,128)(2,1)S(1)} all-gather(bf16[464,256]{1,0:T(8,128)(2,1)S(1)} %pad_maximum_fusion.2), channel_id=2, replica_groups={{0,1,2,3},{4,5,6,7},{8,9,10,11},{12,13,14,15},{16,17,18,19},{20,21,22,2..., dimensions={0}, use_global_device_ids=true | all-gather | bytes 1187840 | tf_op jit(solution)/shard_map/all_gather | solution.py:166
  122.5 2.0 fusion.74
  124.5 2.0 select_convert_fusion.1
  126.6 10.3 %all_to_all.24 = bf16[4,240,256]{2,1,0:T(8,128)(2,1)S(1)} all-to-all(bf16[4,240,256]{2,1,0:T(8,128)(2,1)S(1)} %pad_maximum_fusion.1), channel_id=1, replica_groups={{0,4,8,12},{1,5,9,13},{2,6,10,14},{3,7,11,15},{16,20,24,28},{17,21,25,2..., dimensions={0} | all-to-all | bytes 983040 | tf_op jit(solution)/shard_map/all_to_all | solution.py:62
  137.0 4.4 %fusion.6 = f32[224,256]{1,0:T(8,128)S(1)} fusion(bf16[224,14336]{1,0:T(8,128)(2,1)} %bitcast.78, bf16[256,7168]{1,0:T(8,128)(2,1)} %all-gather.3.cloned.1.call-done, f32[7168]{0:T(1024)S(1)} %copy-done.7), kind=kOutput, calls=%fused_computation.31 | convolution fusion | flops 827588608 | bytes 7139328 | tf_op jit(solution)/shard_map/dot_general | solution.py:18
  142.2 9.1 %all_to_all.25 = bf16[4,240,256]{2,1,0:T(8,128)(2,1)S(1)} all-to-all(bf16[4,240,256]{2,1,0:T(8,128)(2,1)S(1)} %broadcast_in_dim.85), channel_id=1, replica_groups={{0,4,8,12},{1,5,9,13},{2,6,10,14},{3,7,11,15},{16,20,24,28},{17,21,25,2..., dimensions={0} | all-to-all | bytes 983040 | tf_op jit(solution)/shard_map/all_to_all | solution.py:62
  151.4 2.1 convolution_bitcast_fusion
  154.4 11.6 %all_to_all.26 = bf16[4,464,256]{2,1,0:T(8,128)(2,1)S(1)} all-to-all(bf16[4,464,256]{2,1,0:T(8,128)(2,1)S(1)} %pad_maximum_fusion), channel_id=1, replica_groups={{0,1,2,3},{4,5,6,7},{8,9,10,11},{12,13,14,15},{16,17,18,19},{20,21,22,2..., dimensions={0} | all-to-all | bytes 1900544 | tf_op jit(solution)/shard_map/all_to_all | solution.py:57
  169.1 72.5 %all_to_all.27 = bf16[64,4,896]{2,1,0:T(4,128)(2,1)S(1)} all-to-all(bf16[64,4,896]{2,1,0:T(4,128)(2,1)S(1)} %reshape.282), channel_id=1, replica_groups=mesh['seq'=64,'tp'=16] {'seq'}, dimensions={0} | all-to-all | bytes 917504 | tf_op jit(solution)/shard_map/all_to_all | solution.py:76
  242.2 1.6 fusion.5
  (94 shorter events, 17.5 us)
Async XLA Ops:
  7.2 2.6 %copy-start = (bf16[1024,448]{0,1:T(8,128)(2,1)S(1)}, bf16[1024,448]{0,1:T(8,128)(2,1)}, u32[]{:S(2)}) copy-start(bf16[1024,448]{0,1:T(8,128)(2,1)} %param.13) | copy-start | bytes 2752516
  7.2 129.8 %all-gather.3.cloned.1.call-start = ((), (), s32[]{:S(2)}) async-start(), calls=%async_computation.5 | async-start | bytes 3899392 | tf_op jit(solution)/shard_map/all_gather | solution.py:93
  9.8 1.0 copy-start.6
  11.9 88.7 %all-to-all-start = ((bf16[64,4,896]{2,1,0:T(4,128)(2,1)}), bf16[64,4,896]{2,1,0:T(4,128)(2,1)S(1)}, u32[]{:S(2)}, u32[]{:S(2)}) async-start(bf16[64,4,896]{2,1,0:T(4,128)(2,1)} %reshape.266), calls=%async_computation | async-start | bytes 917504 | tf_op jit(solution)/shard_map/cond/branch_1_fun/all_to_all | solution.py:76
  44.7 16.2 %collective-permute-start = (bf16[112,1792]{1,0:T(8,128)(2,1)}, bf16[112,1792]{1,0:T(8,128)(2,1)}, u32[]{:S(2)}, u32[]{:S(2)}) collective-permute-start(bf16[112,1792]{1,0:T(8,128)(2,1)} %get-tuple-element.185), channel_id=1, source_target_pairs={{0,4},{1,5},{2,6},{3,7},{4,8},{5,9},{6,10},{7,11},{8,12},{9,13},{1... | collective-permute-start | bytes 1204232 | tf_op jit(solution)/shard_map/cond/branch_1_fun/ppermute | solution.py:113
  47.9 24.1 %collective-permute-start.1 = (bf16[112,1792]{1,0:T(8,128)(2,1)}, bf16[112,1792]{1,0:T(8,128)(2,1)}, u32[]{:S(2)}, u32[]{:S(2)}) collective-permute-start(bf16[112,1792]{1,0:T(8,128)(2,1)} %get-tuple-element.184), channel_id=1, source_target_pairs={{0,8},{1,9},{2,10},{3,11},{4,12},{5,13},{6,14},{7,15},{8,0},{9,1},... | collective-permute-start | bytes 1204232 | tf_op jit(solution)/shard_map/cond/branch_1_fun/ppermute | solution.py:113
  52.4 20.6 %collective-permute-start.2 = (bf16[112,1792]{1,0:T(8,128)(2,1)}, bf16[112,1792]{1,0:T(8,128)(2,1)}, u32[]{:S(2)}, u32[]{:S(2)}) collective-permute-start(bf16[112,1792]{1,0:T(8,128)(2,1)} %get-tuple-element.183), channel_id=1, source_target_pairs={{0,12},{1,13},{2,14},{3,15},{4,0},{5,1},{6,2},{7,3},{8,4},{9,5},{1... | collective-permute-start | bytes 1204232 | tf_op jit(solution)/shard_map/cond/branch_1_fun/ppermute | solution.py:113
  55.6 21.8 %copy-start.3 = (bf16[16,7168]{1,0:T(8,128)(2,1)S(1)}, bf16[16,7168]{1,0:T(8,128)(2,1)}, u32[]{:S(2)}) copy-start(bf16[16,7168]{1,0:T(8,128)(2,1)} %get-tuple-element.96) | copy-start | bytes 688132 | tf_op jit(solution)/shard_map/cond
  74.1 8.1 %copy-start.1 = (bf16[4,112,1792]{2,1,0:T(8,128)(2,1)}, bf16[4,112,1792]{2,1,0:T(8,128)(2,1)S(1)}, u32[]{:S(2)}) copy-start(bf16[4,112,1792]{2,1,0:T(8,128)(2,1)S(1)} %bitcast_dynamic-update-slice_fusion) | copy-start | bytes 4816900 | tf_op jit(solution)/shard_map/cond
  74.1 8.1 %collective-permute-start.3 = (bf16[4,112,1792]{2,1,0:T(8,128)(2,1)S(1)}, bf16[4,112,1792]{2,1,0:T(8,128)(2,1)}, u32[]{:S(2)}, u32[]{:S(2)}) collective-permute-start(bf16[4,112,1792]{2,1,0:T(8,128)(2,1)S(1)} %bitcast_dynamic-update-slice_fusion), channel_id=1, source_target_pairs={{0,16},{16,0},{32,48},{48,32},{64,80},{80,64},{96,112},{112,96},{1... | collective-permute-start | bytes 4816904 | tf_op jit(solution)/shard_map/cond/branch_1_fun/ppermute | solution.py:119
  77.7 1.6 copy-start.5
  82.3 18.5 %copy-start.2 = (bf16[4,112,1792]{2,1,0:T(8,128)(2,1)S(1)}, bf16[4,112,1792]{2,1,0:T(8,128)(2,1)}, u32[]{:S(2)}) copy-start(bf16[4,112,1792]{2,1,0:T(8,128)(2,1)} %copy-done.1) | copy-start | bytes 4816900 | tf_op jit(solution)/shard_map/cond
  126.5 10.5 %copy-start.7 = (f32[7168]{0:T(1024)S(1)}, f32[7168]{0:T(1024)}, u32[]{:S(2)}) copy-start(f32[7168]{0:T(1024)} %param.14) | copy-start | bytes 86020
  137.0 4.4 %copy-start.4 = (bf16[256,224]{0,1:T(8,128)(2,1)S(1)}, bf16[256,224]{0,1:T(8,128)(2,1)}, u32[]{:S(2)}) copy-start(bf16[256,224]{0,1:T(8,128)(2,1)} %param.17) | copy-start | bytes 344068
Sparse Core Ops, SparseCore 0:
  12.2 109.9 all-gather.2

commit v8 on v7

--- a/solution.py
+++ b/solution.py
@@ -116,6 +116,7 @@
                 [(SIDE * y + x, SIDE * ((y + step) % SIDE) + x) for y in range(SIDE) for x in range(SIDE)],
             )
             fetched_half = lax.dynamic_update_slice(fetched_half, moved[None], ((my_y - step) % SIDE, 0, 0))
+        fetched_half = fetched_half.reshape(SIDE * part, quarter)
         return fetched_half, lax.ppermute(fetched_half, "seq", [(k, k ^ 1) for k in range(groups)])
 
     first = my_core == 0
@@ -154,9 +155,7 @@
     def skip():
         return jax.tree.map(lambda leaf: jnp.zeros(leaf.shape, leaf.dtype), jax.eval_shape(fetch))
 
-    fetched, fetched_half, other_half, gain, hidden_scale, place_left, place_right = lax.cond(my_group < groups, fetch, skip)
-    weights_here = fetched_half.reshape(SIDE * part, quarter)
-    weights_other = other_half.reshape(SIDE * part, quarter)
+    fetched, weights_here, weights_other, gain, hidden_scale, place_left, place_right = lax.cond(my_group < groups, fetch, skip)
 
     emb = contract(fetched, place_left, (0, 0))[:local_width] + contract(fetched, place_right, (0, 0))[local_width:]
     squares = jnp.sum(emb * emb, axis=0, keepdims=True)

time: 251 us -> 252 us (level)
  waiting for transfers between devices: 30.5 us -> 34.2 us
  blocking collectives: 123 us -> 126 us
  local copies, waits for them, and re-layouts: 15.4 us -> 12.5 us
    all_to_all x1, waiting for transfers between devices: 15.5 us -> 20.9 us  [exchange_rows(): moved = lax.all_to_all(both, 'seq', split_axis=0, concat_axis=0, tiled=True)]
    cond x10 -> x2, local copies, waits for them, and re-layouts: 4.06 us -> 0.01 us
  transfers between devices with their start and end apart: 6 -> 6, of which waited for: 3 -> 3; matrix products, arithmetic and copies ran while one was open for 9% -> 7% of each run, Pallas kernels for 1% -> 0%
where the time goes in v8:
time: 252 us
  blocking collectives  126 us (50%)
  starting transfers between devices  44.4 us (18%)
  waiting for transfers between devices  34.2 us (14%)
  matrix products  17 us (7%)
  between operations  14.5 us (6%)
  local copies, waits for them, and re-layouts  12.5 us (5%)
    all_to_all x1, blocking collectives, exchange_rows(): moved = lax.all_to_all(both, 'seq', split_axis=0, concat_axis=0, tiled=True)  74.8 us
    all_to_all x1, starting transfers between devices, exchange_rows(): moved = lax.all_to_all(both, 'seq', split_axis=0, concat_axis=0, tiled=True)  30.4 us
    all_to_all x1, waiting for transfers between devices, exchange_rows(): moved = lax.all_to_all(both, 'seq', split_axis=0, concat_axis=0, tiled=True)  20.9 us
    all_to_all x2, blocking collectives, along_y(): lax.all_to_all(value, 'tp', 0, 0, tiled=True, axis_index_groups=groups)  20 us
    all_gather x1, blocking collectives, local(): lax.all_gather(message, 'tp', axis=0, tiled=False, axis_index_groups=rows...  19.2 us
    dot_general x14, matrix products, contract(): lax.dot_general(left, right, ((dims[:1], dims[1:]), ((), ())), preferred_...  17 us
    ppermute x3, waiting for transfers between devices, fetch_half(): lax.ppermute(piece((my_y + step) % SIDE), 'tp', [(SIDE * y + x, SIDE * ((...  12.6 us
    all_to_all x1, blocking collectives, along_x(): lax.all_to_all(value, 'tp', 0, 0, tiled=True, axis_index_groups=groups)  11.8 us
  transfers between devices with their start and end apart: 6, of which 3 were waited for; matrix products, arithmetic and copies ran while one was open for 7% of the time, Pallas kernels for 0%

profile of v8, /device:TPU:1, one launch (start us, length us, event | category | flops | bytes accessed | tf_op | source)
XLA Modules:
  0.0 251.6 jit_solution(18146166312798408591)
XLA Ops:
  10.8 90.0 %conditional.1 = (bf16[256,896]{1,0:T(8,128)(2,1)S(1)}, bf16[448,1792]{1,0:T(8,128)(2,1)}, bf16[448,1792]{1,0:T(8,128)(2,1)}, f32[448,1]{0,1:T(1,128)S(1)}, bf16...) conditional(s32[]{:T(128)} %convert_element_type.278, () %tuple.20, ...), branch_computations={%region_2.3_spmd, %region_3.5_spmd} | conditional | flops 350607 | bytes 22842752 | solution.py:158
  11.9 30.4 %all-to-all-start = ((bf16[64,4,896]{2,1,0:T(4,128)(2,1)}), bf16[64,4,896]{2,1,0:T(4,128)(2,1)S(1)}, u32[]{:S(2)}, u32[]{:S(2)}) async-start(bf16[64,4,896]{2,1,0:T(4,128)(2,1)} %reshape.260), calls=%async_computation | async-start | bytes 917504 | tf_op jit(solution)/shard_map/cond/branch_1_fun/all_to_all | solution.py:76
  42.4 2.3 fusion.60
  44.7 3.2 %collective-permute-start = (bf16[112,1792]{1,0:T(8,128)(2,1)}, bf16[112,1792]{1,0:T(8,128)(2,1)S(1)}, u32[]{:S(2)}, u32[]{:S(2)}) collective-permute-start(bf16[112,1792]{1,0:T(8,128)(2,1)} %get-tuple-element.215), channel_id=1, source_target_pairs={{0,4},{1,5},{2,6},{3,7},{4,8},{5,9},{6,10},{7,11},{8,12},{9,13},{1... | collective-permute-start | bytes 1204232 | tf_op jit(solution)/shard_map/cond/branch_1_fun/ppermute | solution.py:113
  47.9 4.5 %collective-permute-start.1 = (bf16[112,1792]{1,0:T(8,128)(2,1)}, bf16[112,1792]{1,0:T(8,128)(2,1)S(1)}, u32[]{:S(2)}, u32[]{:S(2)}) collective-permute-start(bf16[112,1792]{1,0:T(8,128)(2,1)} %get-tuple-element.214), channel_id=1, source_target_pairs={{0,8},{1,9},{2,10},{3,11},{4,12},{5,13},{6,14},{7,15},{8,0},{9,1},... | collective-permute-start | bytes 1204232 | tf_op jit(solution)/shard_map/cond/branch_1_fun/ppermute | solution.py:113
  52.4 3.0 %collective-permute-start.2 = (bf16[112,1792]{1,0:T(8,128)(2,1)S(1)}, bf16[112,1792]{1,0:T(8,128)(2,1)S(1)}, u32[]{:S(2)}, u32[]{:S(2)}) collective-permute-start(bf16[112,1792]{1,0:T(8,128)(2,1)S(1)} %get-tuple-element.213), channel_id=1, source_target_pairs={{0,12},{1,13},{2,14},{3,15},{4,0},{5,1},{6,2},{7,3},{8,4},{9,5},{1... | collective-permute-start | bytes 1204232 | tf_op jit(solution)/shard_map/cond/branch_1_fun/ppermute | solution.py:113
  55.5 1.3 broadcast.165
  56.8 1.8 bitcast_dynamic-update-slice_fusion.3
  58.5 2.4 collective-permute-done
  61.7 10.2 %collective-permute-done.1 = bf16[112,1792]{1,0:T(8,128)(2,1)S(1)} collective-permute-done((bf16[112,1792]{1,0:T(8,128)(2,1)}, bf16[112,1792]{1,0:T(8,128)(2,1)S(1)}, u32[]{:S(2)}, u32[]{:S(2)}) %collective-permute-start.1) | collective-permute-done | bytes 401440 | tf_op jit(solution)/shard_map/cond/branch_1_fun/ppermute | solution.py:113
  73.5 3.3 %collective-permute-start.3 = (bf16[448,1792]{1,0:T(8,128)(2,1)}, bf16[448,1792]{1,0:T(8,128)(2,1)}, u32[]{:S(2)}, u32[]{:S(2)}) collective-permute-start(bf16[448,1792]{1,0:T(8,128)(2,1)} %bitcast.4), channel_id=1, source_target_pairs={{0,16},{16,0},{32,48},{48,32},{64,80},{80,64},{96,112},{112,96},{1... | collective-permute-start | bytes 4816904 | tf_op jit(solution)/shard_map/cond/branch_1_fun/ppermute | solution.py:120
  78.6 1.1 branch_1_fun.1
  79.8 20.9 %all-to-all-done = bf16[64,4,896]{2,1,0:T(4,128)(2,1)S(1)} async-done(((bf16[64,4,896]{2,1,0:T(4,128)(2,1)}), bf16[64,4,896]{2,1,0:T(4,128)(2,1)S(1)}, u32[]{:S(2)}, u32[]{:S(2)}) %all-to-all-start) | async-done | bytes 458784 | tf_op jit(solution)/shard_map/cond/branch_1_fun/all_to_all | solution.py:76
  101.5 19.2 %all-gather = bf16[1856,256]{1,0:T(8,128)(2,1)S(1)} all-gather(bf16[464,256]{1,0:T(8,128)(2,1)S(1)} %pad_maximum_fusion.2), channel_id=2, replica_groups={{0,1,2,3},{4,5,6,7},{8,9,10,11},{12,13,14,15},{16,17,18,19},{20,21,22,2..., dimensions={0}, use_global_device_ids=true | all-gather | bytes 1187840 | tf_op jit(solution)/shard_map/all_gather | solution.py:165
  120.9 2.0 fusion.63
  122.9 2.0 select_convert_fusion.1
  125.0 10.9 %all_to_all.24 = bf16[4,240,256]{2,1,0:T(8,128)(2,1)S(1)} all-to-all(bf16[4,240,256]{2,1,0:T(8,128)(2,1)S(1)} %pad_maximum_fusion.1), channel_id=1, replica_groups={{0,4,8,12},{1,5,9,13},{2,6,10,14},{3,7,11,15},{16,20,24,28},{17,21,25,2..., dimensions={0} | all-to-all | bytes 983040 | tf_op jit(solution)/shard_map/all_to_all | solution.py:62
  136.0 4.4 %fusion.5 = f32[224,256]{1,0:T(8,128)S(1)} fusion(bf16[224,14336]{1,0:T(8,128)(2,1)} %bitcast.74, bf16[256,7168]{1,0:T(8,128)(2,1)} %all-gather.3.cloned.1.call-done, f32[7168]{0:T(1024)S(1)} %copy-done.5), kind=kOutput, calls=%fused_computation.29 | convolution fusion | flops 827588608 | bytes 7139328 | tf_op jit(solution)/shard_map/dot_general | solution.py:18
  141.2 9.1 %all_to_all.25 = bf16[4,240,256]{2,1,0:T(8,128)(2,1)S(1)} all-to-all(bf16[4,240,256]{2,1,0:T(8,128)(2,1)S(1)} %broadcast_in_dim.85), channel_id=1, replica_groups={{0,4,8,12},{1,5,9,13},{2,6,10,14},{3,7,11,15},{16,20,24,28},{17,21,25,2..., dimensions={0} | all-to-all | bytes 983040 | tf_op jit(solution)/shard_map/all_to_all | solution.py:62
  150.5 2.1 fusion.64
  152.6 2.2 fusion.3
  154.9 11.8 %all_to_all.26 = bf16[4,464,256]{2,1,0:T(8,128)(2,1)S(1)} all-to-all(bf16[4,464,256]{2,1,0:T(8,128)(2,1)S(1)} %pad_maximum_fusion), channel_id=1, replica_groups={{0,1,2,3},{4,5,6,7},{8,9,10,11},{12,13,14,15},{16,17,18,19},{20,21,22,2..., dimensions={0} | all-to-all | bytes 1900544 | tf_op jit(solution)/shard_map/all_to_all | solution.py:57
  167.9 74.8 %all_to_all.27 = bf16[64,4,896]{2,1,0:T(4,128)(2,1)S(1)} all-to-all(bf16[64,4,896]{2,1,0:T(4,128)(2,1)S(1)} %reshape.279), channel_id=1, replica_groups=mesh['seq'=64,'tp'=16] {'seq'}, dimensions={0} | all-to-all | bytes 917504 | tf_op jit(solution)/shard_map/all_to_all | solution.py:76
  243.2 1.6 fusion.4
  (92 shorter events, 12.7 us)
Async XLA Ops:
  7.2 2.6 %copy-start = (bf16[1024,448]{0,1:T(8,128)(2,1)S(1)}, bf16[1024,448]{0,1:T(8,128)(2,1)}, u32[]{:S(2)}) copy-start(bf16[1024,448]{0,1:T(8,128)(2,1)} %param.13) | copy-start | bytes 2752516
  7.2 128.8 %all-gather.3.cloned.1.call-start = ((), (), s32[]{:S(2)}) async-start(), calls=%async_computation.5 | async-start | bytes 3899392 | tf_op jit(solution)/shard_map/all_gather | solution.py:93
  9.8 1.0 copy-start.1
  9.8 1.0 copy-start.4
  11.9 88.7 %all-to-all-start = ((bf16[64,4,896]{2,1,0:T(4,128)(2,1)}), bf16[64,4,896]{2,1,0:T(4,128)(2,1)S(1)}, u32[]{:S(2)}, u32[]{:S(2)}) async-start(bf16[64,4,896]{2,1,0:T(4,128)(2,1)} %reshape.260), calls=%async_computation | async-start | bytes 917504 | tf_op jit(solution)/shard_map/cond/branch_1_fun/all_to_all | solution.py:76
  44.7 16.2 %collective-permute-start = (bf16[112,1792]{1,0:T(8,128)(2,1)}, bf16[112,1792]{1,0:T(8,128)(2,1)S(1)}, u32[]{:S(2)}, u32[]{:S(2)}) collective-permute-start(bf16[112,1792]{1,0:T(8,128)(2,1)} %get-tuple-element.215), channel_id=1, source_target_pairs={{0,4},{1,5},{2,6},{3,7},{4,8},{5,9},{6,10},{7,11},{8,12},{9,13},{1... | collective-permute-start | bytes 1204232 | tf_op jit(solution)/shard_map/cond/branch_1_fun/ppermute | solution.py:113
  47.9 24.1 %collective-permute-start.1 = (bf16[112,1792]{1,0:T(8,128)(2,1)}, bf16[112,1792]{1,0:T(8,128)(2,1)S(1)}, u32[]{:S(2)}, u32[]{:S(2)}) collective-permute-start(bf16[112,1792]{1,0:T(8,128)(2,1)} %get-tuple-element.214), channel_id=1, source_target_pairs={{0,8},{1,9},{2,10},{3,11},{4,12},{5,13},{6,14},{7,15},{8,0},{9,1},... | collective-permute-start | bytes 1204232 | tf_op jit(solution)/shard_map/cond/branch_1_fun/ppermute | solution.py:113
  52.4 20.3 %collective-permute-start.2 = (bf16[112,1792]{1,0:T(8,128)(2,1)S(1)}, bf16[112,1792]{1,0:T(8,128)(2,1)S(1)}, u32[]{:S(2)}, u32[]{:S(2)}) collective-permute-start(bf16[112,1792]{1,0:T(8,128)(2,1)S(1)} %get-tuple-element.213), channel_id=1, source_target_pairs={{0,12},{1,13},{2,14},{3,15},{4,0},{5,1},{6,2},{7,3},{8,4},{9,5},{1... | collective-permute-start | bytes 1204232 | tf_op jit(solution)/shard_map/cond/branch_1_fun/ppermute | solution.py:113
  73.5 27.3 %collective-permute-start.3 = (bf16[448,1792]{1,0:T(8,128)(2,1)}, bf16[448,1792]{1,0:T(8,128)(2,1)}, u32[]{:S(2)}, u32[]{:S(2)}) collective-permute-start(bf16[448,1792]{1,0:T(8,128)(2,1)} %bitcast.4), channel_id=1, source_target_pairs={{0,16},{16,0},{32,48},{48,32},{64,80},{80,64},{96,112},{112,96},{1... | collective-permute-start | bytes 4816904 | tf_op jit(solution)/shard_map/cond/branch_1_fun/ppermute | solution.py:120
  77.0 1.6 copy-start.3
  124.9 11.1 %copy-start.5 = (f32[7168]{0:T(1024)S(1)}, f32[7168]{0:T(1024)}, u32[]{:S(2)}) copy-start(f32[7168]{0:T(1024)} %param.14) | copy-start | bytes 86020
  135.9 4.4 %copy-start.2 = (bf16[256,224]{0,1:T(8,128)(2,1)S(1)}, bf16[256,224]{0,1:T(8,128)(2,1)}, u32[]{:S(2)}) copy-start(bf16[256,224]{0,1:T(8,128)(2,1)} %param.17) | copy-start | bytes 344068
Sparse Core Ops, SparseCore 0:
  12.2 110.2 all-gather.2
